TPU v7x, 512 devices: a whole 4x8x8 slice. The times are simulated.
512 devices in a mesh: slab: 64 (over z, y), patch: 8 (over x, core).
Axes of the slice: x: 4, y: 8, z: 8, core: 2. Of those that a mesh axis runs over, the one named last changes fastest.
Arguments:
- density: float32 [262144], P(('slab', 'patch')), may hold values from -6 to 6
- counts: int32 [512, 512], P(('slab', 'patch')), may hold values from 1 to 8, as said below
- send_panel: int32 [512, 512, 8], P(('slab', 'patch')), may hold values from 0 to 511
- send_weight: float32 [512, 512, 8], P(('slab', 'patch')), may hold values from -4 to 4
- interp_weight: float32 [512, 512, 8], P(('slab', 'patch')), may hold values from -4 to 4
- recv_row: int32 [512, 512, 8], P(('slab', 'patch')), may hold values from 0 to 255
- recv_col: int32 [512, 512, 8], P(('slab', 'patch')), may hold values from 0 to 511
- kernel: float32 [512, 512, 256], P(('slab', 'patch')), may hold values from 0.1 to 3, as said below
- near_index: int32 [16, 262144], P(None, ('slab', 'patch')), may hold values from 0 to 4095
- near_coef: float32 [16, 262144], P(None, ('slab', 'patch')), may hold values from -1 to 1
Outputs:
- potential: float32 [262144], P(('slab', 'patch'))
Inputs may be any that keep to these rules, and one draw needn't show every extreme that they name: counts[a, b] is the number of used slots of the 8 from device a to grid owner b; in every draw some owner receives 8 from every device, and every device sends 8 to some owner. kernel[kx, ky, kz] = kernel[(-kx) mod 512, (-ky) mod 512, (-kz) mod 256].
All inputs are finite; a program needn't handle non-finite values.
Results may differ from a plain program's by a relative error of at most 0.00011.
Values sent between devices are 32-bit elements; how exact they have to be, the bound alone decides.
No kernel may reach another device: no remote copies, remote signals or barrier semaphores. Data moves between devices by JAX's collectives and lax.ppermute only.
A program may use at most 64 MiB of HBM per device.

v0:
```python
import math

import jax
import jax.numpy as jnp
from jax import lax
from jax.sharding import PartitionSpec as P

HIGH = lax.Precision.HIGHEST


def tables(length, order):
    across = jnp.arange(length, dtype=jnp.int32)
    angles = (order[:, None] * across[None, :] % length).astype(jnp.float32) * (
        2.0 * math.pi / length
    )
    return (jnp.cos(angles), jnp.sin(angles))


def crossed(length, n_slab, n_patch):
    places = jnp.arange(length, dtype=jnp.int32)
    pencil = length // (n_slab * n_patch)
    period = length // n_patch
    return (places % period // pencil * n_patch + places // period) * pencil + places % pencil


def rotate(pattern, real_part, imag_part, cosine, sine_table, sign):
    result_re = jnp.einsum(pattern, real_part, cosine, precision=HIGH) + sign * jnp.einsum(
        pattern, imag_part, sine_table, precision=HIGH
    )
    result_im = jnp.einsum(pattern, imag_part, cosine, precision=HIGH) - sign * jnp.einsum(
        pattern, real_part, sine_table, precision=HIGH
    )
    return (result_re, result_im)


def per_device(
    density,
    counts,
    send_panel,
    send_weight,
    interp_weight,
    recv_row,
    recv_col,
    kernel,
    near_index,
    near_coef,
):
    n_slab = lax.axis_size("slab")
    n_patch = lax.axis_size("patch")
    pencil, size_y, size_z = kernel.shape
    size_x = pencil * n_slab * n_patch
    slab_depth = size_z // n_slab
    patch_rows = size_y // n_patch
    plane = slab_depth * patch_rows
    capacity = send_panel.shape[2]
    slots = jnp.arange(capacity, dtype=jnp.int32)
    in_use = slots[None, :] < counts[0][:, None]
    items = jnp.where(in_use, send_weight[0] * density[send_panel[0]], 0.0)
    outgoing = items.reshape(n_slab, n_patch, capacity)
    arrived = lax.all_to_all(
        lax.all_to_all(outgoing, "slab", split_axis=0, concat_axis=0, tiled=True),
        "patch",
        split_axis=1,
        concat_axis=1,
        tiled=True,
    )
    cells = (recv_row[0] * size_x + recv_col[0]).reshape(-1)
    grid = (
        jnp.zeros((plane * size_x,), jnp.float32)
        .at[cells]
        .add(arrived.reshape(-1))
        .reshape(plane, size_x)
    )
    straight = jnp.arange(size_x, dtype=jnp.int32)
    mixed_order = crossed(size_x, n_slab, n_patch)
    cos_x, sin_x = tables(size_x, straight)
    spec_re = jnp.einsum("rx,kx->kr", grid, cos_x, precision=HIGH)
    spec_im = -jnp.einsum("rx,kx->kr", grid, sin_x, precision=HIGH)
    stacked = jnp.stack([spec_re, spec_im])
    moved = lax.all_to_all(
        lax.all_to_all(stacked, "slab", split_axis=1, concat_axis=2, tiled=True),
        "patch",
        split_axis=1,
        concat_axis=2,
        tiled=True,
    )
    moved = moved.reshape(2, pencil, n_patch, n_slab, slab_depth, patch_rows)
    along_y = "xpszl,kpl->xszk"
    cos_y, sin_y = tables(size_y, jnp.arange(size_y, dtype=jnp.int32))
    cos_y = cos_y.reshape(size_y, n_patch, patch_rows)
    sin_y = sin_y.reshape(size_y, n_patch, patch_rows)
    cos_z, sin_z = tables(size_z, jnp.arange(size_z, dtype=jnp.int32))
    cos_z = cos_z.reshape(size_z, n_slab, slab_depth)
    sin_z = sin_z.reshape(size_z, n_slab, slab_depth)
    part_re, part_im = rotate(along_y, moved[0], moved[1], cos_y, sin_y, 1.0)
    wave_re, wave_im = rotate("xszk,jsz->xkj", part_re, part_im, cos_z, sin_z, 1.0)
    wave_re = wave_re * kernel
    wave_im = wave_im * kernel
    part_re, part_im = rotate("xkj,jsz->xszk", wave_re, wave_im, cos_z, sin_z, -1.0)
    line_re, line_im = rotate("xszk,kpl->spxzl", part_re, part_im, cos_y, sin_y, -1.0)
    leaving = jnp.stack([line_re, line_im]).reshape(2, n_slab, n_patch, pencil, plane)
    returned_lines = lax.all_to_all(
        lax.all_to_all(leaving, "slab", split_axis=1, concat_axis=3, tiled=True),
        "patch",
        split_axis=2,
        concat_axis=3,
        tiled=True,
    )
    returned_lines = returned_lines.reshape(2, size_x, plane)
    cos_back, sin_back = tables(size_x, mixed_order)
    scale = 1.0 / (size_x * size_y * size_z)
    field = (
        jnp.einsum("jr,jx->rx", returned_lines[0], cos_back, precision=HIGH)
        - jnp.einsum("jr,jx->rx", returned_lines[1], sin_back, precision=HIGH)
    ) * scale
    sampled = field.reshape(-1)[cells].reshape(n_slab, n_patch, capacity)
    fetched = lax.all_to_all(
        lax.all_to_all(sampled, "slab", split_axis=0, concat_axis=0, tiled=True),
        "patch",
        split_axis=1,
        concat_axis=1,
        tiled=True,
    )
    terms = jnp.where(in_use, interp_weight[0] * fetched.reshape(-1, capacity), 0.0)
    interp = (
        jnp.zeros((density.shape[0],), jnp.float32)
        .at[send_panel[0].reshape(-1)]
        .add(terms.reshape(-1))
    )
    group = lax.all_gather(density, "patch", axis=0, tiled=True)
    near = jnp.sum(near_coef * group[near_index], axis=0)
    return interp + near


def solution(mesh):
    placed = (
        P(("slab", "patch")),
        P(("slab", "patch"), None),
        P(("slab", "patch"), None, None),
        P(("slab", "patch"), None, None),
        P(("slab", "patch"), None, None),
        P(("slab", "patch"), None, None),
        P(("slab", "patch"), None, None),
        P(("slab", "patch"), None, None),
        P(None, ("slab", "patch")),
        P(None, ("slab", "patch")),
    )
    return jax.shard_map(
        per_device, mesh=mesh, in_specs=placed, out_specs=P(("slab", "patch")), check_vma=False
    )
```

profile of v0, /device:TPU:1, one launch (start us, length us, event | category | flops | bytes accessed | tf_op | source)
XLA Modules:
  0.0 426.5 jit_solution(6870696531433397887)
XLA Ops:
  0.0 0.7 compare_select_fusion.3
  0.7 0.5 broadcast.705
  1.3 0.7 reduce.7
  2.3 0.7 copy-done
  3.0 25.9 %gather_fusion.1 = f32[4096]{0:T(1024)S(1)} fusion(f32[512]{0:T(512)S(1)} %copy-done, s32[4096]{0:T(1024)S(1)} %broadcast_clamp_fusion.2), kind=kCustom, calls=%fused_computation.1 | custom fusion | bytes 49152 | tf_op jit(solution)/shard_map/gather | solution.py:58
  29.3 0.4 copy-done.5
  29.9 0.8 copy.28
  30.8 17.3 %all-to-all-start = ((f32[64,8,8]{1,2,0:T(8,128)}), f32[64,8,8]{1,2,0:T(8,128)S(1)}, u32[]{:S(2)}, u32[]{:S(2)}) async-start(f32[64,8,8]{1,2,0:T(8,128)} %copy.28), calls=%async_computation | async-start | bytes 524288 | tf_op jit(solution)/shard_map/all_to_all | solution.py:61
  48.4 12.3 %all-to-all-done = f32[64,8,8]{1,2,0:T(8,128)S(1)} async-done(((f32[64,8,8]{1,2,0:T(8,128)}), f32[64,8,8]{1,2,0:T(8,128)S(1)}, u32[]{:S(2)}, u32[]{:S(2)}) %all-to-all-start) | async-done | bytes 16416 | tf_op jit(solution)/shard_map/all_to_all | solution.py:61
  60.9 0.7 reshape.469
  61.6 7.5 %all-to-all-start.1 = ((f32[8,1,512]{2,1,0:T(1,128)}), f32[8,1,512]{2,1,0:T(1,128)S(1)}, u32[]{:S(2)}, u32[]{:S(2)}) async-start(f32[8,1,512]{2,1,0:T(1,128)} %reshape.469), calls=%async_computation.1 | async-start | bytes 32768 | tf_op jit(solution)/shard_map/all_to_all | solution.py:60
  69.1 4.6 %all-to-all-done.1 = f32[8,1,512]{2,1,0:T(1,128)S(1)} async-done(((f32[8,1,512]{2,1,0:T(1,128)}), f32[8,1,512]{2,1,0:T(1,128)S(1)}, u32[]{:S(2)}, u32[]{:S(2)}) %all-to-all-start.1) | async-done | bytes 16416 | tf_op jit(solution)/shard_map/all_to_all | solution.py:60
  73.7 0.6 broadcast.706
  74.3 0.7 reduce.8
  75.4 22.3 %scatter_custom_fusion = f32[131072]{0:T(1024)S(1)} fusion(s32[4096]{0:T(1024)S(1)} %bitcast.176, f32[4096]{0:T(1024)S(1)} %reshape.424, f32[]{:T(128)} %constant.101.clone.1), kind=kCustom, calls=%fused_computation.113 | custom fusion | flops 4096 | bytes 524292 | tf_op jit(solution)/shard_map/scatter-add | solution.py:71
  97.8 4.8 %fusion.4 = f32[1,512,256]{2,1,0:T(8,128)S(1)} fusion(f32[256,512]{1,0:T(8,128)S(1)} %reshape.388), kind=kOutput, calls=%fused_computation.30 | convolution fusion | flops 809107456 | bytes 1048576 | tf_op jit(solution)/shard_map/rx,kx->kr/dot_general | solution.py:78
  102.6 4.8 %convolution_bitcast_fusion.8 = f32[1,512,256]{2,1,0:T(8,128)S(1)} fusion(f32[256,512]{1,0:T(8,128)S(1)} %reshape.388), kind=kOutput, calls=%fused_computation.31 | convolution fusion | flops 808976384 | bytes 1048576 | tf_op jit(solution)/shard_map/rx,kx->kr/dot_general | solution.py:77
  107.5 0.8 copy.31
  108.4 31.3 %all_to_all.74 = f32[2,512,256]{2,0,1:T(2,128)S(1)} all-to-all(f32[2,512,256]{2,0,1:T(2,128)S(1)} %copy.31), channel_id=1, replica_groups=mesh['slab'=64,'patch'=8] {'slab'}, dimensions={1} | all-to-all | bytes 2097152 | tf_op jit(solution)/shard_map/all_to_all | solution.py:81
  139.6 1.4 copy.52
  141.0 7.3 %all-to-all-start.3 = ((f32[2,8,16384]{2,0,1:T(2,128)}), f32[2,8,16384]{2,0,1:T(2,128)S(1)}, u32[]{:S(2)}, u32[]{:S(2)}) async-start(f32[2,8,16384]{2,0,1:T(2,128)} %bitcast.61), calls=%async_computation.3 | async-start | bytes 2097152 | tf_op jit(solution)/shard_map/all_to_all | solution.py:80
  148.3 14.5 %all-to-all-done.3 = f32[2,8,16384]{2,0,1:T(2,128)S(1)} async-done(((f32[2,8,16384]{2,0,1:T(2,128)}), f32[2,8,16384]{2,0,1:T(2,128)S(1)}, u32[]{:S(2)}, u32[]{:S(2)}) %all-to-all-start.3) | async-done | bytes 1048608 | tf_op jit(solution)/shard_map/all_to_all | solution.py:80
  162.9 2.7 slice_reduce_fusion.1
  165.6 0.7 reshape.389
  166.2 0.7 reshape.390
  166.9 5.1 %convolution_bitcast_fusion = f32[64,4,512]{2,0,1:T(8,128)S(1)} fusion(f32[8,64,4,64]{3,2,1,0:T(4,128)S(1)} %reshape.389, s32[8,64]{1,0:T(8,128)S(1)} %multiply_add_fusion.1), kind=kOutput, calls=%fused_computation.19 | convolution fusion | flops 808976384 | bytes 1050624 | tf_op jit(solution)/shard_map/xpszl,kpl->xszk/dot_general | solution.py:30
  172.1 5.3 %convolution_bitcast_fusion.2 = f32[64,4,512]{2,0,1:T(8,128)S(1)} fusion(f32[8,64,4,64]{3,2,1,0:T(4,128)S(1)} %reshape.390, s32[8,64]{1,0:T(8,128)S(1)} %multiply_add_fusion.1), kind=kOutput, calls=%fused_computation.21 | convolution fusion | flops 808976384 | bytes 1050624 | tf_op jit(solution)/shard_map/xpszl,kpl->xszk/dot_general | solution.py:27
  177.3 5.1 %fusion.10 = f32[64,4,512]{2,0,1:T(8,128)S(1)} fusion(f32[64,4,512]{2,0,1:T(8,128)S(1)} %convolution_bitcast_fusion, f32[8,64,4,64]{3,2,1,0:T(4,128)S(1)} %reshape.390, s32[8,64]{1,0:T(8,128)S(1)} %multiply_add_fusion.1), kind=kOutput, calls=%fused_computation.39 | convolution fusion | flops 809107456 | bytes 1574912 | tf_op jit(solution)/shard_map/xpszl,kpl->xszk/dot_general | solution.py:30
  182.4 5.5 %fusion.9 = f32[64,4,512]{2,0,1:T(8,128)S(1)} fusion(f32[64,4,512]{2,0,1:T(8,128)S(1)} %convolution_bitcast_fusion.2, f32[8,64,4,64]{3,2,1,0:T(4,128)S(1)} %reshape.389, s32[8,64]{1,0:T(8,128)S(1)} %multiply_add_fusion.1), kind=kOutput, calls=%fused_computation.38 | convolution fusion | flops 809107456 | bytes 1574912 | tf_op jit(solution)/shard_map/xpszl,kpl->xszk/dot_general | solution.py:27
  187.9 1.9 convolution_bitcast_fusion.4
  189.9 1.9 convolution_bitcast_fusion.6
  191.8 1.9 fusion.18
  193.7 1.9 fusion.14
  195.7 2.4 fusion.80
  198.0 2.4 fusion.78
  200.4 2.4 fusion.8
  202.8 2.6 fusion.6
  205.3 5.6 %fusion.30 = f32[8,64,64,4]{2,1,3,0:T(8,128)S(1)} fusion(f32[64,4,512,1]{2,0,1,3:T(8,128)S(1)} %fusion.6, s32[8,64]{1,0:T(8,128)S(1)} %multiply_add_fusion.1), kind=kOutput, calls=%fused_computation.61 | convolution fusion | flops 808976384 | bytes 1050624 | tf_op jit(solution)/shard_map/xszk,kpl->spxzl/dot_general | solution.py:30
  211.0 5.6 %fusion.32 = f32[8,64,64,4]{2,1,3,0:T(8,128)S(1)} fusion(f32[64,4,512,1]{2,0,1,3:T(8,128)S(1)} %fusion.8, s32[8,64]{1,0:T(8,128)S(1)} %multiply_add_fusion.1), kind=kOutput, calls=%fused_computation.63 | convolution fusion | flops 808976384 | bytes 1050624 | tf_op jit(solution)/shard_map/xszk,kpl->spxzl/dot_general | solution.py:27
  216.6 5.9 %fusion = f32[8,64,64,4]{2,1,3,0:T(8,128)S(1)} fusion(f32[8,64,64,4]{2,1,3,0:T(8,128)S(1)} %fusion.30, f32[64,4,512,1]{2,0,1,3:T(8,128)S(1)} %fusion.8, s32[8,64]{1,0:T(8,128)S(1)} %multiply_add_fusion.1), kind=kOutput, calls=%fused_computation.15 | convolution fusion | flops 809238528 | bytes 1574912 | tf_op jit(solution)/shard_map/xszk,kpl->spxzl/dot_general | solution.py:30
  222.5 0.4 copy.38
  222.9 5.7 %fusion.1 = f32[8,64,64,4]{2,1,3,0:T(8,128)S(1)} fusion(f32[8,64,64,4]{2,1,3,0:T(8,128)S(1)} %fusion.32, f32[64,4,512,1]{2,0,1,3:T(8,128)S(1)} %fusion.6, s32[8,64]{1,0:T(8,128)S(1)} %multiply_add_fusion.1), kind=kOutput, calls=%fused_computation.17 | convolution fusion | flops 809238528 | bytes 1574912 | tf_op jit(solution)/shard_map/xszk,kpl->spxzl/dot_general | solution.py:27
  228.6 0.4 copy.37
  229.0 1.1 pad_maximum_fusion.1
  230.0 6.2 %all-to-all-start.4 = ((f32[2,64,8,1,256]{4,2,0,3,1:T(8,128)}), f32[2,64,8,1,256]{4,2,0,3,1:T(8,128)S(1)}, u32[]{:S(2)}, u32[]{:S(2)}) async-start(f32[2,64,8,1,256]{4,2,0,3,1:T(8,128)} %pad_maximum_fusion.1), calls=%async_computation.4 | async-start | bytes 2097152 | tf_op jit(solution)/shard_map/all_to_all | solution.py:103
  236.3 0.7 copy-done.3
  237.1 26.6 %all-to-all-done.4 = f32[2,64,8,1,256]{4,2,0,3,1:T(8,128)S(1)} async-done(((f32[2,64,8,1,256]{4,2,0,3,1:T(8,128)}), f32[2,64,8,1,256]{4,2,0,3,1:T(8,128)S(1)}, u32[]{:S(2)}, u32[]{:S(2)}) %all-to-all-start.4) | async-done | bytes 1048608 | tf_op jit(solution)/shard_map/all_to_all | solution.py:103
  263.7 1.6 copy.39
  265.3 7.3 %all-to-all-start.5 = ((f32[2,1,8,64,256]{4,3,1,0,2:T(8,128)}), f32[2,1,8,64,256]{4,3,1,0,2:T(8,128)S(1)}, u32[]{:S(2)}, u32[]{:S(2)}) async-start(f32[2,1,8,64,256]{4,3,1,0,2:T(8,128)} %copy.39), calls=%async_computation.5 | async-start | bytes 2097152 | tf_op jit(solution)/shard_map/all_to_all | solution.py:102
  273.0 14.8 %all-to-all-done.5 = f32[2,1,8,64,256]{4,3,1,0,2:T(8,128)S(1)} async-done(((f32[2,1,8,64,256]{4,3,1,0,2:T(8,128)}), f32[2,1,8,64,256]{4,3,1,0,2:T(8,128)S(1)}, u32[]{:S(2)}, u32[]{:S(2)}) %all-to-all-start.5) | async-done | bytes 1048608 | tf_op jit(solution)/shard_map/all_to_all | solution.py:102
  287.8 5.0 %fusion.39 = f32[256,512]{1,0:T(8,128)S(1)} fusion(f32[512,256]{1,0:T(8,128)S(1)} %bitcast.169, s32[512]{0:T(512)S(1)} %fusion.107), kind=kOutput, calls=%fused_computation.70 | convolution fusion | flops 808976384 | bytes 1050624 | tf_op jit(solution)/shard_map/jr,jx->rx/dot_general | solution.py:113
  292.9 5.1 %fusion.3 = f32[32,4,8,128]{3,2,1,0:T(8,128)S(1)} fusion(f32[256,512]{1,0:T(8,128)S(1)} %fusion.39, f32[512,256]{1,0:T(8,128)S(1)} %bitcast.168, s32[512]{0:T(512)S(1)} %fusion.107), kind=kOutput, calls=%fused_computation.24 | convolution fusion | flops 809238528 | bytes 1574912 | tf_op jit(solution)/shard_map/jr,jx->rx/dot_general | solution.py:114
  298.1 23.0 %gather_fusion.2 = f32[4096]{0:T(1024)S(1)} fusion(f32[131072]{0:T(1024)S(1)} %bitcast.163, s32[4096]{0:T(1024)S(1)} %broadcast_clamp_fusion.1), kind=kCustom, calls=%fused_computation.2 | custom fusion | bytes 49152 | tf_op jit(solution)/shard_map/gather | solution.py:116
  321.2 0.8 reshape.394
  322.0 6.1 %all-to-all-start.6 = ((f32[64,8,8]{2,1,0:T(8,128)}), f32[64,8,8]{2,1,0:T(8,128)S(1)}, u32[]{:S(2)}, u32[]{:S(2)}) async-start(f32[64,8,8]{2,1,0:T(8,128)} %reshape.394), calls=%async_computation.6 | async-start | bytes 524288 | tf_op jit(solution)/shard_map/all_to_all | solution.py:118
  328.1 12.2 %all-gather = f32[8,1,512]{2,1,0:T(1,128)S(1)} all-gather(f32[1,1,512]{2,1,0:T(1,128)S(1)} %bitcast.161), channel_id=1, replica_groups=mesh['slab'=64,'patch'=8] {'patch'}, dimensions={0}, use_global_device_ids=true | all-gather | bytes 18432 | tf_op jit(solution)/shard_map/all_gather | solution.py:130
  340.3 45.5 %gather_fusion = f32[8192]{0:T(1024)S(1)} fusion(f32[4096]{0:T(1024)S(1)} %bitcast.162, s32[8192]{0:T(1024)S(1)} %broadcast_clamp_fusion), kind=kCustom, calls=%fused_computation | custom fusion | bytes 98304 | tf_op jit(solution)/shard_map/gather | solution.py:131
  386.0 0.7 reshape.471
  386.7 3.9 all-to-all-start.7
  390.6 0.6 multiply_reduce_fusion
  391.3 0.5 copy-done.8
  392.2 3.1 all-to-all-done.7
  395.2 0.7 reduce.9
  396.3 30.0 %scatter_fusion = f32[512]{0:T(512)} fusion(f32[512]{0:T(512)} %multiply_reduce_fusion, s32[4096]{0:T(1024)S(1)} %bitcast.175, f32[4096]{0:T(1024)S(1)} %multiply_select_fusion.1), kind=kCustom, calls=%fused_computation.4 | custom fusion | flops 4096 | bytes 65536 | tf_op jit(solution)/shard_map/scatter-add | solution.py:128
  (57 shorter events, 3.6 us)
Async XLA Ops:
  0.0 1.2 copy-start.9
  2.3 0.7 copy-start
  29.0 0.7 copy-start.5
  30.8 17.3 %copy-start.6 = (s32[1,512,8]{1,2,0:T(8,128)S(1)}, s32[1,512,8]{1,2,0:T(8,128)}, u32[]{:S(2)}) copy-start(s32[1,512,8]{1,2,0:T(8,128)} %param.16) | copy-start | bytes 49156
  30.8 17.3 %copy-start.7 = (s32[1,512,8]{1,2,0:T(8,128)S(1)}, s32[1,512,8]{1,2,0:T(8,128)}, u32[]{:S(2)}) copy-start(s32[1,512,8]{1,2,0:T(8,128)} %param.15) | copy-start | bytes 49156
  30.8 29.9 %all-to-all-start = ((f32[64,8,8]{1,2,0:T(8,128)}), f32[64,8,8]{1,2,0:T(8,128)S(1)}, u32[]{:S(2)}, u32[]{:S(2)}) async-start(f32[64,8,8]{1,2,0:T(8,128)} %copy.28), calls=%async_computation | async-start | bytes 524288 | tf_op jit(solution)/shard_map/all_to_all | solution.py:61
  61.6 12.2 %all-to-all-start.1 = ((f32[8,1,512]{2,1,0:T(1,128)}), f32[8,1,512]{2,1,0:T(1,128)S(1)}, u32[]{:S(2)}, u32[]{:S(2)}) async-start(f32[8,1,512]{2,1,0:T(1,128)} %reshape.469), calls=%async_computation.1 | async-start | bytes 32768 | tf_op jit(solution)/shard_map/all_to_all | solution.py:60
  141.0 21.9 %all-to-all-start.3 = ((f32[2,8,16384]{2,0,1:T(2,128)}), f32[2,8,16384]{2,0,1:T(2,128)S(1)}, u32[]{:S(2)}, u32[]{:S(2)}) async-start(f32[2,8,16384]{2,0,1:T(2,128)} %bitcast.61), calls=%async_computation.3 | async-start | bytes 2097152 | tf_op jit(solution)/shard_map/all_to_all | solution.py:80
  189.9 1.9 copy-start.1
  230.0 33.7 %all-to-all-start.4 = ((f32[2,64,8,1,256]{4,2,0,3,1:T(8,128)}), f32[2,64,8,1,256]{4,2,0,3,1:T(8,128)S(1)}, u32[]{:S(2)}, u32[]{:S(2)}) async-start(f32[2,64,8,1,256]{4,2,0,3,1:T(8,128)} %pad_maximum_fusion.1), calls=%async_computation.4 | async-start | bytes 2097152 | tf_op jit(solution)/shard_map/all_to_all | solution.py:103
  236.2 0.8 copy-start.3
  265.3 7.3 %copy-start.2 = (s32[1,512,8]{1,2,0:T(8,128)S(1)}, s32[1,512,8]{1,2,0:T(8,128)}, u32[]{:S(2)}) copy-start(s32[1,512,8]{1,2,0:T(8,128)} %param.12) | copy-start | bytes 49156
  265.3 22.4 %all-to-all-start.5 = ((f32[2,1,8,64,256]{4,3,1,0,2:T(8,128)}), f32[2,1,8,64,256]{4,3,1,0,2:T(8,128)S(1)}, u32[]{:S(2)}, u32[]{:S(2)}) async-start(f32[2,1,8,64,256]{4,3,1,0,2:T(8,128)} %copy.39), calls=%async_computation.5 | async-start | bytes 2097152 | tf_op jit(solution)/shard_map/all_to_all | solution.py:102
  322.0 63.8 %all-to-all-start.6 = ((f32[64,8,8]{2,1,0:T(8,128)}), f32[64,8,8]{2,1,0:T(8,128)S(1)}, u32[]{:S(2)}, u32[]{:S(2)}) async-start(f32[64,8,8]{2,1,0:T(8,128)} %reshape.394), calls=%async_computation.6 | async-start | bytes 524288 | tf_op jit(solution)/shard_map/all_to_all | solution.py:118
  385.9 4.6 %copy-start.4 = (f32[16,512]{1,0:T(8,128)S(1)}, f32[16,512]{1,0:T(8,128)}, u32[]{:S(2)}) copy-start(f32[16,512]{1,0:T(8,128)} %param.19) | copy-start | bytes 98308
  386.7 8.5 %all-to-all-start.7 = ((f32[8,1,512]{2,1,0:T(1,128)}), f32[8,1,512]{2,1,0:T(1,128)S(1)}, u32[]{:S(2)}, u32[]{:S(2)}) async-start(f32[8,1,512]{2,1,0:T(1,128)} %reshape.471), calls=%async_computation.7 | async-start | bytes 32768 | tf_op jit(solution)/shard_map/all_to_all | solution.py:117
  391.2 0.7 copy-start.8
where the time goes:
time: 431 us; the launch traced here: 426 us
  local copies, waits for them, and re-layouts  113 us (26%)
  matrix products  80.9 us (19%)
  waiting for transfers between devices  75.8 us (18%)
  other arithmetic  57.1 us (13%)
  starting transfers between devices  55.6 us (13%)
  blocking collectives  43.5 us (10%)
    gather x2, local copies, waits for them, and re-layouts, per_device(): near = jnp.sum(near_coef * group[near_index], axis=0)  45.5 us
    all_to_all x1, blocking collectives, per_device(): lax.all_to_all(stacked, 'slab', split_axis=1, concat_axis=2, tiled=True)  31.3 us
    scatter-add x1, other arithmetic, per_device(): interp = jnp.zeros((density.shape[0],), jnp.float32).at[send_panel[0].res...  30 us
    all_to_all x1, waiting for transfers between devices, per_device(): lax.all_to_all(leaving, 'slab', split_axis=1, concat_axis=3, tiled=True)  26.6 us
    gather x3, local copies, waits for them, and re-layouts, per_device(): items = jnp.where(in_use, send_weight[0] * density[send_panel[0]], 0.0)  26.3 us
    gather x1, local copies, waits for them, and re-layouts, per_device(): sampled = field.reshape(-1)[cells].reshape(n_slab, n_patch, capacity)  23 us
    scatter-add x1, other arithmetic, per_device(): grid = jnp.zeros((plane * size_x,), jnp.float32).at[cells].add(arrived.re...  22.3 us
    all_to_all x1, starting transfers between devices, per_device(): lax.all_to_all(outgoing, 'slab', split_axis=0, concat_axis=0, tiled=True)  17.3 us
  transfers between devices with their start and end apart: 7, of which 6 were waited for; matrix products, arithmetic and copies ran while one was open for 11% of the time, Pallas kernels for 0%

commit v1 on v0

v1 whole, which is shorter than its diff:
```python
import math

import jax
import jax.numpy as jnp
import ml_dtypes
import numpy as np
from jax import lax
from jax.experimental import pallas as pl
from jax.experimental.pallas import tpu as pltpu
from jax.sharding import PartitionSpec as P

NX, NY, NZ = 512, 512, 256
N_SLAB, N_PATCH, CAP = 64, 8, 8
DEVICES = N_SLAB * N_PATCH
F32, BF16, I32 = jnp.float32, jnp.bfloat16, jnp.int32
MIB = 1024 * 1024


def halves(table):
    high = table.astype(np.float32).astype(ml_dtypes.bfloat16)
    low = (table - high.astype(np.float64)).astype(np.float32).astype(ml_dtypes.bfloat16)
    return np.stack([high, low])


def waves(first, second, length):
    turns = np.outer(first, second) % length
    angles = turns * (2.0 * np.pi / length)
    cosine, sine = np.cos(angles), np.sin(angles)
    cosine[(4 * turns == length) | (4 * turns == 3 * length)] = 0.0
    sine[(turns == 0) | (2 * turns == length)] = 0.0
    return cosine, sine


def x_tables():
    cosine, sine = waves(np.arange(64), np.arange(64), 64)
    forward = np.block([[cosine, sine], [-sine, cosine]])
    backward = np.block([[cosine, -sine], [sine, cosine]])
    return halves(forward), halves(backward)


def y_tables():
    cosine, sine = waves(np.arange(NY), np.arange(NY // 2), NY)
    sine[:, 0] = 1.0 - 2.0 * (np.arange(NY) % 2)
    return halves(np.concatenate([cosine, sine], axis=1)), halves(np.concatenate([cosine.T, sine.T], axis=0))


def z_tables():
    cosine, sine = waves(np.arange(NZ), np.arange(NZ), NZ)
    depth = NZ // N_SLAB

    def rows(re_part, im_part):
        parts = np.stack([re_part.reshape(N_SLAB, depth, -1), im_part.reshape(N_SLAB, depth, -1)], axis=1)
        return parts.reshape(2 * NZ, -1)

    forward = np.concatenate([rows(cosine, sine), rows(-sine, cosine)], axis=1).T
    backward = np.concatenate([rows(cosine, sine), rows(-sine, cosine)], axis=1)
    return halves(forward), halves(backward)


def split(value):
    high = value.astype(BF16)
    return high, (value - high.astype(F32)).astype(BF16)


def mul(a, b):
    return jnp.dot(a, b, preferred_element_type=F32)


def data_by_table(value, table_ref):
    high, low = split(value)
    return mul(high, table_ref[0]) + mul(low, table_ref[0]) + mul(high, table_ref[1])


def table_by_data(table_ref, value):
    high, low = split(value)
    return mul(table_ref[0], high) + mul(table_ref[0], low) + mul(table_ref[1], high)


def across(a, b):
    return lax.dot_general(
        a, b, (((1,), (1,)), ((), ())), precision=lax.Precision.HIGHEST, preferred_element_type=F32
    )


def iota(shape, dim):
    return lax.broadcasted_iota(I32, shape, dim)


def spread(values):
    keep = (iota((8, DEVICES), 1) & 7) == iota((8, DEVICES), 0)
    rows = [jnp.where(keep, jnp.broadcast_to(values[c : c + 1, :], (8, DEVICES)), 0.0) for c in range(CAP)]
    return jnp.concatenate(rows, axis=0)


def slab_of():
    return ((iota((N_SLAB, DEVICES), 1) >> 3) == iota((N_SLAB, DEVICES), 0)).astype(F32)


def paired(values):
    rows = [
        jnp.concatenate([values[16 * q : 16 * q + 8, :], values[16 * q + 8 : 16 * q + 16, :]], axis=1)
        for q in range(CAP // 2)
    ]
    return jnp.concatenate(rows, axis=0)


def unpaired(values):
    rows = []
    for q in range(CAP // 2):
        rows.append(values[8 * q : 8 * q + 8, :64])
        rows.append(values[8 * q : 8 * q + 8, 64:])
    return jnp.concatenate(rows, axis=0)


def lookup(row, places):
    return jnp.take_along_axis(
        jnp.broadcast_to(row, places.shape), places, axis=1, mode="promise_in_bounds"
    )


def items_kernel(density, counts, panel, weight, row, col, out, cells):
    used = iota((CAP, DEVICES), 0) < counts[...]
    picked = []
    for j in range(4):
        places = panel[:, 128 * j : 128 * (j + 1)]
        low, high = places & 127, places >> 7
        value = jnp.zeros(places.shape, F32)
        for h in range(4):
            value = jnp.where(high == h, lookup(density[h : h + 1, :], low), value)
        picked.append(value)
    items = jnp.where(used, weight[...] * jnp.concatenate(picked, axis=1), 0.0)
    slab = slab_of()
    out[:, 0, :] = across(slab, spread(items))
    place = (row[...] * NX + col[...]).astype(F32)
    cells[...] = paired(across(spread(place), slab))


def message_kernel(arrived, cells, density, out):
    items = paired(arrived[:, 0, :].T)
    for p in range(N_PATCH):
        out[p, 0:32, :] = items
        out[p, 32:64, :] = cells[...]
        out[p, 64:68, :] = density[...]
        out[p, 68:72, :] = density[...]


def phases(cell, p):
    place = (cell + 0.5).astype(I32)
    col = place & (NX - 1)
    angle = ((col * p) & (NX - 1)).astype(F32) * (2.0 * math.pi / NX)
    return (place >> 9).astype(F32), (col & 63).astype(F32), jnp.cos(angle), jnp.sin(angle)


def lanes(ref, block, p, kind=0):
    rows = [ref[kind, block, pl.ds(8 * q + p, 1), :] for q in range(4)]
    return jnp.concatenate(rows, axis=1)


def thick(row, count):
    return jnp.concatenate([jnp.broadcast_to(row, (16, row.shape[1])).astype(BF16)] * count, axis=0)


def one_hot(row, count, size):
    steps = lax.broadcasted_iota(I32, (size, row.shape[1]), 0).astype(F32).astype(BF16)
    return thick(row, count) == steps


def forward_kernel(meta, data, x_table, y_table, out, slots, lines):
    p = meta[0]
    for q in range(4):
        for sender in range(N_PATCH):
            slots[4, :, 8 * q + sender, :] = data[sender, 8 * q : 8 * q + 8, :]
    for block in range(N_PATCH):
        row, low_col, cosine, sine = phases(data[block, 32:64, :], p)
        slots[0, block] = row
        slots[1, block] = low_col
        slots[2, block] = slots[4, block] * cosine
        slots[3, block] = -slots[4, block] * sine

    def one_block(block, carry):
        total = jnp.zeros((256, 256), F32)
        for sender in range(N_PATCH):
            in_row = one_hot(lanes(slots, block, sender, 0), 16, 256)
            in_col = one_hot(lanes(slots, block, sender, 1), 4, 64)
            none = jnp.zeros((64, 512), BF16)
            re_high, re_low = split(lanes(slots, block, sender, 2))
            im_high, im_low = split(lanes(slots, block, sender, 3))
            parts = [jnp.where(in_col, thick(v.astype(F32), 4), none) for v in (re_high, im_high, re_low, im_low)]
            ones = jnp.where(in_row, jnp.ones((256, 512), BF16), jnp.zeros((256, 512), BF16))
            total = total + lax.dot_general(
                jnp.concatenate(parts, axis=0),
                ones,
                (((1,), (1,)), ((), ())),
                preferred_element_type=F32,
            )
        lines[block] = table_by_data(x_table, total[:128, :] + total[128:, :])
        return carry

    lax.fori_loop(0, N_PATCH, one_block, 0)
    lower = iota((128, 128), 1) < 64
    kx = 8 * iota((64, 256), 0) + p
    first = iota((64, 256), 1) == 0
    alone = (kx == 0) | (kx == NX // 2)
    for z in range(4):
        at = slice(128 * (z // 2), 128 * (z // 2) + 128)
        tiles = []
        for t in range(4):
            even, odd = lines[2 * t, :, at], lines[2 * t + 1, :, at]
            if z % 2 == 0:
                tiles.append(jnp.where(lower, even, pltpu.roll(odd, 64, 1)))
            else:
                tiles.append(jnp.where(lower, pltpu.roll(even, 64, 1), odd))
        both = data_by_table(jnp.concatenate(tiles, axis=1), y_table)
        re_cos, re_sin = both[:64, :256], both[:64, 256:]
        im_cos, im_sin = both[64:, :256], both[64:, 256:]
        re_first = jnp.where(kx <= NX // 2, re_cos, re_sin)
        im_first = jnp.where(alone, re_sin, jnp.where(kx < NX // 2, im_cos, im_sin))
        out[:, z, :] = jnp.where(first, re_first, re_cos + im_sin)
        out[:, 4 + z, :] = jnp.where(first, im_first, im_cos - re_sin)


def spectrum_kernel(factor, kernel, lines, forward, backward, out):
    size = NY // 2
    green = kernel[0, :size, :].T
    base = factor[4]
    low, mid = kernel[0, 0:8, :].T[:, 0:1], kernel[0, size : size + 8, :].T[:, 0:1]
    first = iota((NZ, size), 1) == 0
    own = jnp.where(first, factor[0] * low + factor[1] * mid, base * green)
    mirrored = jnp.where(first[:, :128], factor[2] * low + factor[3] * mid, 0.0)
    value = lines[...].reshape(2 * NZ, size)
    sign = jnp.where((iota((2 * NZ, 128), 0) & 4) == 0, 1.0, -1.0)
    wave = table_by_data(forward, value)
    turned = table_by_data(forward, value[:, :128] * sign)
    left = jnp.concatenate([own[:, :128]] * 2, axis=0) * wave[:, :128]
    left = left + jnp.concatenate([mirrored] * 2, axis=0) * turned
    right = jnp.concatenate([own[:, 128:]] * 2, axis=0) * wave[:, 128:]
    scaled = jnp.concatenate([left, right], axis=1)
    out[...] = table_by_data(backward, scaled).reshape(N_SLAB, 8, size)


def backward_kernel(meta, arrived, data, x_table, y_table, out, slots, planes, blocks):
    p = meta[0]
    for block in range(N_PATCH):
        row, low_col, cosine, sine = phases(data[block, 32:64, :], p)
        slots[0, block] = row
        slots[1, block] = low_col
        slots[2, block] = cosine
        slots[3, block] = sine
    value = arrived[...].reshape(512, 256)
    place = iota((512, 256), 0)
    real = (place & 4) == 0
    kx = 8 * (place >> 3) + p
    first = iota((512, 256), 1) == 0
    alone = (kx == 0) | (kx == NX // 2)
    after, before = pltpu.roll(value, 508, 0), pltpu.roll(value, 4, 0)
    keep = (kx <= NX // 2) & (real | ~alone)
    straight = jnp.where(first & ~keep, 0.0, value)
    other = jnp.where(kx > NX // 2, value, jnp.where(alone & real, after, 0.0))
    crossed = jnp.where(first, other, jnp.where(real, -after, before))
    planes[...] = data_by_table(jnp.concatenate([straight, crossed], axis=1), y_table).reshape(64, 8, 512)
    lower = iota((128, 128), 1) < 64
    for pair in range(2):
        plane = []
        for z in (2 * pair, 2 * pair + 1):
            both = jnp.concatenate([planes[:, z, :], planes[:, 4 + z, :]], axis=0)
            plane.append(table_by_data(x_table, both))
        for t in range(4):
            even = plane[0][:, 128 * t : 128 * (t + 1)]
            odd = plane[1][:, 128 * t : 128 * (t + 1)]
            for block, tile in (
                (2 * t, jnp.where(lower, even, pltpu.roll(odd, 64, 1))),
                (2 * t + 1, jnp.where(lower, pltpu.roll(even, 64, 1), odd)),
            ):
                high, low = split(tile)
                blocks[block, :128, 128 * pair : 128 * (pair + 1)] = high
                blocks[block, 128:, 128 * pair : 128 * (pair + 1)] = low

    steps = iota((64, 512), 0).astype(F32)

    def one_block(block, carry):
        field = blocks[block]
        for sender in range(N_PATCH):
            in_row = one_hot(lanes(slots, block, sender, 0), 16, 256)
            ones = jnp.where(in_row, jnp.ones((256, 512), BF16), jnp.zeros((256, 512), BF16))
            near = mul(field, ones)
            re_part = near[0:64] + near[128:192]
            im_part = near[64:128] + near[192:256]
            turned = re_part * lanes(slots, block, sender, 2) - im_part * lanes(slots, block, sender, 3)
            in_col = lanes(slots, block, sender, 1) == steps
            found = jnp.sum(jnp.where(in_col, turned, 0.0), axis=0, keepdims=True)
            for q in range(4):
                out[sender, pl.ds(8 * q + block, 1), :] = found[:, 128 * q : 128 * (q + 1)]
        return carry

    lax.fori_loop(0, N_PATCH, one_block, 0)


def sum_kernel(parts, out):
    total = parts[0]
    for p in range(1, N_PATCH):
        total = total + parts[p]
    out[:, 0, :] = unpaired(total).T


def near_kernel(data, index, coef, out):
    for j in range(4):
        at = slice(128 * j, 128 * (j + 1))
        total = jnp.zeros((8, 128), F32)
        for half in range(2):
            places = index[8 * half : 8 * half + 8, at]
            low, high = places & 127, places >> 7
            value = jnp.zeros(places.shape, F32)
            for h in range(32):
                value = jnp.where(high == h, lookup(data[h // 4, 64 + h % 4 : 65 + h % 4, :], low), value)
            total = total + coef[8 * half : 8 * half + 8, at] * value
        out[j : j + 1, :] = jnp.sum(total, axis=0, keepdims=True)


def interp_kernel(arrived, counts, panel, weight, near, out):
    used = iota((CAP, DEVICES), 0) < counts[...]
    wide = across(arrived[:, 0, :].T, slab_of().T)
    keep = (iota((64, DEVICES), 1) & 7) == (iota((64, DEVICES), 0) & 7)
    wide = jnp.where(keep, wide, 0.0)
    rows = [jnp.sum(wide[8 * c : 8 * c + 8, :], axis=0, keepdims=True) for c in range(CAP)]
    terms = jnp.where(used, weight[...] * jnp.concatenate(rows, axis=0), 0.0)
    places = panel[...]
    low, high = places & 127, places >> 7
    total = jnp.zeros((16, 128), F32)
    part = iota((16, DEVICES), 0)
    for c in range(CAP):
        term = terms[c : c + 1, :]
        top = term.astype(BF16).astype(F32)
        middle = (term - top).astype(BF16).astype(F32)
        bottom = term - top - middle
        shown = jnp.where(part < 4, top, jnp.where(part < 8, middle, jnp.where(part < 12, bottom, 0.0)))
        left = jnp.where((part & 3) == high[c : c + 1, :], shown, 0.0).astype(BF16)
        right = (iota((128, DEVICES), 0) == low[c : c + 1, :]).astype(F32).astype(BF16)
        total = total + lax.dot_general(left, right, (((1,), (1,)), ((), ())), preferred_element_type=F32)
    out[...] = total[0:4] + total[4:8] + total[8:12] + near[...]


VMEM = pl.BlockSpec(memory_space=pltpu.VMEM)
SMEM = pl.BlockSpec(memory_space=pltpu.SMEM)


def call(kernel, shapes, args, scratch=(), scalars=0, vmem=16, flops=0):
    many = isinstance(shapes, list)
    outs = [jax.ShapeDtypeStruct(s, F32) for s in (shapes if many else [shapes])]
    moved = 4 * sum(math.prod(o.shape) for o in outs) + sum(a.size * a.dtype.itemsize for a in args)
    return pl.pallas_call(
        kernel,
        out_shape=outs if many else outs[0],
        in_specs=[SMEM] * scalars + [VMEM] * (len(args) - scalars),
        out_specs=[VMEM] * len(outs) if many else VMEM,
        scratch_shapes=list(scratch),
        compiler_params=pltpu.CompilerParams(vmem_limit_bytes=vmem * MIB),
        cost_estimate=pl.CostEstimate(flops=flops, bytes_accessed=moved, transcendentals=0),
    )(*args)


def exchange(value, axis):
    return lax.all_to_all(value, axis, split_axis=0, concat_axis=0, tiled=True)


def per_device(
    density,
    counts,
    send_panel,
    send_weight,
    interp_weight,
    recv_row,
    recv_col,
    kernel,
    near_index,
    near_coef,
):
    p = lax.axis_index("patch").astype(I32)
    own = lax.axis_index("slab").astype(I32) * N_PATCH + p
    meta = jnp.stack([p, own])
    x_forward, x_backward = (jnp.asarray(t) for t in x_tables())
    y_forward, y_backward = (jnp.asarray(t) for t in y_tables())
    z_forward, z_backward = (jnp.asarray(t) for t in z_tables())
    charge = density.reshape(4, 128)
    panel, weight, back_weight, row, col = (
        jnp.transpose(a[0]) for a in (send_panel, send_weight, interp_weight, recv_row, recv_col)
    )

    items, cells = call(
        items_kernel, [(N_SLAB, 1, 64), (32, 128)], [charge, counts, panel, weight, row, col]
    )
    arrived = exchange(items, "slab")
    message = call(message_kernel, (N_PATCH, 72, 128), [arrived, cells, charge])
    data = exchange(message, "patch")
    near = call(near_kernel, (4, 128), [data, near_index, near_coef])

    lines = call(
        forward_kernel,
        (N_SLAB, 8, 256),
        [meta, data, x_forward, y_forward],
        [pltpu.VMEM((5, N_PATCH, 32, 128), F32), pltpu.VMEM((N_PATCH, 128, 256), F32)],
        scalars=1,
        vmem=32,
    )
    lines = exchange(lines, "slab")

    unit = 2.0 / (NX * NY * NZ)
    alone = (own == 0) | (own == NX // 2)
    below = own < NX // 2
    factor = jnp.stack(
        [
            jnp.where(alone, 0.25 * unit, jnp.where(below, unit, 0.0)),
            jnp.where(alone, 0.25 * unit, jnp.where(below, 0.0, unit)),
            jnp.where(alone, 0.25 * unit, 0.0),
            jnp.where(alone, -0.25 * unit, 0.0),
            jnp.full((), unit, F32),
        ]
    ).astype(F32)
    lines = call(
        spectrum_kernel,
        (N_SLAB, 8, 256),
        [factor, kernel, lines, z_forward, z_backward],
        scalars=1,
        vmem=24,
    )
    lines = exchange(lines, "slab")
    parts = call(
        backward_kernel,
        (N_PATCH, 32, 128),
        [meta, lines, data, x_backward, y_backward],
        [
            pltpu.VMEM((4, N_PATCH, 32, 128), F32),
            pltpu.VMEM((N_SLAB, 8, 512), F32),
            pltpu.VMEM((N_PATCH, 256, 256), BF16),
        ],
        scalars=1,
        vmem=32,
    )
    parts = exchange(parts, "patch")
    sampled = call(sum_kernel, (N_SLAB, 1, 64), [parts])
    sampled = exchange(sampled, "slab")
    result = call(interp_kernel, (4, 128), [sampled, counts, panel, back_weight, near])
    return result.reshape(-1)


def solution(mesh):
    placed = (
        P(("slab", "patch")),
        P(("slab", "patch"), None),
        P(("slab", "patch"), None, None),
        P(("slab", "patch"), None, None),
        P(("slab", "patch"), None, None),
        P(("slab", "patch"), None, None),
        P(("slab", "patch"), None, None),
        P(("slab", "patch"), None, None),
        P(None, ("slab", "patch")),
        P(None, ("slab", "patch")),
    )
    return jax.shard_map(
        per_device, mesh=mesh, in_specs=placed, out_specs=P(("slab", "patch")), check_vma=False
    )
```

time: 431 us -> 145 us (0.34)
  local copies, waits for them, and re-layouts: 113 us -> 4.46 us
  matrix products: 80.9 us -> 0 us
  other arithmetic: 57.1 us -> 0.07 us
  waiting for transfers between devices: 75.8 us -> 34.2 us
  starting transfers between devices: 55.6 us -> 16.1 us
  Pallas kernels: 0 us -> 26.7 us
  blocking collectives: 43.5 us -> 62.7 us
    gather x6 -> x0, local copies, waits for them, and re-layouts: 94.9 us -> none  [the longest x2 45.5 us: per_device(): near = jnp.sum(near_coef * group[near_index], axis=0)]
    dot_general x20 -> x0, matrix products: 80.9 us -> none  [the longest x4 15.5 us: rotate(): jnp.einsum(pattern, real_part, sine_table, precision=HIGH)]
    scatter-add x2 -> x0, other arithmetic: 52.4 us -> none  [the longest x1 30 us: per_device(): interp = jnp.zeros((density.shape[0],), jnp.float32).at[send_panel[0].res...]
    all_to_all x7 -> x3, waiting for transfers between devices: 75.8 us -> 34.2 us  [exchange(): return lax.all_to_all(value, axis, split_axis=0, concat_axis=0, tiled=True)]
    all_to_all x7 -> x3, starting transfers between devices: 55.6 us -> 16.1 us  [exchange(): return lax.all_to_all(value, axis, split_axis=0, concat_axis=0, tiled=True)]
    all_to_all x1 -> x3, blocking collectives: 31.3 us -> 62.7 us  [exchange(): return lax.all_to_all(value, axis, split_axis=0, concat_axis=0, tiled=True)]
    pallas_call x0 -> x8, Pallas kernels: none -> 26.7 us  [call(): pl.pallas_call(kernel, out_shape=outs if many else outs[0], in_specs=[SME...]
    all_gather x1 -> x0, blocking collectives: 12.2 us -> none  [per_device(): group = lax.all_gather(density, 'patch', axis=0, tiled=True)]
  transfers between devices with their start and end apart: 7 -> 3, of which waited for: 6 -> 3; matrix products, arithmetic and copies ran while one was open for 11% -> 0% of each run, Pallas kernels for 0% -> 0%
where the time goes in v1:
time: 145 us; the launch traced here: 144 us
  blocking collectives  62.7 us (43%)
  waiting for transfers between devices  34.2 us (24%)
  Pallas kernels  26.7 us (18%)
  starting transfers between devices  16.1 us (11%)
  local copies, waits for them, and re-layouts  4.46 us (3%)
    all_to_all x3, blocking collectives, exchange(): return lax.all_to_all(value, axis, split_axis=0, concat_axis=0, tiled=True)  62.7 us
    all_to_all x3, waiting for transfers between devices, exchange(): return lax.all_to_all(value, axis, split_axis=0, concat_axis=0, tiled=True)  34.2 us
    pallas_call x8, Pallas kernels, call(): pl.pallas_call(kernel, out_shape=outs if many else outs[0], in_specs=[SME...  26.7 us
    all_to_all x3, starting transfers between devices, exchange(): return lax.all_to_all(value, axis, split_axis=0, concat_axis=0, tiled=True)  16.1 us
    unnamed x36, local copies, waits for them, and re-layouts  4.38 us
  transfers between devices with their start and end apart: 3, of which 3 were waited for; matrix products, arithmetic and copies ran while one was open for 0% of the time, Pallas kernels for 0%

profile of v1, /device:TPU:1, one launch (start us, length us, event | category | flops | bytes accessed | tf_op | source)
XLA Modules:
  0.0 144.4 jit_solution(9981463654022878001)
XLA Ops:
  0.0 0.0 copy-start.1
  0.0 0.0 copy-start.7
  0.0 0.8 copy-done.7
  0.8 0.0 copy-start.11
  0.8 0.7 copy-done.11
  1.5 0.0 copy-start.12
  1.5 0.7 copy-done.12
  2.2 0.0 copy-start.13
  2.2 0.7 copy-done.13
  3.0 0.0 copy-start.15
  3.0 0.7 copy-done.15
  3.6 0.0 copy-start.16
  3.6 0.7 copy-done.16
  4.3 0.4 shard_map.154
  4.8 27.8 %all_to_all.30.arrived = f32[64,1,64]{2,1,0:T(1,128)S(1)} all-to-all(f32[64,1,64]{2,1,0:T(1,128)S(1)} %get-tuple-element.7), channel_id=1, replica_groups=mesh['slab'=64,'patch'=8] {'slab'}, dimensions={0} | all-to-all | bytes 32768 | tf_op jit(solution)/shard_map/all_to_all | solution.py:362
  32.6 0.9 shard_map.155
  33.4 0.0 copy-start.6
  33.4 6.5 %all-to-all-start.1 = ((f32[8,72,128]{2,1,0:T(8,128)}), f32[8,72,128]{2,1,0:T(8,128)S(1)}, u32[]{:S(2)}, u32[]{:S(2)}) async-start(f32[8,72,128]{2,1,0:T(8,128)} %shard_map.155), calls=%async_computation.1 | async-start | bytes 589824 | tf_op jit(solution)/shard_map/all_to_all | solution.py:362
  40.0 0.1 pad_add_fusion.meta
  40.0 0.0 copy-start.2
  40.0 0.0 copy-start.3
  40.0 6.7 %all-to-all-done.1.data = f32[8,72,128]{2,1,0:T(8,128)S(1)} async-done(((f32[8,72,128]{2,1,0:T(8,128)}), f32[8,72,128]{2,1,0:T(8,128)S(1)}, u32[]{:S(2)}, u32[]{:S(2)}) %all-to-all-start.1) | async-done | bytes 294944 | tf_op jit(solution)/shard_map/all_to_all | solution.py:362
  46.8 0.0 copy-done.1
  46.8 0.0 copy-done.6
  46.8 11.3 %shard_map.156 = f32[64,8,256]{2,1,0:T(8,128)} custom-call(s32[2]{0:T(128)S(1)} %pad_add_fusion.meta, f32[8,72,128]{2,1,0:T(8,128)S(1)} %all-to-all-done.1.data, bf16[2,128,128]{2,1,0:T(8,128)(2,1)S(1)} %copy-done.6, bf16[2,512,512]{2,1,0:T(8,128)(2,1)S(1)} %copy-done.1), custom_call_target="tpu_custom_call" | custom-call | bytes 1933320 | tf_op jit(solution)/shard_map/pallas_call | solution.py:350
  58.1 0.0 copy-start.4
  58.1 4.8 %all-to-all-start.2 = ((f32[64,8,256]{2,1,0:T(8,128)}), f32[64,8,256]{2,1,0:T(8,128)S(1)}, u32[]{:S(2)}, u32[]{:S(2)}) async-start(f32[64,8,256]{2,1,0:T(8,128)} %shard_map.156), calls=%async_computation.2 | async-start | bytes 1048576 | tf_op jit(solution)/shard_map/all_to_all | solution.py:362
  62.9 0.1 stack.31.factor
  63.0 17.1 %all-to-all-done.2.lines = f32[64,8,256]{2,1,0:T(8,128)S(1)} async-done(((f32[64,8,256]{2,1,0:T(8,128)}), f32[64,8,256]{2,1,0:T(8,128)S(1)}, u32[]{:S(2)}, u32[]{:S(2)}) %all-to-all-start.2) | async-done | bytes 524320 | tf_op jit(solution)/shard_map/all_to_all | solution.py:362
  80.1 0.0 copy-done.2
  80.1 0.0 copy-done.3
  80.1 0.0 copy-done.4
  80.1 0.0 copy-start.5
  80.1 2.8 %shard_map.157 = f32[64,8,256]{2,1,0:T(8,128)S(1)} custom-call(f32[5]{0:T(128)S(1)} %stack.31.factor, f32[1,512,256]{2,1,0:T(8,128)S(1)} %copy-done.4, f32[64,8,256]{2,1,0:T(8,128)S(1)} %all-to-all-done.2.lines, bf16[2,512,512]{2,1,0:T(8,128)(2,1)S(1)} %copy-done.2, bf16[2,512,512]{2,1,0:T(8,128)(2,1)S(1)} %copy-done.3), custom_call_target="tpu_custom_call" | custom-call | bytes 3670036 | tf_op jit(solution)/shard_map/pallas_call | solution.py:350
  82.9 0.0 copy-start
  82.9 22.4 %all_to_all.31.arrived = f32[64,8,256]{2,1,0:T(8,128)S(1)} all-to-all(f32[64,8,256]{2,1,0:T(8,128)S(1)} %shard_map.157), channel_id=1, replica_groups=mesh['slab'=64,'patch'=8] {'slab'}, dimensions={0} | all-to-all | bytes 1048576 | tf_op jit(solution)/shard_map/all_to_all | solution.py:362
  105.3 0.0 copy-done.5
  105.3 0.0 copy-done
  105.3 8.8 %shard_map.158 = f32[8,32,128]{2,1,0:T(8,128)S(1)} custom-call(s32[2]{0:T(128)S(1)} %pad_add_fusion.meta, f32[64,8,256]{2,1,0:T(8,128)S(1)} %all_to_all.31.arrived, f32[8,72,128]{2,1,0:T(8,128)S(1)} %all-to-all-done.1.data, bf16[2,128,128]{2,1,0:T(8,128)(2,1)S(1)} %copy-done.5, bf16[2,512,512]{2,1,0:T(8,128)(2,1)S(1)} %copy-done), custom_call_target="tpu_custom_call" | custom-call | bytes 2064392 | tf_op jit(solution)/shard_map/pallas_call | solution.py:350
  114.1 12.5 %all_to_all.32.parts = f32[8,32,128]{2,1,0:T(8,128)S(1)} all-to-all(f32[8,32,128]{2,1,0:T(8,128)S(1)} %shard_map.158), channel_id=1, replica_groups=mesh['slab'=64,'patch'=8] {'patch'}, dimensions={0} | all-to-all | bytes 262144 | tf_op jit(solution)/shard_map/all_to_all | solution.py:362
  126.6 0.8 shard_map.159
  127.4 0.0 copy-start.9
  127.4 0.0 copy-start.10
  127.4 4.8 %all-to-all-start.5 = ((f32[64,1,64]{2,1,0:T(1,128)}), f32[64,1,64]{2,1,0:T(1,128)S(1)}, u32[]{:S(2)}, u32[]{:S(2)}) async-start(f32[64,1,64]{2,1,0:T(1,128)} %shard_map.159), calls=%async_computation.5 | async-start | bytes 65536 | tf_op jit(solution)/shard_map/all_to_all | solution.py:362
  132.2 0.0 copy-done.9
  132.2 0.0 copy-done.10
  132.3 0.0 copy-start.8
  132.3 0.0 copy-start.14
  132.3 0.0 copy-start.17
  132.3 0.4 shard_map.160.near
  132.7 10.4 %all-to-all-done.5.arrived = f32[64,1,64]{2,1,0:T(1,128)S(1)} async-done(((f32[64,1,64]{2,1,0:T(1,128)}), f32[64,1,64]{2,1,0:T(1,128)S(1)}, u32[]{:S(2)}, u32[]{:S(2)}) %all-to-all-start.5) | async-done | bytes 16416 | tf_op jit(solution)/shard_map/all_to_all | solution.py:362
  143.1 0.0 copy-done.8
  143.1 0.0 copy-done.14
  143.1 0.0 copy-done.17
  143.1 1.3 shard_map.161
Async XLA Ops:
  0.0 46.8 %copy-start.1 = (bf16[2,512,512]{2,1,0:T(8,128)(2,1)S(1)}, bf16[2,512,512]{2,1,0:T(8,128)(2,1)}, u32[]{:S(2)}) copy-start(bf16[2,512,512]{2,1,0:T(8,128)(2,1)} %constant.39.clone.y_table) | copy-start | bytes 3145732
  0.0 0.8 copy-start.7
  0.8 0.7 copy-start.11
  1.5 0.7 copy-start.12
  2.2 0.7 copy-start.13
  3.0 0.7 copy-start.15
  3.6 0.7 copy-start.16
  33.4 13.4 %copy-start.6 = (bf16[2,128,128]{2,1,0:T(8,128)(2,1)S(1)}, bf16[2,128,128]{2,1,0:T(8,128)(2,1)}, u32[]{:S(2)}) copy-start(bf16[2,128,128]{2,1,0:T(8,128)(2,1)} %constant.37.clone.x_table) | copy-start | bytes 196612
  33.4 13.3 %all-to-all-start.1 = ((f32[8,72,128]{2,1,0:T(8,128)}), f32[8,72,128]{2,1,0:T(8,128)S(1)}, u32[]{:S(2)}, u32[]{:S(2)}) async-start(f32[8,72,128]{2,1,0:T(8,128)} %shard_map.155), calls=%async_computation.1 | async-start | bytes 589824 | tf_op jit(solution)/shard_map/all_to_all | solution.py:362
  40.0 40.0 %copy-start.2 = (bf16[2,512,512]{2,1,0:T(8,128)(2,1)S(1)}, bf16[2,512,512]{2,1,0:T(8,128)(2,1)}, u32[]{:S(2)}) copy-start(bf16[2,512,512]{2,1,0:T(8,128)(2,1)} %constant.41.clone.forward) | copy-start | bytes 3145732
  40.0 40.0 %copy-start.3 = (bf16[2,512,512]{2,1,0:T(8,128)(2,1)S(1)}, bf16[2,512,512]{2,1,0:T(8,128)(2,1)}, u32[]{:S(2)}) copy-start(bf16[2,512,512]{2,1,0:T(8,128)(2,1)} %constant.42.clone.backward) | copy-start | bytes 3145732
  58.1 22.0 %copy-start.4 = (f32[1,512,256]{2,1,0:T(8,128)S(1)}, f32[1,512,256]{2,1,0:T(8,128)}, u32[]{:S(2)}) copy-start(f32[1,512,256]{2,1,0:T(8,128)} %kernel.1) | copy-start | bytes 1572868
  58.1 22.0 %all-to-all-start.2 = ((f32[64,8,256]{2,1,0:T(8,128)}), f32[64,8,256]{2,1,0:T(8,128)S(1)}, u32[]{:S(2)}, u32[]{:S(2)}) async-start(f32[64,8,256]{2,1,0:T(8,128)} %shard_map.156), calls=%async_computation.2 | async-start | bytes 1048576 | tf_op jit(solution)/shard_map/all_to_all | solution.py:362
  80.1 25.2 %copy-start.5 = (bf16[2,128,128]{2,1,0:T(8,128)(2,1)S(1)}, bf16[2,128,128]{2,1,0:T(8,128)(2,1)}, u32[]{:S(2)}) copy-start(bf16[2,128,128]{2,1,0:T(8,128)(2,1)} %constant.38.clone.x_table) | copy-start | bytes 196612
  82.9 22.4 %copy-start = (bf16[2,512,512]{2,1,0:T(8,128)(2,1)S(1)}, bf16[2,512,512]{2,1,0:T(8,128)(2,1)}, u32[]{:S(2)}) copy-start(bf16[2,512,512]{2,1,0:T(8,128)(2,1)} %constant.40.clone.y_table) | copy-start | bytes 3145732
  127.4 4.8 %copy-start.9 = (s32[16,512]{1,0:T(8,128)S(1)}, s32[16,512]{1,0:T(8,128)}, u32[]{:S(2)}) copy-start(s32[16,512]{1,0:T(8,128)} %index.1) | copy-start | bytes 98308
  127.4 4.9 %copy-start.10 = (f32[16,512]{1,0:T(8,128)S(1)}, f32[16,512]{1,0:T(8,128)}, u32[]{:S(2)}) copy-start(f32[16,512]{1,0:T(8,128)} %coef.1) | copy-start | bytes 98308
  127.4 15.7 %all-to-all-start.5 = ((f32[64,1,64]{2,1,0:T(1,128)}), f32[64,1,64]{2,1,0:T(1,128)S(1)}, u32[]{:S(2)}, u32[]{:S(2)}) async-start(f32[64,1,64]{2,1,0:T(1,128)} %shard_map.159), calls=%async_computation.5 | async-start | bytes 65536 | tf_op jit(solution)/shard_map/all_to_all | solution.py:362
  132.3 10.8 %copy-start.8 = (s32[1,512,8]{1,2,0:T(8,128)S(1)}, s32[1,512,8]{1,2,0:T(8,128)}, u32[]{:S(2)}) copy-start(s32[1,512,8]{1,2,0:T(8,128)} %param.18) | copy-start | bytes 49156
  132.3 10.8 %copy-start.14 = (f32[1,512,8]{1,2,0:T(8,128)S(1)}, f32[1,512,8]{1,2,0:T(8,128)}, u32[]{:S(2)}) copy-start(f32[1,512,8]{1,2,0:T(8,128)} %param.20) | copy-start | bytes 49156
  132.3 10.8 %copy-start.17 = (s32[1,512]{1,0:T(1,128)S(1)}, s32[1,512]{1,0:T(1,128)}, u32[]{:S(2)}) copy-start(s32[1,512]{1,0:T(1,128)} %counts.3) | copy-start | bytes 6148

commit v2 on v1

--- a/solution.py
+++ b/solution.py
@@ -22,6 +22,11 @@
     return np.stack([high, low])
 
 
+def wide(table):
+    high, low = halves(table)
+    return np.concatenate([high, high, low], axis=1)
+
+
 def waves(first, second, length):
     turns = np.outer(first, second) % length
     angles = turns * (2.0 * np.pi / length)
@@ -35,7 +40,7 @@
     cosine, sine = waves(np.arange(64), np.arange(64), 64)
     forward = np.block([[cosine, sine], [-sine, cosine]])
     backward = np.block([[cosine, -sine], [sine, cosine]])
-    return halves(forward), halves(backward)
+    return wide(forward), wide(backward)
 
 
 def y_tables():
@@ -57,6 +62,11 @@
     return halves(forward), halves(backward)
 
 
+def quarter_table():
+    cosine, sine = waves(np.arange(128), np.ones(1, np.int64), NX)
+    return np.stack([cosine[:, 0], sine[:, 0]]).astype(np.float32)
+
+
 def split(value):
     high = value.astype(BF16)
     return high, (value - high.astype(F32)).astype(BF16)
@@ -74,6 +84,11 @@
 def table_by_data(table_ref, value):
     high, low = split(value)
     return mul(table_ref[0], high) + mul(table_ref[0], low) + mul(table_ref[1], high)
+
+
+def wide_by_data(table_ref, value):
+    high, low = split(value)
+    return mul(table_ref[...], jnp.concatenate([high, low, high], axis=0))
 
 
 def across(a, b):
@@ -118,7 +133,22 @@
     )
 
 
-def items_kernel(density, counts, panel, weight, row, col, out, cells):
+def items_kernel(*refs):
+    sources, (out, message), held, (told, done, sent) = refs[:6], refs[6:8], refs[8:14], refs[14:]
+    copies = [pltpu.make_async_copy(a, b, done.at[k]) for k, (a, b) in enumerate(zip(sources, held))]
+    for copy in copies:
+        copy.start()
+    density, counts, panel, weight, row, col = held
+    for copy in copies:
+        copy.wait()
+    slab = slab_of()
+    place = (row[...] * NX + col[...]).astype(F32)
+    told[0:32, :] = paired(across(spread(place), slab))
+    told[32:36, :] = density[...]
+    told[36:40, :] = density[...]
+    copies = [pltpu.make_async_copy(told, message.at[p, 32:72], sent.at[p]) for p in range(N_PATCH)]
+    for copy in copies:
+        copy.start()
     used = iota((CAP, DEVICES), 0) < counts[...]
     picked = []
     for j in range(4):
@@ -129,30 +159,36 @@
             value = jnp.where(high == h, lookup(density[h : h + 1, :], low), value)
         picked.append(value)
     items = jnp.where(used, weight[...] * jnp.concatenate(picked, axis=1), 0.0)
-    slab = slab_of()
     out[:, 0, :] = across(slab, spread(items))
-    place = (row[...] * NX + col[...]).astype(F32)
-    cells[...] = paired(across(spread(place), slab))
-
-
-def message_kernel(arrived, cells, density, out):
-    items = paired(arrived[:, 0, :].T)
-    for p in range(N_PATCH):
-        out[p, 0:32, :] = items
-        out[p, 32:64, :] = cells[...]
-        out[p, 64:68, :] = density[...]
-        out[p, 68:72, :] = density[...]
-
-
-def phases(cell, p):
+    for copy in copies:
+        copy.wait()
+
+
+def message_kernel(arrived, message, out, items, sent):
+    del message
+    items[...] = paired(arrived[:, 0, :].T)
+    copies = [pltpu.make_async_copy(items, out.at[p, 0:32], sent.at[p]) for p in range(N_PATCH)]
+    for copy in copies:
+        copy.start()
+    for copy in copies:
+        copy.wait()
+
+
+def phases(cell, p, quarter):
     place = (cell + 0.5).astype(I32)
     col = place & (NX - 1)
-    angle = ((col * p) & (NX - 1)).astype(F32) * (2.0 * math.pi / NX)
-    return (place >> 9).astype(F32), (col & 63).astype(F32), jnp.cos(angle), jnp.sin(angle)
+    turn = (col * p) & (NX - 1)
+    part, within = turn >> 7, turn & 127
+    cosine, sine = lookup(quarter[0:1, :], within), lookup(quarter[1:2, :], within)
+    odd = (part & 1) == 1
+    real, imag = jnp.where(odd, sine, cosine), jnp.where(odd, cosine, sine)
+    real = jnp.where((part == 1) | (part == 2), -real, real)
+    imag = jnp.where(part >= 2, -imag, imag)
+    return (place >> 9).astype(F32), (col & 63).astype(F32), real, imag
 
 
 def lanes(ref, block, p, kind=0):
-    rows = [ref[kind, block, pl.ds(8 * q + p, 1), :] for q in range(4)]
+    rows = [ref[kind, block, 8 * q + p : 8 * q + p + 1, :] for q in range(4)]
     return jnp.concatenate(rows, axis=1)
 
 
@@ -165,19 +201,19 @@
     return thick(row, count) == steps
 
 
-def forward_kernel(meta, data, x_table, y_table, out, slots, lines):
+def forward_kernel(meta, data, quarter, x_table, y_table, out, slots, lines):
     p = meta[0]
     for q in range(4):
         for sender in range(N_PATCH):
             slots[4, :, 8 * q + sender, :] = data[sender, 8 * q : 8 * q + 8, :]
     for block in range(N_PATCH):
-        row, low_col, cosine, sine = phases(data[block, 32:64, :], p)
+        row, low_col, cosine, sine = phases(data[block, 32:64, :], p, quarter)
         slots[0, block] = row
         slots[1, block] = low_col
         slots[2, block] = slots[4, block] * cosine
         slots[3, block] = -slots[4, block] * sine
 
-    def one_block(block, carry):
+    for block in range(N_PATCH):
         total = jnp.zeros((256, 256), F32)
         for sender in range(N_PATCH):
             in_row = one_hot(lanes(slots, block, sender, 0), 16, 256)
@@ -193,26 +229,28 @@
                 (((1,), (1,)), ((), ())),
                 preferred_element_type=F32,
             )
-        lines[block] = table_by_data(x_table, total[:128, :] + total[128:, :])
-        return carry
-
-    lax.fori_loop(0, N_PATCH, one_block, 0)
+        lines[block] = total[:128, :] + total[128:, :]
+    waved = wide_by_data(x_table, jnp.concatenate([lines[b] for b in range(N_PATCH)], axis=1))
     lower = iota((128, 128), 1) < 64
+    rows = []
+    for z in range(4):
+        tiles = []
+        for t in range(4):
+            start = 512 * t + 128 * (z // 2)
+            even, odd = waved[:, start : start + 128], waved[:, start + 256 : start + 384]
+            if z % 2 == 0:
+                tiles.append(jnp.where(lower, even, pltpu.roll(odd, 64, 1)))
+            else:
+                tiles.append(jnp.where(lower, pltpu.roll(even, 64, 1), odd))
+        rows.append(jnp.concatenate(tiles, axis=1))
+    both = data_by_table(jnp.concatenate(rows, axis=0), y_table)
     kx = 8 * iota((64, 256), 0) + p
     first = iota((64, 256), 1) == 0
     alone = (kx == 0) | (kx == NX // 2)
     for z in range(4):
-        at = slice(128 * (z // 2), 128 * (z // 2) + 128)
-        tiles = []
-        for t in range(4):
-            even, odd = lines[2 * t, :, at], lines[2 * t + 1, :, at]
-            if z % 2 == 0:
-                tiles.append(jnp.where(lower, even, pltpu.roll(odd, 64, 1)))
-            else:
-                tiles.append(jnp.where(lower, pltpu.roll(even, 64, 1), odd))
-        both = data_by_table(jnp.concatenate(tiles, axis=1), y_table)
-        re_cos, re_sin = both[:64, :256], both[:64, 256:]
-        im_cos, im_sin = both[64:, :256], both[64:, 256:]
+        real, imag = both[128 * z : 128 * z + 64], both[128 * z + 64 : 128 * z + 128]
+        re_cos, re_sin = real[:, :256], real[:, 256:]
+        im_cos, im_sin = imag[:, :256], imag[:, 256:]
         re_first = jnp.where(kx <= NX // 2, re_cos, re_sin)
         im_first = jnp.where(alone, re_sin, jnp.where(kx < NX // 2, im_cos, im_sin))
         out[:, z, :] = jnp.where(first, re_first, re_cos + im_sin)
@@ -238,10 +276,10 @@
     out[...] = table_by_data(backward, scaled).reshape(N_SLAB, 8, size)
 
 
-def backward_kernel(meta, arrived, data, x_table, y_table, out, slots, planes, blocks):
+def backward_kernel(meta, arrived, data, quarter, x_table, y_table, out, slots, planes, blocks):
     p = meta[0]
     for block in range(N_PATCH):
-        row, low_col, cosine, sine = phases(data[block, 32:64, :], p)
+        row, low_col, cosine, sine = phases(data[block, 32:64, :], p, quarter)
         slots[0, block] = row
         slots[1, block] = low_col
         slots[2, block] = cosine
@@ -259,14 +297,12 @@
     crossed = jnp.where(first, other, jnp.where(real, -after, before))
     planes[...] = data_by_table(jnp.concatenate([straight, crossed], axis=1), y_table).reshape(64, 8, 512)
     lower = iota((128, 128), 1) < 64
+    both = [jnp.concatenate([planes[:, z, :], planes[:, 4 + z, :]], axis=0) for z in range(4)]
+    waved = wide_by_data(x_table, jnp.concatenate(both, axis=1))
     for pair in range(2):
-        plane = []
-        for z in (2 * pair, 2 * pair + 1):
-            both = jnp.concatenate([planes[:, z, :], planes[:, 4 + z, :]], axis=0)
-            plane.append(table_by_data(x_table, both))
         for t in range(4):
-            even = plane[0][:, 128 * t : 128 * (t + 1)]
-            odd = plane[1][:, 128 * t : 128 * (t + 1)]
+            start = 1024 * pair + 128 * t
+            even, odd = waved[:, start : start + 128], waved[:, start + 512 : start + 640]
             for block, tile in (
                 (2 * t, jnp.where(lower, even, pltpu.roll(odd, 64, 1))),
                 (2 * t + 1, jnp.where(lower, pltpu.roll(even, 64, 1), odd)),
@@ -277,7 +313,7 @@
 
     steps = iota((64, 512), 0).astype(F32)
 
-    def one_block(block, carry):
+    for block in range(N_PATCH):
         field = blocks[block]
         for sender in range(N_PATCH):
             in_row = one_hot(lanes(slots, block, sender, 0), 16, 256)
@@ -289,10 +325,7 @@
             in_col = lanes(slots, block, sender, 1) == steps
             found = jnp.sum(jnp.where(in_col, turned, 0.0), axis=0, keepdims=True)
             for q in range(4):
-                out[sender, pl.ds(8 * q + block, 1), :] = found[:, 128 * q : 128 * (q + 1)]
-        return carry
-
-    lax.fori_loop(0, N_PATCH, one_block, 0)
+                out[sender, 8 * q + block : 8 * q + block + 1, :] = found[:, 128 * q : 128 * (q + 1)]
 
 
 def sum_kernel(parts, out):
@@ -341,25 +374,85 @@
 
 VMEM = pl.BlockSpec(memory_space=pltpu.VMEM)
 SMEM = pl.BlockSpec(memory_space=pltpu.SMEM)
-
-
-def call(kernel, shapes, args, scratch=(), scalars=0, vmem=16, flops=0):
+FAR = pl.BlockSpec(memory_space=pltpu.HBM)
+
+
+def call(kernel, shapes, args, scratch=(), scalars=0, vmem=16, sources=None, outs=VMEM, aliases=None):
     many = isinstance(shapes, list)
-    outs = [jax.ShapeDtypeStruct(s, F32) for s in (shapes if many else [shapes])]
-    moved = 4 * sum(math.prod(o.shape) for o in outs) + sum(a.size * a.dtype.itemsize for a in args)
+    shape = [jax.ShapeDtypeStruct(s, F32) for s in (shapes if many else [shapes])]
+    moved = 4 * sum(math.prod(o.shape) for o in shape) + sum(a.size * a.dtype.itemsize for a in args)
     return pl.pallas_call(
         kernel,
-        out_shape=outs if many else outs[0],
-        in_specs=[SMEM] * scalars + [VMEM] * (len(args) - scalars),
-        out_specs=[VMEM] * len(outs) if many else VMEM,
+        out_shape=shape if many else shape[0],
+        in_specs=sources or [SMEM] * scalars + [VMEM] * (len(args) - scalars),
+        out_specs=outs,
         scratch_shapes=list(scratch),
+        input_output_aliases=aliases or {},
         compiler_params=pltpu.CompilerParams(vmem_limit_bytes=vmem * MIB),
-        cost_estimate=pl.CostEstimate(flops=flops, bytes_accessed=moved, transcendentals=0),
+        cost_estimate=pl.CostEstimate(flops=0, bytes_accessed=moved, transcendentals=0),
     )(*args)
+
+
+def run_items(*args):
+    held = [pltpu.VMEM(a.shape, a.dtype) for a in args]
+    return call(
+        items_kernel,
+        [(N_SLAB, 1, 64), (N_PATCH, 72, 128)],
+        args,
+        held + [pltpu.VMEM((40, 128), F32), pltpu.SemaphoreType.DMA((6,)), pltpu.SemaphoreType.DMA((8,))],
+        vmem=60,
+        sources=[FAR] * 6,
+        outs=[VMEM, FAR],
+    )
+
+
+def run_message(arrived, message):
+    return call(
+        message_kernel,
+        (N_PATCH, 72, 128),
+        [arrived, message],
+        [pltpu.VMEM((32, 128), F32), pltpu.SemaphoreType.DMA((8,))],
+        vmem=60,
+        sources=[VMEM, FAR],
+        outs=FAR,
+        aliases={1: 0},
+    )
 
 
 def exchange(value, axis):
     return lax.all_to_all(value, axis, split_axis=0, concat_axis=0, tiled=True)
+
+
+def run_forward(meta, data, quarter, x_table, y_table):
+    return call(
+        forward_kernel,
+        (N_SLAB, 8, 256),
+        [meta, data, quarter, x_table, y_table],
+        [pltpu.VMEM((5, N_PATCH, 32, 128), F32), pltpu.VMEM((N_PATCH, 128, 256), F32)],
+        scalars=1,
+        vmem=32,
+    )
+
+
+def run_spectrum(factor, kernel, lines, forward, backward):
+    return call(
+        spectrum_kernel, (N_SLAB, 8, 256), [factor, kernel, lines, forward, backward], scalars=1, vmem=24
+    )
+
+
+def run_backward(meta, lines, data, quarter, x_table, y_table):
+    return call(
+        backward_kernel,
+        (N_PATCH, 32, 128),
+        [meta, lines, data, quarter, x_table, y_table],
+        [
+            pltpu.VMEM((4, N_PATCH, 32, 128), F32),
+            pltpu.VMEM((N_SLAB, 8, 512), F32),
+            pltpu.VMEM((N_PATCH, 256, 256), BF16),
+        ],
+        scalars=1,
+        vmem=32,
+    )
 
 
 def per_device(
@@ -377,6 +470,7 @@
     p = lax.axis_index("patch").astype(I32)
     own = lax.axis_index("slab").astype(I32) * N_PATCH + p
     meta = jnp.stack([p, own])
+    quarter = jnp.asarray(quarter_table())
     x_forward, x_backward = (jnp.asarray(t) for t in x_tables())
     y_forward, y_backward = (jnp.asarray(t) for t in y_tables())
     z_forward, z_backward = (jnp.asarray(t) for t in z_tables())
@@ -385,22 +479,12 @@
         jnp.transpose(a[0]) for a in (send_panel, send_weight, interp_weight, recv_row, recv_col)
     )
 
-    items, cells = call(
-        items_kernel, [(N_SLAB, 1, 64), (32, 128)], [charge, counts, panel, weight, row, col]
-    )
-    arrived = exchange(items, "slab")
-    message = call(message_kernel, (N_PATCH, 72, 128), [arrived, cells, charge])
+    items, message = run_items(charge, counts, panel, weight, row, col)
+    message = run_message(exchange(items, "slab"), message)
     data = exchange(message, "patch")
     near = call(near_kernel, (4, 128), [data, near_index, near_coef])
 
-    lines = call(
-        forward_kernel,
-        (N_SLAB, 8, 256),
-        [meta, data, x_forward, y_forward],
-        [pltpu.VMEM((5, N_PATCH, 32, 128), F32), pltpu.VMEM((N_PATCH, 128, 256), F32)],
-        scalars=1,
-        vmem=32,
-    )
+    lines = run_forward(meta, data, quarter, x_forward, y_forward)
     lines = exchange(lines, "slab")
 
     unit = 2.0 / (NX * NY * NZ)
@@ -415,26 +499,9 @@
             jnp.full((), unit, F32),
         ]
     ).astype(F32)
-    lines = call(
-        spectrum_kernel,
-        (N_SLAB, 8, 256),
-        [factor, kernel, lines, z_forward, z_backward],
-        scalars=1,
-        vmem=24,
-    )
+    lines = run_spectrum(factor, kernel, lines, z_forward, z_backward)
     lines = exchange(lines, "slab")
-    parts = call(
-        backward_kernel,
-        (N_PATCH, 32, 128),
-        [meta, lines, data, x_backward, y_backward],
-        [
-            pltpu.VMEM((4, N_PATCH, 32, 128), F32),
-            pltpu.VMEM((N_SLAB, 8, 512), F32),
-            pltpu.VMEM((N_PATCH, 256, 256), BF16),
-        ],
-        scalars=1,
-        vmem=32,
-    )
+    parts = run_backward(meta, lines, data, quarter, x_backward, y_backward)
     parts = exchange(parts, "patch")
     sampled = call(sum_kernel, (N_SLAB, 1, 64), [parts])
     sampled = exchange(sampled, "slab")

time: 145 us -> 138 us (0.952)
  local copies, waits for them, and re-layouts: 4.46 us -> 0.15 us
  Pallas kernels: 26.7 us -> 24 us
    unnamed x36 -> x26, local copies, waits for them, and re-layouts: 4.38 us -> 0.07 us
    pallas_call x8, Pallas kernels: 26.7 us -> 24 us  [call(): pl.pallas_call(kernel, out_shape=shape if many else shape[0], in_specs=so...]
where the time goes in v2:
time: 138 us
  blocking collectives  63 us (46%)
  waiting for transfers between devices  34.2 us (25%)
  Pallas kernels  24 us (17%)
  starting transfers between devices  16 us (12%)
    all_to_all x3, blocking collectives, exchange(): return lax.all_to_all(value, axis, split_axis=0, concat_axis=0, tiled=True)  63 us
    all_to_all x3, waiting for transfers between devices, exchange(): return lax.all_to_all(value, axis, split_axis=0, concat_axis=0, tiled=True)  34.2 us
    pallas_call x8, Pallas kernels, call(): pl.pallas_call(kernel, out_shape=shape if many else shape[0], in_specs=so...  24 us
    all_to_all x3, starting transfers between devices, exchange(): return lax.all_to_all(value, axis, split_axis=0, concat_axis=0, tiled=True)  16 us
  transfers between devices with their start and end apart: 3, of which 3 were waited for; matrix products, arithmetic and copies ran while one was open for 0% of the time, Pallas kernels for 0%

profile of v2, /device:TPU:1, one launch (start us, length us, event | category | flops | bytes accessed | tf_op | source)
XLA Modules:
  0.0 137.6 jit_solution(12665444980522733066)
XLA Ops:
  0.0 0.0 copy-start.1
  0.0 2.7 %shard_map.163 = (f32[64,1,64]{2,1,0:T(1,128)}, f32[8,72,128]{2,1,0:T(8,128)}) custom-call(f32[4,128]{1,0:T(4,128)} %bitcast.29, s32[1,512]{1,0:T(1,128)} %counts.1, s32[8,512]{1,0:T(8,128)} %bitcast.23, f32[8,512]{1,0:T(8,128)} %bitcast.26, s32[8,512]{1,0:T(8,128)} %bitcast.27, s32[8,512]{1,0:T(8,128)} %bitcast.28), custom_call_target="tpu_custom_call" | custom-call | bytes 380928 | tf_op jit(solution)/shard_map/pallas_call | solution.py:384
  2.7 28.1 %all_to_all.30.arrived = f32[64,1,64]{2,1,0:T(1,128)} all-to-all(f32[64,1,64]{2,1,0:T(1,128)} %get-tuple-element.7), channel_id=1, replica_groups=mesh['slab'=64,'patch'=8] {'slab'}, dimensions={0} | all-to-all | bytes 32768 | tf_op jit(solution)/shard_map/all_to_all | solution.py:423
  30.9 1.7 %shard_map.164 = f32[8,72,128]{2,1,0:T(8,128)} custom-call(f32[64,1,64]{2,1,0:T(1,128)} %all_to_all.30.arrived, f32[8,72,128]{2,1,0:T(8,128)} %get-tuple-element.8.message), custom_call_target="tpu_custom_call", output_to_operand_aliasing={{}: (1, {})} | custom-call | bytes 606208 | tf_op jit(solution)/shard_map/pallas_call | solution.py:384
  32.5 0.0 copy-start.6
  32.5 6.4 %all-to-all-start.1 = ((f32[8,72,128]{2,1,0:T(8,128)}), f32[8,72,128]{2,1,0:T(8,128)S(1)}, u32[]{:S(2)}, u32[]{:S(2)}) async-start(f32[8,72,128]{2,1,0:T(8,128)} %shard_map.164), calls=%async_computation.1 | async-start | bytes 589824 | tf_op jit(solution)/shard_map/all_to_all | solution.py:423
  39.0 0.0 copy-start.12
  39.0 0.1 pad_add_fusion.meta
  39.0 0.0 copy-start.2
  39.0 0.0 copy-start.3
  39.0 6.7 %all-to-all-done.1.data = f32[8,72,128]{2,1,0:T(8,128)S(1)} async-done(((f32[8,72,128]{2,1,0:T(8,128)}), f32[8,72,128]{2,1,0:T(8,128)S(1)}, u32[]{:S(2)}, u32[]{:S(2)}) %all-to-all-start.1) | async-done | bytes 294944 | tf_op jit(solution)/shard_map/all_to_all | solution.py:423
  45.8 0.0 copy-done.1
  45.8 0.0 copy-done.6
  45.8 0.0 copy-done.12
  45.8 7.2 %shard_map.165 = f32[64,8,256]{2,1,0:T(8,128)} custom-call(s32[2]{0:T(128)S(1)} %pad_add_fusion.meta, f32[8,72,128]{2,1,0:T(8,128)S(1)} %all-to-all-done.1.data, f32[2,128]{1,0:T(2,128)S(1)} %copy-done.12, bf16[128,384]{1,0:T(8,128)(2,1)S(1)} %copy-done.6, bf16[2,512,512]{2,1,0:T(8,128)(2,1)S(1)} %copy-done.1), custom_call_target="tpu_custom_call" | custom-call | bytes 1967112 | tf_op jit(solution)/shard_map/pallas_call | solution.py:384
  53.0 0.0 copy-start.4
  53.0 4.8 %all-to-all-start.2 = ((f32[64,8,256]{2,1,0:T(8,128)}), f32[64,8,256]{2,1,0:T(8,128)S(1)}, u32[]{:S(2)}, u32[]{:S(2)}) async-start(f32[64,8,256]{2,1,0:T(8,128)} %shard_map.165), calls=%async_computation.2 | async-start | bytes 1048576 | tf_op jit(solution)/shard_map/all_to_all | solution.py:423
  57.7 0.1 stack.31.factor
  57.8 17.1 %all-to-all-done.2.lines = f32[64,8,256]{2,1,0:T(8,128)S(1)} async-done(((f32[64,8,256]{2,1,0:T(8,128)}), f32[64,8,256]{2,1,0:T(8,128)S(1)}, u32[]{:S(2)}, u32[]{:S(2)}) %all-to-all-start.2) | async-done | bytes 524320 | tf_op jit(solution)/shard_map/all_to_all | solution.py:423
  74.9 0.0 copy-done.2
  74.9 0.0 copy-done.3
  74.9 0.0 copy-done.4
  74.9 0.0 copy-start.5
  74.9 2.8 %shard_map.166 = f32[64,8,256]{2,1,0:T(8,128)S(1)} custom-call(f32[5]{0:T(128)S(1)} %stack.31.factor, f32[1,512,256]{2,1,0:T(8,128)S(1)} %copy-done.4, f32[64,8,256]{2,1,0:T(8,128)S(1)} %all-to-all-done.2.lines, bf16[2,512,512]{2,1,0:T(8,128)(2,1)S(1)} %copy-done.2, bf16[2,512,512]{2,1,0:T(8,128)(2,1)S(1)} %copy-done.3), custom_call_target="tpu_custom_call" | custom-call | bytes 3670036 | tf_op jit(solution)/shard_map/pallas_call | solution.py:384
  77.7 0.0 copy-start
  77.8 22.4 %all_to_all.31.arrived = f32[64,8,256]{2,1,0:T(8,128)S(1)} all-to-all(f32[64,8,256]{2,1,0:T(8,128)S(1)} %shard_map.166), channel_id=1, replica_groups=mesh['slab'=64,'patch'=8] {'slab'}, dimensions={0} | all-to-all | bytes 1048576 | tf_op jit(solution)/shard_map/all_to_all | solution.py:423
  100.1 0.0 copy-done.5
  100.1 0.0 copy-done
  100.1 7.2 %shard_map.167 = f32[8,32,128]{2,1,0:T(8,128)S(1)} custom-call(s32[2]{0:T(128)S(1)} %pad_add_fusion.meta, f32[64,8,256]{2,1,0:T(8,128)S(1)} %all_to_all.31.arrived, f32[8,72,128]{2,1,0:T(8,128)S(1)} %all-to-all-done.1.data, f32[2,128]{1,0:T(2,128)S(1)} %copy-done.12, bf16[128,384]{1,0:T(8,128)(2,1)S(1)} %copy-done.5, bf16[2,512,512]{2,1,0:T(8,128)(2,1)S(1)} %copy-done), custom_call_target="tpu_custom_call" | custom-call | bytes 2098184 | tf_op jit(solution)/shard_map/pallas_call | solution.py:384
  107.3 12.5 %all_to_all.32.parts = f32[8,32,128]{2,1,0:T(8,128)S(1)} all-to-all(f32[8,32,128]{2,1,0:T(8,128)S(1)} %shard_map.167), channel_id=1, replica_groups=mesh['slab'=64,'patch'=8] {'patch'}, dimensions={0} | all-to-all | bytes 262144 | tf_op jit(solution)/shard_map/all_to_all | solution.py:423
  119.8 0.8 shard_map.168
  120.6 0.0 copy-start.8
  120.6 0.0 copy-start.9
  120.6 4.8 %all-to-all-start.5 = ((f32[64,1,64]{2,1,0:T(1,128)}), f32[64,1,64]{2,1,0:T(1,128)S(1)}, u32[]{:S(2)}, u32[]{:S(2)}) async-start(f32[64,1,64]{2,1,0:T(1,128)} %shard_map.168), calls=%async_computation.5 | async-start | bytes 65536 | tf_op jit(solution)/shard_map/all_to_all | solution.py:423
  125.5 0.0 copy-done.8
  125.5 0.0 copy-done.9
  125.5 0.0 copy-start.7
  125.5 0.0 copy-start.10
  125.5 0.0 copy-start.11
  125.5 0.4 shard_map.169.near
  125.9 10.4 %all-to-all-done.5.arrived = f32[64,1,64]{2,1,0:T(1,128)S(1)} async-done(((f32[64,1,64]{2,1,0:T(1,128)}), f32[64,1,64]{2,1,0:T(1,128)S(1)}, u32[]{:S(2)}, u32[]{:S(2)}) %all-to-all-start.5) | async-done | bytes 16416 | tf_op jit(solution)/shard_map/all_to_all | solution.py:423
  136.3 0.0 copy-done.7
  136.3 0.0 copy-done.10
  136.3 0.0 copy-done.11
  136.3 1.3 shard_map.170
Async XLA Ops:
  0.0 45.8 %copy-start.1 = (bf16[2,512,512]{2,1,0:T(8,128)(2,1)S(1)}, bf16[2,512,512]{2,1,0:T(8,128)(2,1)}, u32[]{:S(2)}) copy-start(bf16[2,512,512]{2,1,0:T(8,128)(2,1)} %constant.42.clone.y_table) | copy-start | bytes 3145732
  32.5 13.3 %copy-start.6 = (bf16[128,384]{1,0:T(8,128)(2,1)S(1)}, bf16[128,384]{1,0:T(8,128)(2,1)}, u32[]{:S(2)}) copy-start(bf16[128,384]{1,0:T(8,128)(2,1)} %constant.40.clone.x_table) | copy-start | bytes 294916
  32.5 13.2 %all-to-all-start.1 = ((f32[8,72,128]{2,1,0:T(8,128)}), f32[8,72,128]{2,1,0:T(8,128)S(1)}, u32[]{:S(2)}, u32[]{:S(2)}) async-start(f32[8,72,128]{2,1,0:T(8,128)} %shard_map.164), calls=%async_computation.1 | async-start | bytes 589824 | tf_op jit(solution)/shard_map/all_to_all | solution.py:423
  39.0 6.8 %copy-start.12 = (f32[2,128]{1,0:T(2,128)S(1)}, f32[2,128]{1,0:T(2,128)}, u32[]{:S(2)}) copy-start(f32[2,128]{1,0:T(2,128)} %constant.39.clone.quarter) | copy-start | bytes 3076
  39.0 35.9 %copy-start.2 = (bf16[2,512,512]{2,1,0:T(8,128)(2,1)S(1)}, bf16[2,512,512]{2,1,0:T(8,128)(2,1)}, u32[]{:S(2)}) copy-start(bf16[2,512,512]{2,1,0:T(8,128)(2,1)} %constant.44.clone.forward) | copy-start | bytes 3145732
  39.0 35.9 %copy-start.3 = (bf16[2,512,512]{2,1,0:T(8,128)(2,1)S(1)}, bf16[2,512,512]{2,1,0:T(8,128)(2,1)}, u32[]{:S(2)}) copy-start(bf16[2,512,512]{2,1,0:T(8,128)(2,1)} %constant.45.clone.backward) | copy-start | bytes 3145732
  53.0 22.0 %copy-start.4 = (f32[1,512,256]{2,1,0:T(8,128)S(1)}, f32[1,512,256]{2,1,0:T(8,128)}, u32[]{:S(2)}) copy-start(f32[1,512,256]{2,1,0:T(8,128)} %kernel.1) | copy-start | bytes 1572868
  53.0 22.0 %all-to-all-start.2 = ((f32[64,8,256]{2,1,0:T(8,128)}), f32[64,8,256]{2,1,0:T(8,128)S(1)}, u32[]{:S(2)}, u32[]{:S(2)}) async-start(f32[64,8,256]{2,1,0:T(8,128)} %shard_map.165), calls=%async_computation.2 | async-start | bytes 1048576 | tf_op jit(solution)/shard_map/all_to_all | solution.py:423
  74.9 25.2 %copy-start.5 = (bf16[128,384]{1,0:T(8,128)(2,1)S(1)}, bf16[128,384]{1,0:T(8,128)(2,1)}, u32[]{:S(2)}) copy-start(bf16[128,384]{1,0:T(8,128)(2,1)} %constant.41.clone.x_table) | copy-start | bytes 294916
  77.7 22.4 %copy-start = (bf16[2,512,512]{2,1,0:T(8,128)(2,1)S(1)}, bf16[2,512,512]{2,1,0:T(8,128)(2,1)}, u32[]{:S(2)}) copy-start(bf16[2,512,512]{2,1,0:T(8,128)(2,1)} %constant.43.clone.y_table) | copy-start | bytes 3145732
  120.6 4.9 %copy-start.8 = (s32[16,512]{1,0:T(8,128)S(1)}, s32[16,512]{1,0:T(8,128)}, u32[]{:S(2)}) copy-start(s32[16,512]{1,0:T(8,128)} %index.1) | copy-start | bytes 98308
  120.6 4.9 %copy-start.9 = (f32[16,512]{1,0:T(8,128)S(1)}, f32[16,512]{1,0:T(8,128)}, u32[]{:S(2)}) copy-start(f32[16,512]{1,0:T(8,128)} %coef.1) | copy-start | bytes 98308
  120.6 15.7 %all-to-all-start.5 = ((f32[64,1,64]{2,1,0:T(1,128)}), f32[64,1,64]{2,1,0:T(1,128)S(1)}, u32[]{:S(2)}, u32[]{:S(2)}) async-start(f32[64,1,64]{2,1,0:T(1,128)} %shard_map.168), calls=%async_computation.5 | async-start | bytes 65536 | tf_op jit(solution)/shard_map/all_to_all | solution.py:423
  125.5 10.8 %copy-start.7 = (s32[1,512,8]{1,2,0:T(8,128)S(1)}, s32[1,512,8]{1,2,0:T(8,128)}, u32[]{:S(2)}) copy-start(s32[1,512,8]{1,2,0:T(8,128)} %param.19) | copy-start | bytes 49156
  125.5 10.8 %copy-start.10 = (f32[1,512,8]{1,2,0:T(8,128)S(1)}, f32[1,512,8]{1,2,0:T(8,128)}, u32[]{:S(2)}) copy-start(f32[1,512,8]{1,2,0:T(8,128)} %param.21) | copy-start | bytes 49156
  125.5 10.8 %copy-start.11 = (s32[1,512]{1,0:T(1,128)S(1)}, s32[1,512]{1,0:T(1,128)}, u32[]{:S(2)}) copy-start(s32[1,512]{1,0:T(1,128)} %counts.1) | copy-start | bytes 6148

commit v3 on v2

--- a/solution.py
+++ b/solution.py
@@ -59,7 +59,7 @@
 
     forward = np.concatenate([rows(cosine, sine), rows(-sine, cosine)], axis=1).T
     backward = np.concatenate([rows(cosine, sine), rows(-sine, cosine)], axis=1)
-    return halves(forward), halves(backward)
+    return wide(forward), wide(backward)
 
 
 def quarter_table():
@@ -79,11 +79,6 @@
 def data_by_table(value, table_ref):
     high, low = split(value)
     return mul(high, table_ref[0]) + mul(low, table_ref[0]) + mul(high, table_ref[1])
-
-
-def table_by_data(table_ref, value):
-    high, low = split(value)
-    return mul(table_ref[0], high) + mul(table_ref[0], low) + mul(table_ref[1], high)
 
 
 def wide_by_data(table_ref, value):
@@ -133,22 +128,18 @@
     )
 
 
-def items_kernel(*refs):
-    sources, (out, message), held, (told, done, sent) = refs[:6], refs[6:8], refs[8:14], refs[14:]
+def fetch(sources, held, done):
     copies = [pltpu.make_async_copy(a, b, done.at[k]) for k, (a, b) in enumerate(zip(sources, held))]
     for copy in copies:
         copy.start()
-    density, counts, panel, weight, row, col = held
     for copy in copies:
         copy.wait()
-    slab = slab_of()
-    place = (row[...] * NX + col[...]).astype(F32)
-    told[0:32, :] = paired(across(spread(place), slab))
-    told[32:36, :] = density[...]
-    told[36:40, :] = density[...]
-    copies = [pltpu.make_async_copy(told, message.at[p, 32:72], sent.at[p]) for p in range(N_PATCH)]
-    for copy in copies:
-        copy.start()
+
+
+def items_kernel(*refs):
+    sources, out, held, done = refs[:4], refs[4], refs[5:9], refs[9]
+    fetch(sources, held, done)
+    density, counts, panel, weight = held
     used = iota((CAP, DEVICES), 0) < counts[...]
     picked = []
     for j in range(4):
@@ -159,19 +150,21 @@
             value = jnp.where(high == h, lookup(density[h : h + 1, :], low), value)
         picked.append(value)
     items = jnp.where(used, weight[...] * jnp.concatenate(picked, axis=1), 0.0)
-    out[:, 0, :] = across(slab, spread(items))
-    for copy in copies:
-        copy.wait()
-
-
-def message_kernel(arrived, message, out, items, sent):
-    del message
-    items[...] = paired(arrived[:, 0, :].T)
-    copies = [pltpu.make_async_copy(items, out.at[p, 0:32], sent.at[p]) for p in range(N_PATCH)]
-    for copy in copies:
-        copy.start()
-    for copy in copies:
-        copy.wait()
+    out[:, 0, :] = across(slab_of(), spread(items))
+
+
+def cells_kernel(density, row, col, out):
+    place = (row[...] * NX + col[...]).astype(F32)
+    out[0:32, :] = paired(across(spread(place), slab_of()))
+    out[32:36, :] = density[...]
+    out[36:40, :] = density[...]
+
+
+def message_kernel(arrived, cells, out):
+    items = paired(arrived[:, 0, :].T)
+    for p in range(N_PATCH):
+        out[p, 0:32, :] = items
+        out[p, 32:72, :] = cells[...]
 
 
 def phases(cell, p, quarter):
@@ -267,13 +260,13 @@
     mirrored = jnp.where(first[:, :128], factor[2] * low + factor[3] * mid, 0.0)
     value = lines[...].reshape(2 * NZ, size)
     sign = jnp.where((iota((2 * NZ, 128), 0) & 4) == 0, 1.0, -1.0)
-    wave = table_by_data(forward, value)
-    turned = table_by_data(forward, value[:, :128] * sign)
+    wave = wide_by_data(forward, value)
+    turned = wide_by_data(forward, value[:, :128] * sign)
     left = jnp.concatenate([own[:, :128]] * 2, axis=0) * wave[:, :128]
     left = left + jnp.concatenate([mirrored] * 2, axis=0) * turned
     right = jnp.concatenate([own[:, 128:]] * 2, axis=0) * wave[:, 128:]
     scaled = jnp.concatenate([left, right], axis=1)
-    out[...] = table_by_data(backward, scaled).reshape(N_SLAB, 8, size)
+    out[...] = wide_by_data(backward, scaled).reshape(N_SLAB, 8, size)
 
 
 def backward_kernel(meta, arrived, data, quarter, x_table, y_table, out, slots, planes, blocks):
@@ -351,10 +344,15 @@
 
 def interp_kernel(arrived, counts, panel, weight, near, out):
     used = iota((CAP, DEVICES), 0) < counts[...]
-    wide = across(arrived[:, 0, :].T, slab_of().T)
+    thin = arrived[:, 0, :].T
+    top = thin.astype(BF16)
+    middle = (thin - top.astype(F32)).astype(BF16)
+    bottom = (thin - top.astype(F32) - middle.astype(F32)).astype(BF16)
+    slab = slab_of().astype(BF16)
+    expanded = mul(jnp.concatenate([top, middle, bottom], axis=1), jnp.concatenate([slab] * 3, axis=0))
     keep = (iota((64, DEVICES), 1) & 7) == (iota((64, DEVICES), 0) & 7)
-    wide = jnp.where(keep, wide, 0.0)
-    rows = [jnp.sum(wide[8 * c : 8 * c + 8, :], axis=0, keepdims=True) for c in range(CAP)]
+    expanded = jnp.where(keep, expanded, 0.0)
+    rows = [jnp.sum(expanded[8 * c : 8 * c + 8, :], axis=0, keepdims=True) for c in range(CAP)]
     terms = jnp.where(used, weight[...] * jnp.concatenate(rows, axis=0), 0.0)
     places = panel[...]
     low, high = places & 127, places >> 7
@@ -377,7 +375,7 @@
 FAR = pl.BlockSpec(memory_space=pltpu.HBM)
 
 
-def call(kernel, shapes, args, scratch=(), scalars=0, vmem=16, sources=None, outs=VMEM, aliases=None):
+def call(kernel, shapes, args, scratch=(), scalars=0, vmem=16, sources=None):
     many = isinstance(shapes, list)
     shape = [jax.ShapeDtypeStruct(s, F32) for s in (shapes if many else [shapes])]
     moved = 4 * sum(math.prod(o.shape) for o in shape) + sum(a.size * a.dtype.itemsize for a in args)
@@ -385,38 +383,41 @@
         kernel,
         out_shape=shape if many else shape[0],
         in_specs=sources or [SMEM] * scalars + [VMEM] * (len(args) - scalars),
-        out_specs=outs,
+        out_specs=[VMEM] * len(shape) if many else VMEM,
         scratch_shapes=list(scratch),
-        input_output_aliases=aliases or {},
         compiler_params=pltpu.CompilerParams(vmem_limit_bytes=vmem * MIB),
         cost_estimate=pl.CostEstimate(flops=0, bytes_accessed=moved, transcendentals=0),
     )(*args)
 
 
-def run_items(*args):
+def call_far(kernel, shape, args):
     held = [pltpu.VMEM(a.shape, a.dtype) for a in args]
-    return call(
-        items_kernel,
-        [(N_SLAB, 1, 64), (N_PATCH, 72, 128)],
-        args,
-        held + [pltpu.VMEM((40, 128), F32), pltpu.SemaphoreType.DMA((6,)), pltpu.SemaphoreType.DMA((8,))],
-        vmem=60,
-        sources=[FAR] * 6,
-        outs=[VMEM, FAR],
-    )
-
-
-def run_message(arrived, message):
-    return call(
-        message_kernel,
-        (N_PATCH, 72, 128),
-        [arrived, message],
-        [pltpu.VMEM((32, 128), F32), pltpu.SemaphoreType.DMA((8,))],
-        vmem=60,
-        sources=[VMEM, FAR],
-        outs=FAR,
-        aliases={1: 0},
-    )
+    done = [pltpu.SemaphoreType.DMA((len(args),))]
+    return call(kernel, shape, args, held + done, vmem=60, sources=[FAR] * len(args))
+
+
+def run_items(density, counts, panel, weight):
+    return call_far(items_kernel, (N_SLAB, 1, 64), [density, counts, panel, weight])
+
+
+def run_cells(density, row, col):
+    return call(cells_kernel, (40, 128), [density, row, col])
+
+
+def run_message(arrived, cells):
+    return call(message_kernel, (N_PATCH, 72, 128), [arrived, cells])
+
+
+def run_sum(parts):
+    return call(sum_kernel, (N_SLAB, 1, 64), [parts])
+
+
+def run_near(data, index, coef):
+    return call(near_kernel, (4, 128), [data, index, coef])
+
+
+def run_interp(*args):
+    return call(interp_kernel, (4, 128), list(args))
 
 
 def exchange(value, axis):
@@ -479,14 +480,6 @@
         jnp.transpose(a[0]) for a in (send_panel, send_weight, interp_weight, recv_row, recv_col)
     )
 
-    items, message = run_items(charge, counts, panel, weight, row, col)
-    message = run_message(exchange(items, "slab"), message)
-    data = exchange(message, "patch")
-    near = call(near_kernel, (4, 128), [data, near_index, near_coef])
-
-    lines = run_forward(meta, data, quarter, x_forward, y_forward)
-    lines = exchange(lines, "slab")
-
     unit = 2.0 / (NX * NY * NZ)
     alone = (own == 0) | (own == NX // 2)
     below = own < NX // 2
@@ -499,13 +492,22 @@
             jnp.full((), unit, F32),
         ]
     ).astype(F32)
+
+    items = exchange(run_items(charge, counts, panel, weight), "slab")
+    message = run_message(items, run_cells(charge, row, col))
+    data = exchange(message, "patch")
+    near = run_near(data, near_index, near_coef)
+
+    lines = run_forward(meta, data, quarter, x_forward, y_forward)
+    lines = exchange(lines, "slab")
+
     lines = run_spectrum(factor, kernel, lines, z_forward, z_backward)
     lines = exchange(lines, "slab")
     parts = run_backward(meta, lines, data, quarter, x_backward, y_backward)
     parts = exchange(parts, "patch")
-    sampled = call(sum_kernel, (N_SLAB, 1, 64), [parts])
+    sampled = run_sum(parts)
     sampled = exchange(sampled, "slab")
-    result = call(interp_kernel, (4, 128), [sampled, counts, panel, back_weight, near])
+    result = run_interp(sampled, counts, panel, back_weight, near)
     return result.reshape(-1)
 
 

time: 138 us -> 140 us (1.014)
  blocking collectives: 63 us -> 34.9 us
  starting transfers between devices: 16 us -> 32.9 us
  waiting for transfers between devices: 34.2 us -> 42.7 us
  local copies, waits for them, and re-layouts: 0.15 us -> 6.27 us
    all_to_all x3 -> x2, blocking collectives: 63 us -> 34.9 us  [exchange(): return lax.all_to_all(value, axis, split_axis=0, concat_axis=0, tiled=True)]
    all_to_all x3 -> x4, starting transfers between devices: 16 us -> 32.9 us  [exchange(): return lax.all_to_all(value, axis, split_axis=0, concat_axis=0, tiled=True)]
    all_to_all x3 -> x4, waiting for transfers between devices: 34.2 us -> 42.7 us  [exchange(): return lax.all_to_all(value, axis, split_axis=0, concat_axis=0, tiled=True)]
    unnamed x26 -> x34, local copies, waits for them, and re-layouts: 0.07 us -> 6.18 us
    pallas_call x8 -> x9, Pallas kernels: 24 us -> 22.7 us  [call(): pl.pallas_call(kernel, out_shape=shape if many else shape[0], in_specs=so...]
  transfers between devices with their start and end apart: 3 -> 4, of which waited for: 3 -> 4; matrix products, arithmetic and copies ran while one was open for 0% -> 0% of each run, Pallas kernels for 0% -> 1%
where the time goes in v3:
time: 140 us
  waiting for transfers between devices  42.7 us (30%)
  blocking collectives  34.9 us (25%)
  starting transfers between devices  32.9 us (24%)
  Pallas kernels  22.7 us (16%)
  local copies, waits for them, and re-layouts  6.27 us (4%)
    all_to_all x4, waiting for transfers between devices, exchange(): return lax.all_to_all(value, axis, split_axis=0, concat_axis=0, tiled=True)  42.7 us
    all_to_all x2, blocking collectives, exchange(): return lax.all_to_all(value, axis, split_axis=0, concat_axis=0, tiled=True)  34.9 us
    all_to_all x4, starting transfers between devices, exchange(): return lax.all_to_all(value, axis, split_axis=0, concat_axis=0, tiled=True)  32.9 us
    pallas_call x9, Pallas kernels, call(): pl.pallas_call(kernel, out_shape=shape if many else shape[0], in_specs=so...  22.7 us
    unnamed x34, local copies, waits for them, and re-layouts  6.18 us
  transfers between devices with their start and end apart: 4, of which 4 were waited for; matrix products, arithmetic and copies ran while one was open for 0% of the time, Pallas kernels for 1%

profile of v3, /device:TPU:1, one launch (start us, length us, event | category | flops | bytes accessed | tf_op | source)
XLA Modules:
  0.0 139.6 jit_solution(4473480683441893506)
XLA Ops:
  0.0 0.0 copy-start.3
  0.0 1.9 %shard_map.163 = f32[64,1,64]{2,1,0:T(1,128)} custom-call(f32[4,128]{1,0:T(4,128)} %bitcast.28, s32[1,512]{1,0:T(1,128)} %counts.1, s32[8,512]{1,0:T(8,128)} %bitcast.23, f32[8,512]{1,0:T(8,128)} %bitcast.30), custom_call_target="tpu_custom_call" | custom-call | bytes 53248 | tf_op jit(solution)/shard_map/pallas_call | solution.py:382
  1.9 17.1 %all-to-all-start = ((f32[64,1,64]{2,1,0:T(1,128)}), f32[64,1,64]{2,1,0:T(1,128)S(1)}, u32[]{:S(2)}, u32[]{:S(2)}) async-start(f32[64,1,64]{2,1,0:T(1,128)} %shard_map.163), calls=%async_computation | async-start | bytes 65536 | tf_op jit(solution)/shard_map/all_to_all | solution.py:424
  19.0 0.0 copy-start.10
  19.1 0.7 copy-done.10
  19.8 0.0 copy-start.11
  19.8 0.7 copy-done.11
  20.5 0.0 copy-start.13
  20.5 0.7 copy-done.13
  21.2 0.3 shard_map.164.cells
  21.5 8.4 %all-to-all-done.arrived = f32[64,1,64]{2,1,0:T(1,128)S(1)} async-done(((f32[64,1,64]{2,1,0:T(1,128)}), f32[64,1,64]{2,1,0:T(1,128)S(1)}, u32[]{:S(2)}, u32[]{:S(2)}) %all-to-all-start) | async-done | bytes 16416 | tf_op jit(solution)/shard_map/all_to_all | solution.py:424
  29.9 0.9 shard_map.165
  30.8 6.4 %all-to-all-start.1 = ((f32[8,72,128]{2,1,0:T(8,128)}), f32[8,72,128]{2,1,0:T(8,128)S(1)}, u32[]{:S(2)}, u32[]{:S(2)}) async-start(f32[8,72,128]{2,1,0:T(8,128)} %shard_map.165), calls=%async_computation.1 | async-start | bytes 589824 | tf_op jit(solution)/shard_map/all_to_all | solution.py:424
  37.1 0.0 copy-start
  37.1 0.1 pad_add_fusion.meta
  37.2 6.7 %all-to-all-done.1.data = f32[8,72,128]{2,1,0:T(8,128)S(1)} async-done(((f32[8,72,128]{2,1,0:T(8,128)}), f32[8,72,128]{2,1,0:T(8,128)S(1)}, u32[]{:S(2)}, u32[]{:S(2)}) %all-to-all-start.1) | async-done | bytes 294944 | tf_op jit(solution)/shard_map/all_to_all | solution.py:424
  43.9 0.0 copy-done.3
  44.0 0.0 copy-start.6
  44.0 0.9 copy-done.6
  44.8 0.0 copy-start.15
  44.8 0.7 copy-done.15
  45.5 7.2 %shard_map.166 = f32[64,8,256]{2,1,0:T(8,128)} custom-call(s32[2]{0:T(128)S(1)} %pad_add_fusion.meta, f32[8,72,128]{2,1,0:T(8,128)S(1)} %all-to-all-done.1.data, f32[2,128]{1,0:T(2,128)S(1)} %copy-done.15, bf16[128,384]{1,0:T(8,128)(2,1)S(1)} %copy-done.6, bf16[2,512,512]{2,1,0:T(8,128)(2,1)S(1)} %copy-done.3), custom_call_target="tpu_custom_call" | custom-call | bytes 1967112 | tf_op jit(solution)/shard_map/pallas_call | solution.py:382
  52.7 4.6 %all-to-all-start.2 = ((f32[64,8,256]{2,1,0:T(8,128)}), f32[64,8,256]{2,1,0:T(8,128)S(1)}, u32[]{:S(2)}, u32[]{:S(2)}) async-start(f32[64,8,256]{2,1,0:T(8,128)} %shard_map.166), calls=%async_computation.2 | async-start | bytes 1048576 | tf_op jit(solution)/shard_map/all_to_all | solution.py:424
  57.4 0.1 stack.31.factor
  57.5 17.1 %all-to-all-done.2.lines = f32[64,8,256]{2,1,0:T(8,128)S(1)} async-done(((f32[64,8,256]{2,1,0:T(8,128)}), f32[64,8,256]{2,1,0:T(8,128)S(1)}, u32[]{:S(2)}, u32[]{:S(2)}) %all-to-all-start.2) | async-done | bytes 524320 | tf_op jit(solution)/shard_map/all_to_all | solution.py:424
  74.5 0.0 copy-done
  74.5 0.0 copy-start.1
  74.5 1.4 %copy-done.1 = bf16[512,1536]{1,0:T(8,128)(2,1)S(1)} copy-done((bf16[512,1536]{1,0:T(8,128)(2,1)S(1)}, bf16[512,1536]{1,0:T(8,128)(2,1)}, u32[]{:S(2)}) %copy-start.1) | copy-done | bytes 1572888
  75.9 0.0 copy-start.4
  75.9 1.0 copy-done.4
  77.0 0.0 copy-start.5
  77.0 0.0 copy-start.16
  77.0 2.8 %shard_map.167 = f32[64,8,256]{2,1,0:T(8,128)S(1)} custom-call(f32[5]{0:T(128)S(1)} %stack.31.factor, f32[1,512,256]{2,1,0:T(8,128)S(1)} %copy-done.4, f32[64,8,256]{2,1,0:T(8,128)S(1)} %all-to-all-done.2.lines, bf16[512,1536]{1,0:T(8,128)(2,1)S(1)} %copy-done, bf16[512,1536]{1,0:T(8,128)(2,1)S(1)} %copy-done.1), custom_call_target="tpu_custom_call" | custom-call | bytes 4718612 | tf_op jit(solution)/shard_map/pallas_call | solution.py:382
  79.8 0.0 copy-start.2
  79.8 0.0 copy-start.8
  79.8 0.0 copy-start.9
  79.8 22.4 %all_to_all.30.arrived = f32[64,8,256]{2,1,0:T(8,128)S(1)} all-to-all(f32[64,8,256]{2,1,0:T(8,128)S(1)} %shard_map.167), channel_id=1, replica_groups=mesh['slab'=64,'patch'=8] {'slab'}, dimensions={0} | all-to-all | bytes 1048576 | tf_op jit(solution)/shard_map/all_to_all | solution.py:424
  102.2 0.0 copy-done.5
  102.2 0.0 copy-done.16
  102.2 0.0 copy-done.2
  102.2 0.0 copy-start.7
  102.2 0.0 copy-start.12
  102.2 0.0 copy-start.14
  102.2 7.2 %shard_map.168 = f32[8,32,128]{2,1,0:T(8,128)S(1)} custom-call(s32[2]{0:T(128)S(1)} %pad_add_fusion.meta, f32[64,8,256]{2,1,0:T(8,128)S(1)} %all_to_all.30.arrived, f32[8,72,128]{2,1,0:T(8,128)S(1)} %all-to-all-done.1.data, f32[2,128]{1,0:T(2,128)S(1)} %copy-done.16, bf16[128,384]{1,0:T(8,128)(2,1)S(1)} %copy-done.5, bf16[2,512,512]{2,1,0:T(8,128)(2,1)S(1)} %copy-done.2), custom_call_target="tpu_custom_call" | custom-call | bytes 2098184 | tf_op jit(solution)/shard_map/pallas_call | solution.py:382
  109.4 12.5 %all_to_all.31.parts = f32[8,32,128]{2,1,0:T(8,128)S(1)} all-to-all(f32[8,32,128]{2,1,0:T(8,128)S(1)} %shard_map.168), channel_id=1, replica_groups=mesh['slab'=64,'patch'=8] {'patch'}, dimensions={0} | all-to-all | bytes 262144 | tf_op jit(solution)/shard_map/all_to_all | solution.py:424
  121.9 0.8 shard_map.169
  122.7 4.7 %all-to-all-start.5 = ((f32[64,1,64]{2,1,0:T(1,128)}), f32[64,1,64]{2,1,0:T(1,128)S(1)}, u32[]{:S(2)}, u32[]{:S(2)}) async-start(f32[64,1,64]{2,1,0:T(1,128)} %shard_map.169), calls=%async_computation.5 | async-start | bytes 65536 | tf_op jit(solution)/shard_map/all_to_all | solution.py:424
  127.4 0.0 copy-done.8
  127.5 0.0 copy-done.9
  127.5 0.4 shard_map.170.near
  127.8 10.5 %all-to-all-done.5.arrived = f32[64,1,64]{2,1,0:T(1,128)S(1)} async-done(((f32[64,1,64]{2,1,0:T(1,128)}), f32[64,1,64]{2,1,0:T(1,128)S(1)}, u32[]{:S(2)}, u32[]{:S(2)}) %all-to-all-start.5) | async-done | bytes 16416 | tf_op jit(solution)/shard_map/all_to_all | solution.py:424
  138.3 0.0 copy-done.7
  138.3 0.0 copy-done.12
  138.3 0.0 copy-done.14
  138.3 1.3 shard_map.171
Async XLA Ops:
  0.0 44.0 %copy-start.3 = (bf16[2,512,512]{2,1,0:T(8,128)(2,1)S(1)}, bf16[2,512,512]{2,1,0:T(8,128)(2,1)}, u32[]{:S(2)}) copy-start(bf16[2,512,512]{2,1,0:T(8,128)(2,1)} %constant.42.clone.y_table) | copy-start | bytes 3145732
  1.9 28.0 %all-to-all-start = ((f32[64,1,64]{2,1,0:T(1,128)}), f32[64,1,64]{2,1,0:T(1,128)S(1)}, u32[]{:S(2)}, u32[]{:S(2)}) async-start(f32[64,1,64]{2,1,0:T(1,128)} %shard_map.163), calls=%async_computation | async-start | bytes 65536 | tf_op jit(solution)/shard_map/all_to_all | solution.py:424
  19.0 0.7 copy-start.10
  19.8 0.7 copy-start.11
  20.5 0.7 copy-start.13
  30.8 13.2 %all-to-all-start.1 = ((f32[8,72,128]{2,1,0:T(8,128)}), f32[8,72,128]{2,1,0:T(8,128)S(1)}, u32[]{:S(2)}, u32[]{:S(2)}) async-start(f32[8,72,128]{2,1,0:T(8,128)} %shard_map.165), calls=%async_computation.1 | async-start | bytes 589824 | tf_op jit(solution)/shard_map/all_to_all | solution.py:424
  37.1 37.4 %copy-start = (bf16[512,1536]{1,0:T(8,128)(2,1)S(1)}, bf16[512,1536]{1,0:T(8,128)(2,1)}, u32[]{:S(2)}) copy-start(bf16[512,1536]{1,0:T(8,128)(2,1)} %constant.44.clone.forward) | copy-start | bytes 4718596
  44.0 0.9 copy-start.6
  44.8 0.7 copy-start.15
  52.7 21.8 %all-to-all-start.2 = ((f32[64,8,256]{2,1,0:T(8,128)}), f32[64,8,256]{2,1,0:T(8,128)S(1)}, u32[]{:S(2)}, u32[]{:S(2)}) async-start(f32[64,8,256]{2,1,0:T(8,128)} %shard_map.166), calls=%async_computation.2 | async-start | bytes 1048576 | tf_op jit(solution)/shard_map/all_to_all | solution.py:424
  74.5 1.4 %copy-start.1 = (bf16[512,1536]{1,0:T(8,128)(2,1)S(1)}, bf16[512,1536]{1,0:T(8,128)(2,1)}, u32[]{:S(2)}) copy-start(bf16[512,1536]{1,0:T(8,128)(2,1)} %constant.45.clone.backward) | copy-start | bytes 4718596
  75.9 1.0 copy-start.4
  77.0 25.2 %copy-start.5 = (bf16[128,384]{1,0:T(8,128)(2,1)S(1)}, bf16[128,384]{1,0:T(8,128)(2,1)}, u32[]{:S(2)}) copy-start(bf16[128,384]{1,0:T(8,128)(2,1)} %constant.41.clone.x_table) | copy-start | bytes 294916
  77.0 25.2 %copy-start.16 = (f32[2,128]{1,0:T(2,128)S(1)}, f32[2,128]{1,0:T(2,128)}, u32[]{:S(2)}) copy-start(f32[2,128]{1,0:T(2,128)} %constant.39.clone.quarter) | copy-start | bytes 3076
  79.8 22.4 %copy-start.2 = (bf16[2,512,512]{2,1,0:T(8,128)(2,1)S(1)}, bf16[2,512,512]{2,1,0:T(8,128)(2,1)}, u32[]{:S(2)}) copy-start(bf16[2,512,512]{2,1,0:T(8,128)(2,1)} %constant.43.clone.y_table) | copy-start | bytes 3145732
  79.8 47.7 %copy-start.8 = (s32[16,512]{1,0:T(8,128)S(1)}, s32[16,512]{1,0:T(8,128)}, u32[]{:S(2)}) copy-start(s32[16,512]{1,0:T(8,128)} %index.1) | copy-start | bytes 98308
  79.8 47.7 %copy-start.9 = (f32[16,512]{1,0:T(8,128)S(1)}, f32[16,512]{1,0:T(8,128)}, u32[]{:S(2)}) copy-start(f32[16,512]{1,0:T(8,128)} %coef.1) | copy-start | bytes 98308
  102.2 36.1 %copy-start.7 = (s32[1,512,8]{1,2,0:T(8,128)S(1)}, s32[1,512,8]{1,2,0:T(8,128)}, u32[]{:S(2)}) copy-start(s32[1,512,8]{1,2,0:T(8,128)} %param.19) | copy-start | bytes 49156
  102.2 36.1 %copy-start.12 = (f32[1,512,8]{1,2,0:T(8,128)S(1)}, f32[1,512,8]{1,2,0:T(8,128)}, u32[]{:S(2)}) copy-start(f32[1,512,8]{1,2,0:T(8,128)} %param.21) | copy-start | bytes 49156
  102.2 36.1 %copy-start.14 = (s32[1,512]{1,0:T(1,128)S(1)}, s32[1,512]{1,0:T(1,128)}, u32[]{:S(2)}) copy-start(s32[1,512]{1,0:T(1,128)} %counts.1) | copy-start | bytes 6148
  122.7 15.6 %all-to-all-start.5 = ((f32[64,1,64]{2,1,0:T(1,128)}), f32[64,1,64]{2,1,0:T(1,128)S(1)}, u32[]{:S(2)}, u32[]{:S(2)}) async-start(f32[64,1,64]{2,1,0:T(1,128)} %shard_map.169), calls=%async_computation.5 | async-start | bytes 65536 | tf_op jit(solution)/shard_map/all_to_all | solution.py:424

commit v4 on v3

--- a/solution.py
+++ b/solution.py
@@ -59,7 +59,7 @@
 
     forward = np.concatenate([rows(cosine, sine), rows(-sine, cosine)], axis=1).T
     backward = np.concatenate([rows(cosine, sine), rows(-sine, cosine)], axis=1)
-    return wide(forward), wide(backward)
+    return halves(forward), halves(backward)
 
 
 def quarter_table():
@@ -79,6 +79,11 @@
 def data_by_table(value, table_ref):
     high, low = split(value)
     return mul(high, table_ref[0]) + mul(low, table_ref[0]) + mul(high, table_ref[1])
+
+
+def table_by_data(table_ref, value):
+    high, low = split(value)
+    return mul(table_ref[0], high) + mul(table_ref[0], low) + mul(table_ref[1], high)
 
 
 def wide_by_data(table_ref, value):
@@ -260,13 +265,13 @@
     mirrored = jnp.where(first[:, :128], factor[2] * low + factor[3] * mid, 0.0)
     value = lines[...].reshape(2 * NZ, size)
     sign = jnp.where((iota((2 * NZ, 128), 0) & 4) == 0, 1.0, -1.0)
-    wave = wide_by_data(forward, value)
-    turned = wide_by_data(forward, value[:, :128] * sign)
+    wave = table_by_data(forward, value)
+    turned = table_by_data(forward, value[:, :128] * sign)
     left = jnp.concatenate([own[:, :128]] * 2, axis=0) * wave[:, :128]
     left = left + jnp.concatenate([mirrored] * 2, axis=0) * turned
     right = jnp.concatenate([own[:, 128:]] * 2, axis=0) * wave[:, 128:]
     scaled = jnp.concatenate([left, right], axis=1)
-    out[...] = wide_by_data(backward, scaled).reshape(N_SLAB, 8, size)
+    out[...] = table_by_data(backward, scaled).reshape(N_SLAB, 8, size)
 
 
 def backward_kernel(meta, arrived, data, quarter, x_table, y_table, out, slots, planes, blocks):
@@ -375,7 +380,7 @@
 FAR = pl.BlockSpec(memory_space=pltpu.HBM)
 
 
-def call(kernel, shapes, args, scratch=(), scalars=0, vmem=16, sources=None):
+def call(kernel, shapes, args, scratch=(), scalars=0, vmem=16, sources=None, flops=10**7):
     many = isinstance(shapes, list)
     shape = [jax.ShapeDtypeStruct(s, F32) for s in (shapes if many else [shapes])]
     moved = 4 * sum(math.prod(o.shape) for o in shape) + sum(a.size * a.dtype.itemsize for a in args)
@@ -386,7 +391,7 @@
         out_specs=[VMEM] * len(shape) if many else VMEM,
         scratch_shapes=list(scratch),
         compiler_params=pltpu.CompilerParams(vmem_limit_bytes=vmem * MIB),
-        cost_estimate=pl.CostEstimate(flops=0, bytes_accessed=moved, transcendentals=0),
+        cost_estimate=pl.CostEstimate(flops=flops, bytes_accessed=moved, transcendentals=0),
     )(*args)
 
 
@@ -401,11 +406,11 @@
 
 
 def run_cells(density, row, col):
-    return call(cells_kernel, (40, 128), [density, row, col])
+    return call(cells_kernel, (40, 128), [density, row, col], flops=10**9)
 
 
 def run_message(arrived, cells):
-    return call(message_kernel, (N_PATCH, 72, 128), [arrived, cells])
+    return call(message_kernel, (N_PATCH, 72, 128), [arrived, cells], flops=10**9)
 
 
 def run_sum(parts):
@@ -432,12 +437,13 @@
         [pltpu.VMEM((5, N_PATCH, 32, 128), F32), pltpu.VMEM((N_PATCH, 128, 256), F32)],
         scalars=1,
         vmem=32,
+        flops=6 * 10**9,
     )
 
 
 def run_spectrum(factor, kernel, lines, forward, backward):
     return call(
-        spectrum_kernel, (N_SLAB, 8, 256), [factor, kernel, lines, forward, backward], scalars=1, vmem=24
+        spectrum_kernel, (N_SLAB, 8, 256), [factor, kernel, lines, forward, backward], scalars=1, vmem=24, flops=10**9
     )
 
 
@@ -453,6 +459,7 @@
         ],
         scalars=1,
         vmem=32,
+        flops=6 * 10**9,
     )
 
 

time: 140 us -> 137 us (0.979)
  local copies, waits for them, and re-layouts: 6.27 us -> 0.82 us
    unnamed x34 -> x32, local copies, waits for them, and re-layouts: 6.18 us -> 0.74 us
where the time goes in v4:
time: 137 us; the launch traced here: 136 us
  waiting for transfers between devices  44 us (32%)
  blocking collectives  34.9 us (25%)
  starting transfers between devices  33.3 us (24%)
  Pallas kernels  22.6 us (16%)
    all_to_all x4, waiting for transfers between devices, exchange(): return lax.all_to_all(value, axis, split_axis=0, concat_axis=0, tiled=True)  44 us
    all_to_all x2, blocking collectives, exchange(): return lax.all_to_all(value, axis, split_axis=0, concat_axis=0, tiled=True)  34.9 us
    all_to_all x4, starting transfers between devices, exchange(): return lax.all_to_all(value, axis, split_axis=0, concat_axis=0, tiled=True)  33.3 us
    pallas_call x9, Pallas kernels, call(): pl.pallas_call(kernel, out_shape=shape if many else shape[0], in_specs=so...  22.6 us
  transfers between devices with their start and end apart: 4, of which 4 were waited for; matrix products, arithmetic and copies ran while one was open for 0% of the time, Pallas kernels for 1%

profile of v4, /device:TPU:1, one launch (start us, length us, event | category | flops | bytes accessed | tf_op | source)
XLA Modules:
  0.0 135.9 jit_solution(16949440929358138638)
XLA Ops:
  0.0 1.8 %shard_map.163 = f32[64,1,64]{2,1,0:T(1,128)} custom-call(f32[4,128]{1,0:T(4,128)} %bitcast.26, s32[1,512]{1,0:T(1,128)} %counts.1, s32[8,512]{1,0:T(8,128)} %bitcast.23, f32[8,512]{1,0:T(8,128)} %bitcast.30), custom_call_target="tpu_custom_call" | custom-call | flops 10000000 | bytes 53248 | tf_op jit(solution)/shard_map/pallas_call | solution.py:387
  1.8 0.0 copy-start.7
  1.8 0.0 copy-start.8
  1.8 17.1 %all-to-all-start = ((f32[64,1,64]{2,1,0:T(1,128)}), f32[64,1,64]{2,1,0:T(1,128)S(1)}, u32[]{:S(2)}, u32[]{:S(2)}) async-start(f32[64,1,64]{2,1,0:T(1,128)} %shard_map.163), calls=%async_computation | async-start | bytes 65536 | tf_op jit(solution)/shard_map/all_to_all | solution.py:429
  19.0 0.0 copy-start.5
  19.0 0.0 copy-done.7
  19.0 0.0 copy-done.8
  19.0 0.7 copy-done.5
  19.6 0.3 shard_map.164.cells
  20.0 0.0 copy-start.12
  20.0 9.8 %all-to-all-done.arrived = f32[64,1,64]{2,1,0:T(1,128)S(1)} async-done(((f32[64,1,64]{2,1,0:T(1,128)}), f32[64,1,64]{2,1,0:T(1,128)S(1)}, u32[]{:S(2)}, u32[]{:S(2)}) %all-to-all-start) | async-done | bytes 16416 | tf_op jit(solution)/shard_map/all_to_all | solution.py:429
  29.8 0.9 shard_map.165
  30.7 0.0 copy-start.14
  30.7 6.6 %all-to-all-start.1 = ((f32[8,72,128]{2,1,0:T(8,128)}), f32[8,72,128]{2,1,0:T(8,128)S(1)}, u32[]{:S(2)}, u32[]{:S(2)}) async-start(f32[8,72,128]{2,1,0:T(8,128)} %shard_map.165), calls=%async_computation.1 | async-start | bytes 589824 | tf_op jit(solution)/shard_map/all_to_all | solution.py:429
  37.2 0.0 copy-start.15
  37.2 0.1 pad_add_fusion.meta
  37.3 6.7 %all-to-all-done.1.data = f32[8,72,128]{2,1,0:T(8,128)S(1)} async-done(((f32[8,72,128]{2,1,0:T(8,128)}), f32[8,72,128]{2,1,0:T(8,128)S(1)}, u32[]{:S(2)}, u32[]{:S(2)}) %all-to-all-start.1) | async-done | bytes 294944 | tf_op jit(solution)/shard_map/all_to_all | solution.py:429
  44.0 0.0 copy-done.12
  44.0 0.0 copy-done.14
  44.0 0.0 copy-done.15
  44.0 0.0 copy-start.10
  44.1 0.0 copy-start.11
  44.1 7.2 %shard_map.166 = f32[64,8,256]{2,1,0:T(8,128)} custom-call(s32[2]{0:T(128)S(1)} %pad_add_fusion.meta, f32[8,72,128]{2,1,0:T(8,128)S(1)} %all-to-all-done.1.data, f32[2,128]{1,0:T(2,128)S(1)} %copy-done.15, bf16[128,384]{1,0:T(8,128)(2,1)S(1)} %copy-done.14, bf16[2,512,512]{2,1,0:T(8,128)(2,1)S(1)} %copy-done.12), custom_call_target="tpu_custom_call" | custom-call | flops 6000000000 | bytes 1967112 | tf_op jit(solution)/shard_map/pallas_call | solution.py:387
  51.3 0.0 copy-start.6
  51.3 4.8 %all-to-all-start.2 = ((f32[64,8,256]{2,1,0:T(8,128)}), f32[64,8,256]{2,1,0:T(8,128)S(1)}, u32[]{:S(2)}, u32[]{:S(2)}) async-start(f32[64,8,256]{2,1,0:T(8,128)} %shard_map.166), calls=%async_computation.2 | async-start | bytes 1048576 | tf_op jit(solution)/shard_map/all_to_all | solution.py:429
  56.0 0.1 stack.31.factor
  56.1 17.1 %all-to-all-done.2.lines = f32[64,8,256]{2,1,0:T(8,128)S(1)} async-done(((f32[64,8,256]{2,1,0:T(8,128)}), f32[64,8,256]{2,1,0:T(8,128)S(1)}, u32[]{:S(2)}, u32[]{:S(2)}) %all-to-all-start.2) | async-done | bytes 524320 | tf_op jit(solution)/shard_map/all_to_all | solution.py:429
  73.2 0.0 copy-done.10
  73.2 0.0 copy-done.11
  73.2 0.0 copy-done.6
  73.2 0.0 copy-start.13
  73.2 2.8 %shard_map.167 = f32[64,8,256]{2,1,0:T(8,128)S(1)} custom-call(f32[5]{0:T(128)S(1)} %stack.31.factor, f32[1,512,256]{2,1,0:T(8,128)S(1)} %copy-done.6, f32[64,8,256]{2,1,0:T(8,128)S(1)} %all-to-all-done.2.lines, bf16[2,512,512]{2,1,0:T(8,128)(2,1)S(1)} %copy-done.10, bf16[2,512,512]{2,1,0:T(8,128)(2,1)S(1)} %copy-done.11), custom_call_target="tpu_custom_call" | custom-call | flops 1000000000 | bytes 3670036 | tf_op jit(solution)/shard_map/pallas_call | solution.py:387
  76.0 0.0 copy-start.9
  76.1 22.4 %all_to_all.30.arrived = f32[64,8,256]{2,1,0:T(8,128)S(1)} all-to-all(f32[64,8,256]{2,1,0:T(8,128)S(1)} %shard_map.167), channel_id=1, replica_groups=mesh['slab'=64,'patch'=8] {'slab'}, dimensions={0} | all-to-all | bytes 1048576 | tf_op jit(solution)/shard_map/all_to_all | solution.py:429
  98.4 0.0 copy-done.13
  98.5 0.0 copy-done.9
  98.5 7.2 %shard_map.168 = f32[8,32,128]{2,1,0:T(8,128)S(1)} custom-call(s32[2]{0:T(128)S(1)} %pad_add_fusion.meta, f32[64,8,256]{2,1,0:T(8,128)S(1)} %all_to_all.30.arrived, f32[8,72,128]{2,1,0:T(8,128)S(1)} %all-to-all-done.1.data, f32[2,128]{1,0:T(2,128)S(1)} %copy-done.15, bf16[128,384]{1,0:T(8,128)(2,1)S(1)} %copy-done.13, bf16[2,512,512]{2,1,0:T(8,128)(2,1)S(1)} %copy-done.9), custom_call_target="tpu_custom_call" | custom-call | flops 6000000000 | bytes 2098184 | tf_op jit(solution)/shard_map/pallas_call | solution.py:387
  105.6 12.5 %all_to_all.31.parts = f32[8,32,128]{2,1,0:T(8,128)S(1)} all-to-all(f32[8,32,128]{2,1,0:T(8,128)S(1)} %shard_map.168), channel_id=1, replica_groups=mesh['slab'=64,'patch'=8] {'patch'}, dimensions={0} | all-to-all | bytes 262144 | tf_op jit(solution)/shard_map/all_to_all | solution.py:429
  118.1 0.8 shard_map.169
  118.9 0.0 copy-start.1
  118.9 0.0 copy-start.2
  118.9 4.9 %all-to-all-start.5 = ((f32[64,1,64]{2,1,0:T(1,128)}), f32[64,1,64]{2,1,0:T(1,128)S(1)}, u32[]{:S(2)}, u32[]{:S(2)}) async-start(f32[64,1,64]{2,1,0:T(1,128)} %shard_map.169), calls=%async_computation.5 | async-start | bytes 65536 | tf_op jit(solution)/shard_map/all_to_all | solution.py:429
  123.8 0.0 copy-done.1
  123.8 0.0 copy-done.2
  123.8 0.0 copy-start
  123.8 0.0 copy-start.3
  123.8 0.0 copy-start.4
  123.8 0.4 shard_map.170.near
  124.2 10.4 %all-to-all-done.5.arrived = f32[64,1,64]{2,1,0:T(1,128)S(1)} async-done(((f32[64,1,64]{2,1,0:T(1,128)}), f32[64,1,64]{2,1,0:T(1,128)S(1)}, u32[]{:S(2)}, u32[]{:S(2)}) %all-to-all-start.5) | async-done | bytes 16416 | tf_op jit(solution)/shard_map/all_to_all | solution.py:429
  134.6 0.0 copy-done
  134.6 0.0 copy-done.3
  134.6 0.0 copy-done.4
  134.6 1.3 shard_map.171
Async XLA Ops:
  1.8 17.2 %copy-start.7 = (s32[1,512,8]{1,2,0:T(8,128)S(1)}, s32[1,512,8]{1,2,0:T(8,128)}, u32[]{:S(2)}) copy-start(s32[1,512,8]{1,2,0:T(8,128)} %param.22) | copy-start | bytes 49156
  1.8 17.2 %copy-start.8 = (s32[1,512,8]{1,2,0:T(8,128)S(1)}, s32[1,512,8]{1,2,0:T(8,128)}, u32[]{:S(2)}) copy-start(s32[1,512,8]{1,2,0:T(8,128)} %param.23) | copy-start | bytes 49156
  1.8 28.0 %all-to-all-start = ((f32[64,1,64]{2,1,0:T(1,128)}), f32[64,1,64]{2,1,0:T(1,128)S(1)}, u32[]{:S(2)}, u32[]{:S(2)}) async-start(f32[64,1,64]{2,1,0:T(1,128)} %shard_map.163), calls=%async_computation | async-start | bytes 65536 | tf_op jit(solution)/shard_map/all_to_all | solution.py:429
  19.0 0.7 copy-start.5
  20.0 24.1 %copy-start.12 = (bf16[2,512,512]{2,1,0:T(8,128)(2,1)S(1)}, bf16[2,512,512]{2,1,0:T(8,128)(2,1)}, u32[]{:S(2)}) copy-start(bf16[2,512,512]{2,1,0:T(8,128)(2,1)} %constant.42.clone.y_table) | copy-start | bytes 3145732
  30.7 13.4 %copy-start.14 = (bf16[128,384]{1,0:T(8,128)(2,1)S(1)}, bf16[128,384]{1,0:T(8,128)(2,1)}, u32[]{:S(2)}) copy-start(bf16[128,384]{1,0:T(8,128)(2,1)} %constant.40.clone.x_table) | copy-start | bytes 294916
  30.7 13.4 %all-to-all-start.1 = ((f32[8,72,128]{2,1,0:T(8,128)}), f32[8,72,128]{2,1,0:T(8,128)S(1)}, u32[]{:S(2)}, u32[]{:S(2)}) async-start(f32[8,72,128]{2,1,0:T(8,128)} %shard_map.165), calls=%async_computation.1 | async-start | bytes 589824 | tf_op jit(solution)/shard_map/all_to_all | solution.py:429
  37.2 6.8 %copy-start.15 = (f32[2,128]{1,0:T(2,128)S(1)}, f32[2,128]{1,0:T(2,128)}, u32[]{:S(2)}) copy-start(f32[2,128]{1,0:T(2,128)} %constant.39.clone.quarter) | copy-start | bytes 3076
  44.0 29.2 %copy-start.10 = (bf16[2,512,512]{2,1,0:T(8,128)(2,1)S(1)}, bf16[2,512,512]{2,1,0:T(8,128)(2,1)}, u32[]{:S(2)}) copy-start(bf16[2,512,512]{2,1,0:T(8,128)(2,1)} %constant.44.clone.forward) | copy-start | bytes 3145732
  44.1 29.1 %copy-start.11 = (bf16[2,512,512]{2,1,0:T(8,128)(2,1)S(1)}, bf16[2,512,512]{2,1,0:T(8,128)(2,1)}, u32[]{:S(2)}) copy-start(bf16[2,512,512]{2,1,0:T(8,128)(2,1)} %constant.45.clone.backward) | copy-start | bytes 3145732
  51.3 22.0 %copy-start.6 = (f32[1,512,256]{2,1,0:T(8,128)S(1)}, f32[1,512,256]{2,1,0:T(8,128)}, u32[]{:S(2)}) copy-start(f32[1,512,256]{2,1,0:T(8,128)} %kernel.1) | copy-start | bytes 1572868
  51.3 21.9 %all-to-all-start.2 = ((f32[64,8,256]{2,1,0:T(8,128)}), f32[64,8,256]{2,1,0:T(8,128)S(1)}, u32[]{:S(2)}, u32[]{:S(2)}) async-start(f32[64,8,256]{2,1,0:T(8,128)} %shard_map.166), calls=%async_computation.2 | async-start | bytes 1048576 | tf_op jit(solution)/shard_map/all_to_all | solution.py:429
  73.2 25.2 %copy-start.13 = (bf16[128,384]{1,0:T(8,128)(2,1)S(1)}, bf16[128,384]{1,0:T(8,128)(2,1)}, u32[]{:S(2)}) copy-start(bf16[128,384]{1,0:T(8,128)(2,1)} %constant.41.clone.x_table) | copy-start | bytes 294916
  76.0 22.4 %copy-start.9 = (bf16[2,512,512]{2,1,0:T(8,128)(2,1)S(1)}, bf16[2,512,512]{2,1,0:T(8,128)(2,1)}, u32[]{:S(2)}) copy-start(bf16[2,512,512]{2,1,0:T(8,128)(2,1)} %constant.43.clone.y_table) | copy-start | bytes 3145732
  118.9 4.9 %copy-start.1 = (s32[16,512]{1,0:T(8,128)S(1)}, s32[16,512]{1,0:T(8,128)}, u32[]{:S(2)}) copy-start(s32[16,512]{1,0:T(8,128)} %index.1) | copy-start | bytes 98308
  118.9 4.9 %copy-start.2 = (f32[16,512]{1,0:T(8,128)S(1)}, f32[16,512]{1,0:T(8,128)}, u32[]{:S(2)}) copy-start(f32[16,512]{1,0:T(8,128)} %coef.1) | copy-start | bytes 98308
  118.9 15.7 %all-to-all-start.5 = ((f32[64,1,64]{2,1,0:T(1,128)}), f32[64,1,64]{2,1,0:T(1,128)S(1)}, u32[]{:S(2)}, u32[]{:S(2)}) async-start(f32[64,1,64]{2,1,0:T(1,128)} %shard_map.169), calls=%async_computation.5 | async-start | bytes 65536 | tf_op jit(solution)/shard_map/all_to_all | solution.py:429
  123.8 10.8 %copy-start = (s32[1,512,8]{1,2,0:T(8,128)S(1)}, s32[1,512,8]{1,2,0:T(8,128)}, u32[]{:S(2)}) copy-start(s32[1,512,8]{1,2,0:T(8,128)} %param.19) | copy-start | bytes 49156
  123.8 10.8 %copy-start.3 = (f32[1,512,8]{1,2,0:T(8,128)S(1)}, f32[1,512,8]{1,2,0:T(8,128)}, u32[]{:S(2)}) copy-start(f32[1,512,8]{1,2,0:T(8,128)} %param.21) | copy-start | bytes 49156
  123.8 10.8 %copy-start.4 = (s32[1,512]{1,0:T(1,128)S(1)}, s32[1,512]{1,0:T(1,128)}, u32[]{:S(2)}) copy-start(s32[1,512]{1,0:T(1,128)} %counts.1) | copy-start | bytes 6148

commit v5 on v4

--- a/solution.py
+++ b/solution.py
@@ -14,6 +14,7 @@
 DEVICES = N_SLAB * N_PATCH
 F32, BF16, I32 = jnp.float32, jnp.bfloat16, jnp.int32
 MIB = 1024 * 1024
+GATHERED = (0, 4)
 
 
 def halves(table):
@@ -24,7 +25,7 @@
 
 def wide(table):
     high, low = halves(table)
-    return np.concatenate([high, high, low], axis=1)
+    return np.block([[high, high], [low, np.zeros_like(low)]])
 
 
 def waves(first, second, length):
@@ -87,14 +88,19 @@
 
 
 def wide_by_data(table_ref, value):
-    high, low = split(value)
-    return mul(table_ref[...], jnp.concatenate([high, low, high], axis=0))
+    both = mul(table_ref[...], jnp.concatenate(split(value), axis=0))
+    return both[:128] + both[128:]
+
+
+def thirds(value):
+    top = value.astype(BF16)
+    rest = value - top.astype(F32)
+    middle = rest.astype(BF16)
+    return [top, middle, (rest - middle.astype(F32)).astype(BF16)]
 
 
 def across(a, b):
-    return lax.dot_general(
-        a, b, (((1,), (1,)), ((), ())), precision=lax.Precision.HIGHEST, preferred_element_type=F32
-    )
+    return lax.dot_general(a, b, (((1,), (1,)), ((), ())), preferred_element_type=F32)
 
 
 def iota(shape, dim):
@@ -108,7 +114,7 @@
 
 
 def slab_of():
-    return ((iota((N_SLAB, DEVICES), 1) >> 3) == iota((N_SLAB, DEVICES), 0)).astype(F32)
+    return ((iota((N_SLAB, DEVICES), 1) >> 3) == iota((N_SLAB, DEVICES), 0)).astype(F32).astype(BF16)
 
 
 def paired(values):
@@ -143,6 +149,7 @@
 
 def items_kernel(*refs):
     sources, out, held, done = refs[:4], refs[4], refs[5:9], refs[9]
+    slab = slab_of()
     fetch(sources, held, done)
     density, counts, panel, weight = held
     used = iota((CAP, DEVICES), 0) < counts[...]
@@ -155,12 +162,14 @@
             value = jnp.where(high == h, lookup(density[h : h + 1, :], low), value)
         picked.append(value)
     items = jnp.where(used, weight[...] * jnp.concatenate(picked, axis=1), 0.0)
-    out[:, 0, :] = across(slab_of(), spread(items))
+    parts = across(slab, jnp.concatenate(thirds(spread(items)), axis=0))
+    out[:, 0, :] = parts[:, :64] + parts[:, 64:128] + parts[:, 128:]
 
 
 def cells_kernel(density, row, col, out):
     place = (row[...] * NX + col[...]).astype(F32)
-    out[0:32, :] = paired(across(spread(place), slab_of()))
+    parts = across(jnp.concatenate(thirds(spread(place)), axis=0), slab_of())
+    out[0:32, :] = paired(parts[:64] + parts[64:128] + parts[128:])
     out[32:36, :] = density[...]
     out[36:40, :] = density[...]
 
@@ -274,7 +283,25 @@
     out[...] = table_by_data(backward, scaled).reshape(N_SLAB, 8, size)
 
 
-def backward_kernel(meta, arrived, data, quarter, x_table, y_table, out, slots, planes, blocks):
+def gathered(whole, block, slot):
+    row, low_col, cosine, sine = (jnp.broadcast_to(v, (8, 128)) for v in slot)
+    row = row.astype(I32)
+    low, upper = row & 127, row >= 128
+    step = iota((8, 128), 0).astype(F32)
+    total = jnp.zeros((8, 128), F32)
+    for group in range(8):
+        part = []
+        for kind in range(2):
+            at = slice(64 * kind + 8 * group, 64 * kind + 8 * group + 8)
+            near = jnp.take_along_axis(whole[block, at, :128], low, axis=1, mode="promise_in_bounds")
+            far = jnp.take_along_axis(whole[block, at, 128:], low, axis=1, mode="promise_in_bounds")
+            part.append(jnp.where(upper, far, near))
+        turned = part[0] * cosine - part[1] * sine
+        total = total + jnp.where(low_col == step + 8.0 * group, turned, 0.0)
+    return jnp.sum(total, axis=0, keepdims=True)
+
+
+def backward_kernel(meta, arrived, data, quarter, x_table, y_table, out, slots, planes, blocks, whole):
     p = meta[0]
     for block in range(N_PATCH):
         row, low_col, cosine, sine = phases(data[block, 32:64, :], p, quarter)
@@ -305,6 +332,7 @@
                 (2 * t, jnp.where(lower, even, pltpu.roll(odd, 64, 1))),
                 (2 * t + 1, jnp.where(lower, pltpu.roll(even, 64, 1), odd)),
             ):
+                whole[block, :, 128 * pair : 128 * (pair + 1)] = tile
                 high, low = split(tile)
                 blocks[block, :128, 128 * pair : 128 * (pair + 1)] = high
                 blocks[block, 128:, 128 * pair : 128 * (pair + 1)] = low
@@ -314,6 +342,13 @@
     for block in range(N_PATCH):
         field = blocks[block]
         for sender in range(N_PATCH):
+            if sender in GATHERED:
+                for q in range(4):
+                    at = slice(8 * q + sender, 8 * q + sender + 1)
+                    out[sender, 8 * q + block : 8 * q + block + 1, :] = gathered(
+                        whole, block, [slots[k, block, at, :] for k in range(4)]
+                    )
+                continue
             in_row = one_hot(lanes(slots, block, sender, 0), 16, 256)
             ones = jnp.where(in_row, jnp.ones((256, 512), BF16), jnp.zeros((256, 512), BF16))
             near = mul(field, ones)
@@ -349,12 +384,8 @@
 
 def interp_kernel(arrived, counts, panel, weight, near, out):
     used = iota((CAP, DEVICES), 0) < counts[...]
-    thin = arrived[:, 0, :].T
-    top = thin.astype(BF16)
-    middle = (thin - top.astype(F32)).astype(BF16)
-    bottom = (thin - top.astype(F32) - middle.astype(F32)).astype(BF16)
-    slab = slab_of().astype(BF16)
-    expanded = mul(jnp.concatenate([top, middle, bottom], axis=1), jnp.concatenate([slab] * 3, axis=0))
+    thin = jnp.concatenate(thirds(arrived[:, 0, :].T), axis=1)
+    expanded = mul(thin, jnp.concatenate([slab_of()] * 3, axis=0))
     keep = (iota((64, DEVICES), 1) & 7) == (iota((64, DEVICES), 0) & 7)
     expanded = jnp.where(keep, expanded, 0.0)
     rows = [jnp.sum(expanded[8 * c : 8 * c + 8, :], axis=0, keepdims=True) for c in range(CAP)]
@@ -456,6 +487,7 @@
             pltpu.VMEM((4, N_PATCH, 32, 128), F32),
             pltpu.VMEM((N_SLAB, 8, 512), F32),
             pltpu.VMEM((N_PATCH, 256, 256), BF16),
+            pltpu.VMEM((N_PATCH, 128, 256), F32),
         ],
         scalars=1,
         vmem=32,

time: 137 us -> 136 us (level)
  transfers between devices with their start and end apart: 4 -> 4, of which waited for: 4 -> 4; matrix products, arithmetic and copies ran while one was open for 0% -> 0% of each run, Pallas kernels for 1% -> 0%
where the time goes in v5:
time: 136 us
  waiting for transfers between devices  44 us (32%)
  blocking collectives  35 us (26%)
  starting transfers between devices  33.2 us (24%)
  Pallas kernels  21.7 us (16%)
  local copies, waits for them, and re-layouts  1.72 us (1%)
    all_to_all x4, waiting for transfers between devices, exchange(): return lax.all_to_all(value, axis, split_axis=0, concat_axis=0, tiled=True)  44 us
    all_to_all x2, blocking collectives, exchange(): return lax.all_to_all(value, axis, split_axis=0, concat_axis=0, tiled=True)  35 us
    all_to_all x4, starting transfers between devices, exchange(): return lax.all_to_all(value, axis, split_axis=0, concat_axis=0, tiled=True)  33.2 us
    pallas_call x9, Pallas kernels, call(): pl.pallas_call(kernel, out_shape=shape if many else shape[0], in_specs=so...  21.7 us
  transfers between devices with their start and end apart: 4, of which 4 were waited for; matrix products, arithmetic and copies ran while one was open for 0% of the time, Pallas kernels for 0%

profile of v5, /device:TPU:1, one launch (start us, length us, event | category | flops | bytes accessed | tf_op | source)
XLA Modules:
  0.0 135.8 jit_solution(13891319780289202225)
XLA Ops:
  0.0 1.8 %shard_map.163 = f32[64,1,64]{2,1,0:T(1,128)} custom-call(f32[4,128]{1,0:T(4,128)} %bitcast.26, s32[1,512]{1,0:T(1,128)} %counts.1, s32[8,512]{1,0:T(8,128)} %bitcast.23, f32[8,512]{1,0:T(8,128)} %bitcast.30), custom_call_target="tpu_custom_call" | custom-call | flops 10000000 | bytes 53248 | tf_op jit(solution)/shard_map/pallas_call | solution.py:418
  1.8 0.0 copy-start.7
  1.8 0.0 copy-start.8
  1.8 17.1 %all-to-all-start = ((f32[64,1,64]{2,1,0:T(1,128)}), f32[64,1,64]{2,1,0:T(1,128)S(1)}, u32[]{:S(2)}, u32[]{:S(2)}) async-start(f32[64,1,64]{2,1,0:T(1,128)} %shard_map.163), calls=%async_computation | async-start | bytes 65536 | tf_op jit(solution)/shard_map/all_to_all | solution.py:460
  19.0 0.0 copy-start.5
  19.0 0.0 copy-done.7
  19.0 0.0 copy-done.8
  19.0 0.7 copy-done.5
  19.6 0.3 shard_map.164.cells
  19.9 0.0 copy-start.12
  19.9 9.9 %all-to-all-done.arrived = f32[64,1,64]{2,1,0:T(1,128)S(1)} async-done(((f32[64,1,64]{2,1,0:T(1,128)}), f32[64,1,64]{2,1,0:T(1,128)S(1)}, u32[]{:S(2)}, u32[]{:S(2)}) %all-to-all-start) | async-done | bytes 16416 | tf_op jit(solution)/shard_map/all_to_all | solution.py:460
  29.8 0.9 shard_map.165
  30.7 6.4 %all-to-all-start.1 = ((f32[8,72,128]{2,1,0:T(8,128)}), f32[8,72,128]{2,1,0:T(8,128)S(1)}, u32[]{:S(2)}, u32[]{:S(2)}) async-start(f32[8,72,128]{2,1,0:T(8,128)} %shard_map.165), calls=%async_computation.1 | async-start | bytes 589824 | tf_op jit(solution)/shard_map/all_to_all | solution.py:460
  37.1 0.0 copy-start.15
  37.1 0.1 pad_add_fusion.meta
  37.2 6.7 %all-to-all-done.1.data = f32[8,72,128]{2,1,0:T(8,128)S(1)} async-done(((f32[8,72,128]{2,1,0:T(8,128)}), f32[8,72,128]{2,1,0:T(8,128)S(1)}, u32[]{:S(2)}, u32[]{:S(2)}) %all-to-all-start.1) | async-done | bytes 294944 | tf_op jit(solution)/shard_map/all_to_all | solution.py:460
  43.9 0.0 copy-done.12
  43.9 0.0 copy-done.15
  43.9 0.0 copy-start.14
  43.9 0.9 copy-done.14
  44.8 0.0 copy-start.10
  44.8 0.0 copy-start.11
  44.8 7.2 %shard_map.166 = f32[64,8,256]{2,1,0:T(8,128)} custom-call(s32[2]{0:T(128)S(1)} %pad_add_fusion.meta, f32[8,72,128]{2,1,0:T(8,128)S(1)} %all-to-all-done.1.data, f32[2,128]{1,0:T(2,128)S(1)} %copy-done.15, bf16[256,256]{1,0:T(8,128)(2,1)S(1)} %copy-done.14, bf16[2,512,512]{2,1,0:T(8,128)(2,1)S(1)} %copy-done.12), custom_call_target="tpu_custom_call" | custom-call | flops 6000000000 | bytes 1999880 | tf_op jit(solution)/shard_map/pallas_call | solution.py:418
  52.0 0.0 copy-start.6
  52.0 4.8 %all-to-all-start.2 = ((f32[64,8,256]{2,1,0:T(8,128)}), f32[64,8,256]{2,1,0:T(8,128)S(1)}, u32[]{:S(2)}, u32[]{:S(2)}) async-start(f32[64,8,256]{2,1,0:T(8,128)} %shard_map.166), calls=%async_computation.2 | async-start | bytes 1048576 | tf_op jit(solution)/shard_map/all_to_all | solution.py:460
  56.8 0.1 stack.31.factor
  56.9 17.0 %all-to-all-done.2.lines = f32[64,8,256]{2,1,0:T(8,128)S(1)} async-done(((f32[64,8,256]{2,1,0:T(8,128)}), f32[64,8,256]{2,1,0:T(8,128)S(1)}, u32[]{:S(2)}, u32[]{:S(2)}) %all-to-all-start.2) | async-done | bytes 524320 | tf_op jit(solution)/shard_map/all_to_all | solution.py:460
  73.9 0.0 copy-done.10
  73.9 0.0 copy-done.11
  73.9 0.0 copy-done.6
  73.9 0.0 copy-start.13
  73.9 2.8 %shard_map.167 = f32[64,8,256]{2,1,0:T(8,128)S(1)} custom-call(f32[5]{0:T(128)S(1)} %stack.31.factor, f32[1,512,256]{2,1,0:T(8,128)S(1)} %copy-done.6, f32[64,8,256]{2,1,0:T(8,128)S(1)} %all-to-all-done.2.lines, bf16[2,512,512]{2,1,0:T(8,128)(2,1)S(1)} %copy-done.10, bf16[2,512,512]{2,1,0:T(8,128)(2,1)S(1)} %copy-done.11), custom_call_target="tpu_custom_call" | custom-call | flops 1000000000 | bytes 3670036 | tf_op jit(solution)/shard_map/pallas_call | solution.py:418
  76.7 0.0 copy-start.9
  76.7 22.4 %all_to_all.30.arrived = f32[64,8,256]{2,1,0:T(8,128)S(1)} all-to-all(f32[64,8,256]{2,1,0:T(8,128)S(1)} %shard_map.167), channel_id=1, replica_groups=mesh['slab'=64,'patch'=8] {'slab'}, dimensions={0} | all-to-all | bytes 1048576 | tf_op jit(solution)/shard_map/all_to_all | solution.py:460
  99.2 0.0 copy-done.13
  99.2 0.0 copy-done.9
  99.2 6.4 %shard_map.168 = f32[8,32,128]{2,1,0:T(8,128)S(1)} custom-call(s32[2]{0:T(128)S(1)} %pad_add_fusion.meta, f32[64,8,256]{2,1,0:T(8,128)S(1)} %all_to_all.30.arrived, f32[8,72,128]{2,1,0:T(8,128)S(1)} %all-to-all-done.1.data, f32[2,128]{1,0:T(2,128)S(1)} %copy-done.15, bf16[256,256]{1,0:T(8,128)(2,1)S(1)} %copy-done.13, bf16[2,512,512]{2,1,0:T(8,128)(2,1)S(1)} %copy-done.9), custom_call_target="tpu_custom_call" | custom-call | flops 6000000000 | bytes 2130952 | tf_op jit(solution)/shard_map/pallas_call | solution.py:418
  105.5 12.5 %all_to_all.31.parts = f32[8,32,128]{2,1,0:T(8,128)S(1)} all-to-all(f32[8,32,128]{2,1,0:T(8,128)S(1)} %shard_map.168), channel_id=1, replica_groups=mesh['slab'=64,'patch'=8] {'patch'}, dimensions={0} | all-to-all | bytes 262144 | tf_op jit(solution)/shard_map/all_to_all | solution.py:460
  118.1 0.8 shard_map.169
  118.8 0.0 copy-start.1
  118.8 0.0 copy-start.2
  118.8 4.8 %all-to-all-start.5 = ((f32[64,1,64]{2,1,0:T(1,128)}), f32[64,1,64]{2,1,0:T(1,128)S(1)}, u32[]{:S(2)}, u32[]{:S(2)}) async-start(f32[64,1,64]{2,1,0:T(1,128)} %shard_map.169), calls=%async_computation.5 | async-start | bytes 65536 | tf_op jit(solution)/shard_map/all_to_all | solution.py:460
  123.7 0.0 copy-done.1
  123.7 0.0 copy-done.2
  123.7 0.0 copy-start
  123.7 0.0 copy-start.3
  123.7 0.0 copy-start.4
  123.7 0.4 shard_map.170.near
  124.1 10.4 %all-to-all-done.5.arrived = f32[64,1,64]{2,1,0:T(1,128)S(1)} async-done(((f32[64,1,64]{2,1,0:T(1,128)}), f32[64,1,64]{2,1,0:T(1,128)S(1)}, u32[]{:S(2)}, u32[]{:S(2)}) %all-to-all-start.5) | async-done | bytes 16416 | tf_op jit(solution)/shard_map/all_to_all | solution.py:460
  134.5 0.0 copy-done
  134.5 0.0 copy-done.3
  134.5 0.0 copy-done.4
  134.5 1.3 shard_map.171
Async XLA Ops:
  1.8 17.2 %copy-start.7 = (s32[1,512,8]{1,2,0:T(8,128)S(1)}, s32[1,512,8]{1,2,0:T(8,128)}, u32[]{:S(2)}) copy-start(s32[1,512,8]{1,2,0:T(8,128)} %param.22) | copy-start | bytes 49156
  1.8 17.2 %copy-start.8 = (s32[1,512,8]{1,2,0:T(8,128)S(1)}, s32[1,512,8]{1,2,0:T(8,128)}, u32[]{:S(2)}) copy-start(s32[1,512,8]{1,2,0:T(8,128)} %param.23) | copy-start | bytes 49156
  1.8 28.0 %all-to-all-start = ((f32[64,1,64]{2,1,0:T(1,128)}), f32[64,1,64]{2,1,0:T(1,128)S(1)}, u32[]{:S(2)}, u32[]{:S(2)}) async-start(f32[64,1,64]{2,1,0:T(1,128)} %shard_map.163), calls=%async_computation | async-start | bytes 65536 | tf_op jit(solution)/shard_map/all_to_all | solution.py:460
  19.0 0.7 copy-start.5
  19.9 24.0 %copy-start.12 = (bf16[2,512,512]{2,1,0:T(8,128)(2,1)S(1)}, bf16[2,512,512]{2,1,0:T(8,128)(2,1)}, u32[]{:S(2)}) copy-start(bf16[2,512,512]{2,1,0:T(8,128)(2,1)} %constant.42.clone.y_table) | copy-start | bytes 3145732
  30.7 13.2 %all-to-all-start.1 = ((f32[8,72,128]{2,1,0:T(8,128)}), f32[8,72,128]{2,1,0:T(8,128)S(1)}, u32[]{:S(2)}, u32[]{:S(2)}) async-start(f32[8,72,128]{2,1,0:T(8,128)} %shard_map.165), calls=%async_computation.1 | async-start | bytes 589824 | tf_op jit(solution)/shard_map/all_to_all | solution.py:460
  37.1 6.8 %copy-start.15 = (f32[2,128]{1,0:T(2,128)S(1)}, f32[2,128]{1,0:T(2,128)}, u32[]{:S(2)}) copy-start(f32[2,128]{1,0:T(2,128)} %constant.39.clone.quarter) | copy-start | bytes 3076
  43.9 0.9 copy-start.14
  44.8 29.0 %copy-start.10 = (bf16[2,512,512]{2,1,0:T(8,128)(2,1)S(1)}, bf16[2,512,512]{2,1,0:T(8,128)(2,1)}, u32[]{:S(2)}) copy-start(bf16[2,512,512]{2,1,0:T(8,128)(2,1)} %constant.44.clone.forward) | copy-start | bytes 3145732
  44.8 29.0 %copy-start.11 = (bf16[2,512,512]{2,1,0:T(8,128)(2,1)S(1)}, bf16[2,512,512]{2,1,0:T(8,128)(2,1)}, u32[]{:S(2)}) copy-start(bf16[2,512,512]{2,1,0:T(8,128)(2,1)} %constant.45.clone.backward) | copy-start | bytes 3145732
  52.0 21.9 %copy-start.6 = (f32[1,512,256]{2,1,0:T(8,128)S(1)}, f32[1,512,256]{2,1,0:T(8,128)}, u32[]{:S(2)}) copy-start(f32[1,512,256]{2,1,0:T(8,128)} %kernel.1) | copy-start | bytes 1572868
  52.0 21.9 %all-to-all-start.2 = ((f32[64,8,256]{2,1,0:T(8,128)}), f32[64,8,256]{2,1,0:T(8,128)S(1)}, u32[]{:S(2)}, u32[]{:S(2)}) async-start(f32[64,8,256]{2,1,0:T(8,128)} %shard_map.166), calls=%async_computation.2 | async-start | bytes 1048576 | tf_op jit(solution)/shard_map/all_to_all | solution.py:460
  73.9 25.3 %copy-start.13 = (bf16[256,256]{1,0:T(8,128)(2,1)S(1)}, bf16[256,256]{1,0:T(8,128)(2,1)}, u32[]{:S(2)}) copy-start(bf16[256,256]{1,0:T(8,128)(2,1)} %constant.41.clone.x_table) | copy-start | bytes 393220
  76.7 22.5 %copy-start.9 = (bf16[2,512,512]{2,1,0:T(8,128)(2,1)S(1)}, bf16[2,512,512]{2,1,0:T(8,128)(2,1)}, u32[]{:S(2)}) copy-start(bf16[2,512,512]{2,1,0:T(8,128)(2,1)} %constant.43.clone.y_table) | copy-start | bytes 3145732
  118.8 4.8 %copy-start.1 = (s32[16,512]{1,0:T(8,128)S(1)}, s32[16,512]{1,0:T(8,128)}, u32[]{:S(2)}) copy-start(s32[16,512]{1,0:T(8,128)} %index.1) | copy-start | bytes 98308
  118.8 4.9 %copy-start.2 = (f32[16,512]{1,0:T(8,128)S(1)}, f32[16,512]{1,0:T(8,128)}, u32[]{:S(2)}) copy-start(f32[16,512]{1,0:T(8,128)} %coef.1) | copy-start | bytes 98308
  118.8 15.7 %all-to-all-start.5 = ((f32[64,1,64]{2,1,0:T(1,128)}), f32[64,1,64]{2,1,0:T(1,128)S(1)}, u32[]{:S(2)}, u32[]{:S(2)}) async-start(f32[64,1,64]{2,1,0:T(1,128)} %shard_map.169), calls=%async_computation.5 | async-start | bytes 65536 | tf_op jit(solution)/shard_map/all_to_all | solution.py:460
  123.7 10.8 %copy-start = (s32[1,512,8]{1,2,0:T(8,128)S(1)}, s32[1,512,8]{1,2,0:T(8,128)}, u32[]{:S(2)}) copy-start(s32[1,512,8]{1,2,0:T(8,128)} %param.19) | copy-start | bytes 49156
  123.7 10.8 %copy-start.3 = (f32[1,512,8]{1,2,0:T(8,128)S(1)}, f32[1,512,8]{1,2,0:T(8,128)}, u32[]{:S(2)}) copy-start(f32[1,512,8]{1,2,0:T(8,128)} %param.21) | copy-start | bytes 49156
  123.7 10.8 %copy-start.4 = (s32[1,512]{1,0:T(1,128)S(1)}, s32[1,512]{1,0:T(1,128)}, u32[]{:S(2)}) copy-start(s32[1,512]{1,0:T(1,128)} %counts.1) | copy-start | bytes 6148

commit v6 on v5

--- a/solution.py
+++ b/solution.py
@@ -25,7 +25,7 @@
 
 def wide(table):
     high, low = halves(table)
-    return np.block([[high, high], [low, np.zeros_like(low)]])
+    return np.concatenate([high, high, low], axis=1)
 
 
 def waves(first, second, length):
@@ -88,8 +88,8 @@
 
 
 def wide_by_data(table_ref, value):
-    both = mul(table_ref[...], jnp.concatenate(split(value), axis=0))
-    return both[:128] + both[128:]
+    high, low = split(value)
+    return mul(table_ref[...], jnp.concatenate([high, low, high], axis=0))
 
 
 def thirds(value):

time: 136 us -> 136 us (level)
  no operation moved by 1% of the time
where the time goes in v6:
time: 136 us; the launch traced here: 135 us
  waiting for transfers between devices  44.1 us (32%)
  blocking collectives  34.9 us (26%)
  starting transfers between devices  33.3 us (24%)
  Pallas kernels  21.7 us (16%)
    all_to_all x4, waiting for transfers between devices, exchange(): return lax.all_to_all(value, axis, split_axis=0, concat_axis=0, tiled=True)  44.1 us
    all_to_all x2, blocking collectives, exchange(): return lax.all_to_all(value, axis, split_axis=0, concat_axis=0, tiled=True)  34.9 us
    all_to_all x4, starting transfers between devices, exchange(): return lax.all_to_all(value, axis, split_axis=0, concat_axis=0, tiled=True)  33.3 us
    pallas_call x9, Pallas kernels, call(): pl.pallas_call(kernel, out_shape=shape if many else shape[0], in_specs=so...  21.7 us
  transfers between devices with their start and end apart: 4, of which 4 were waited for; matrix products, arithmetic and copies ran while one was open for 0% of the time, Pallas kernels for 0%

profile of v6, /device:TPU:1, one launch (start us, length us, event | category | flops | bytes accessed | tf_op | source)
XLA Modules:
  0.0 135.1 jit_solution(9776785648212906862)
XLA Ops:
  0.0 1.8 %shard_map.163 = f32[64,1,64]{2,1,0:T(1,128)} custom-call(f32[4,128]{1,0:T(4,128)} %bitcast.26, s32[1,512]{1,0:T(1,128)} %counts.1, s32[8,512]{1,0:T(8,128)} %bitcast.23, f32[8,512]{1,0:T(8,128)} %bitcast.30), custom_call_target="tpu_custom_call" | custom-call | flops 10000000 | bytes 53248 | tf_op jit(solution)/shard_map/pallas_call | solution.py:418
  1.8 0.0 copy-start.7
  1.8 0.0 copy-start.8
  1.8 17.1 %all-to-all-start = ((f32[64,1,64]{2,1,0:T(1,128)}), f32[64,1,64]{2,1,0:T(1,128)S(1)}, u32[]{:S(2)}, u32[]{:S(2)}) async-start(f32[64,1,64]{2,1,0:T(1,128)} %shard_map.163), calls=%async_computation | async-start | bytes 65536 | tf_op jit(solution)/shard_map/all_to_all | solution.py:460
  19.0 0.0 copy-start.5
  19.0 0.0 copy-done.7
  19.0 0.0 copy-done.8
  19.0 0.7 copy-done.5
  19.6 0.3 shard_map.164.cells
  19.9 0.0 copy-start.12
  19.9 9.9 %all-to-all-done.arrived = f32[64,1,64]{2,1,0:T(1,128)S(1)} async-done(((f32[64,1,64]{2,1,0:T(1,128)}), f32[64,1,64]{2,1,0:T(1,128)S(1)}, u32[]{:S(2)}, u32[]{:S(2)}) %all-to-all-start) | async-done | bytes 16416 | tf_op jit(solution)/shard_map/all_to_all | solution.py:460
  29.8 0.9 shard_map.165
  30.7 0.0 copy-start.14
  30.7 6.6 %all-to-all-start.1 = ((f32[8,72,128]{2,1,0:T(8,128)}), f32[8,72,128]{2,1,0:T(8,128)S(1)}, u32[]{:S(2)}, u32[]{:S(2)}) async-start(f32[8,72,128]{2,1,0:T(8,128)} %shard_map.165), calls=%async_computation.1 | async-start | bytes 589824 | tf_op jit(solution)/shard_map/all_to_all | solution.py:460
  37.2 0.0 copy-start.15
  37.2 0.1 pad_add_fusion.meta
  37.3 6.7 %all-to-all-done.1.data = f32[8,72,128]{2,1,0:T(8,128)S(1)} async-done(((f32[8,72,128]{2,1,0:T(8,128)}), f32[8,72,128]{2,1,0:T(8,128)S(1)}, u32[]{:S(2)}, u32[]{:S(2)}) %all-to-all-start.1) | async-done | bytes 294944 | tf_op jit(solution)/shard_map/all_to_all | solution.py:460
  44.0 0.0 copy-done.12
  44.0 0.0 copy-done.14
  44.0 0.0 copy-done.15
  44.1 0.0 copy-start.10
  44.1 0.0 copy-start.11
  44.1 7.2 %shard_map.166 = f32[64,8,256]{2,1,0:T(8,128)} custom-call(s32[2]{0:T(128)S(1)} %pad_add_fusion.meta, f32[8,72,128]{2,1,0:T(8,128)S(1)} %all-to-all-done.1.data, f32[2,128]{1,0:T(2,128)S(1)} %copy-done.15, bf16[128,384]{1,0:T(8,128)(2,1)S(1)} %copy-done.14, bf16[2,512,512]{2,1,0:T(8,128)(2,1)S(1)} %copy-done.12), custom_call_target="tpu_custom_call" | custom-call | flops 6000000000 | bytes 1967112 | tf_op jit(solution)/shard_map/pallas_call | solution.py:418
  51.3 0.0 copy-start.6
  51.3 4.8 %all-to-all-start.2 = ((f32[64,8,256]{2,1,0:T(8,128)}), f32[64,8,256]{2,1,0:T(8,128)S(1)}, u32[]{:S(2)}, u32[]{:S(2)}) async-start(f32[64,8,256]{2,1,0:T(8,128)} %shard_map.166), calls=%async_computation.2 | async-start | bytes 1048576 | tf_op jit(solution)/shard_map/all_to_all | solution.py:460
  56.1 0.1 stack.31.factor
  56.1 17.1 %all-to-all-done.2.lines = f32[64,8,256]{2,1,0:T(8,128)S(1)} async-done(((f32[64,8,256]{2,1,0:T(8,128)}), f32[64,8,256]{2,1,0:T(8,128)S(1)}, u32[]{:S(2)}, u32[]{:S(2)}) %all-to-all-start.2) | async-done | bytes 524320 | tf_op jit(solution)/shard_map/all_to_all | solution.py:460
  73.2 0.0 copy-done.10
  73.2 0.0 copy-done.11
  73.2 0.0 copy-done.6
  73.2 0.0 copy-start.13
  73.2 2.8 %shard_map.167 = f32[64,8,256]{2,1,0:T(8,128)S(1)} custom-call(f32[5]{0:T(128)S(1)} %stack.31.factor, f32[1,512,256]{2,1,0:T(8,128)S(1)} %copy-done.6, f32[64,8,256]{2,1,0:T(8,128)S(1)} %all-to-all-done.2.lines, bf16[2,512,512]{2,1,0:T(8,128)(2,1)S(1)} %copy-done.10, bf16[2,512,512]{2,1,0:T(8,128)(2,1)S(1)} %copy-done.11), custom_call_target="tpu_custom_call" | custom-call | flops 1000000000 | bytes 3670036 | tf_op jit(solution)/shard_map/pallas_call | solution.py:418
  76.0 0.0 copy-start.9
  76.0 22.4 %all_to_all.30.arrived = f32[64,8,256]{2,1,0:T(8,128)S(1)} all-to-all(f32[64,8,256]{2,1,0:T(8,128)S(1)} %shard_map.167), channel_id=1, replica_groups=mesh['slab'=64,'patch'=8] {'slab'}, dimensions={0} | all-to-all | bytes 1048576 | tf_op jit(solution)/shard_map/all_to_all | solution.py:460
  98.4 0.0 copy-done.13
  98.4 0.0 copy-done.9
  98.4 6.4 %shard_map.168 = f32[8,32,128]{2,1,0:T(8,128)S(1)} custom-call(s32[2]{0:T(128)S(1)} %pad_add_fusion.meta, f32[64,8,256]{2,1,0:T(8,128)S(1)} %all_to_all.30.arrived, f32[8,72,128]{2,1,0:T(8,128)S(1)} %all-to-all-done.1.data, f32[2,128]{1,0:T(2,128)S(1)} %copy-done.15, bf16[128,384]{1,0:T(8,128)(2,1)S(1)} %copy-done.13, bf16[2,512,512]{2,1,0:T(8,128)(2,1)S(1)} %copy-done.9), custom_call_target="tpu_custom_call" | custom-call | flops 6000000000 | bytes 2098184 | tf_op jit(solution)/shard_map/pallas_call | solution.py:418
  104.9 12.5 %all_to_all.31.parts = f32[8,32,128]{2,1,0:T(8,128)S(1)} all-to-all(f32[8,32,128]{2,1,0:T(8,128)S(1)} %shard_map.168), channel_id=1, replica_groups=mesh['slab'=64,'patch'=8] {'patch'}, dimensions={0} | all-to-all | bytes 262144 | tf_op jit(solution)/shard_map/all_to_all | solution.py:460
  117.4 0.8 shard_map.169
  118.1 0.0 copy-start.1
  118.1 0.0 copy-start.2
  118.1 4.8 %all-to-all-start.5 = ((f32[64,1,64]{2,1,0:T(1,128)}), f32[64,1,64]{2,1,0:T(1,128)S(1)}, u32[]{:S(2)}, u32[]{:S(2)}) async-start(f32[64,1,64]{2,1,0:T(1,128)} %shard_map.169), calls=%async_computation.5 | async-start | bytes 65536 | tf_op jit(solution)/shard_map/all_to_all | solution.py:460
  123.0 0.0 copy-done.1
  123.0 0.0 copy-done.2
  123.0 0.0 copy-start
  123.0 0.0 copy-start.3
  123.0 0.0 copy-start.4
  123.0 0.4 shard_map.170.near
  123.4 10.4 %all-to-all-done.5.arrived = f32[64,1,64]{2,1,0:T(1,128)S(1)} async-done(((f32[64,1,64]{2,1,0:T(1,128)}), f32[64,1,64]{2,1,0:T(1,128)S(1)}, u32[]{:S(2)}, u32[]{:S(2)}) %all-to-all-start.5) | async-done | bytes 16416 | tf_op jit(solution)/shard_map/all_to_all | solution.py:460
  133.8 0.0 copy-done
  133.8 0.0 copy-done.3
  133.8 0.0 copy-done.4
  133.8 1.3 shard_map.171
Async XLA Ops:
  1.8 17.2 %copy-start.7 = (s32[1,512,8]{1,2,0:T(8,128)S(1)}, s32[1,512,8]{1,2,0:T(8,128)}, u32[]{:S(2)}) copy-start(s32[1,512,8]{1,2,0:T(8,128)} %param.22) | copy-start | bytes 49156
  1.8 17.2 %copy-start.8 = (s32[1,512,8]{1,2,0:T(8,128)S(1)}, s32[1,512,8]{1,2,0:T(8,128)}, u32[]{:S(2)}) copy-start(s32[1,512,8]{1,2,0:T(8,128)} %param.23) | copy-start | bytes 49156
  1.8 28.0 %all-to-all-start = ((f32[64,1,64]{2,1,0:T(1,128)}), f32[64,1,64]{2,1,0:T(1,128)S(1)}, u32[]{:S(2)}, u32[]{:S(2)}) async-start(f32[64,1,64]{2,1,0:T(1,128)} %shard_map.163), calls=%async_computation | async-start | bytes 65536 | tf_op jit(solution)/shard_map/all_to_all | solution.py:460
  19.0 0.7 copy-start.5
  19.9 24.1 %copy-start.12 = (bf16[2,512,512]{2,1,0:T(8,128)(2,1)S(1)}, bf16[2,512,512]{2,1,0:T(8,128)(2,1)}, u32[]{:S(2)}) copy-start(bf16[2,512,512]{2,1,0:T(8,128)(2,1)} %constant.42.clone.y_table) | copy-start | bytes 3145732
  30.7 13.4 %copy-start.14 = (bf16[128,384]{1,0:T(8,128)(2,1)S(1)}, bf16[128,384]{1,0:T(8,128)(2,1)}, u32[]{:S(2)}) copy-start(bf16[128,384]{1,0:T(8,128)(2,1)} %constant.40.clone.x_table) | copy-start | bytes 294916
  30.7 13.4 %all-to-all-start.1 = ((f32[8,72,128]{2,1,0:T(8,128)}), f32[8,72,128]{2,1,0:T(8,128)S(1)}, u32[]{:S(2)}, u32[]{:S(2)}) async-start(f32[8,72,128]{2,1,0:T(8,128)} %shard_map.165), calls=%async_computation.1 | async-start | bytes 589824 | tf_op jit(solution)/shard_map/all_to_all | solution.py:460
  37.2 6.8 %copy-start.15 = (f32[2,128]{1,0:T(2,128)S(1)}, f32[2,128]{1,0:T(2,128)}, u32[]{:S(2)}) copy-start(f32[2,128]{1,0:T(2,128)} %constant.39.clone.quarter) | copy-start | bytes 3076
  44.1 29.1 %copy-start.10 = (bf16[2,512,512]{2,1,0:T(8,128)(2,1)S(1)}, bf16[2,512,512]{2,1,0:T(8,128)(2,1)}, u32[]{:S(2)}) copy-start(bf16[2,512,512]{2,1,0:T(8,128)(2,1)} %constant.44.clone.forward) | copy-start | bytes 3145732
  44.1 29.1 %copy-start.11 = (bf16[2,512,512]{2,1,0:T(8,128)(2,1)S(1)}, bf16[2,512,512]{2,1,0:T(8,128)(2,1)}, u32[]{:S(2)}) copy-start(bf16[2,512,512]{2,1,0:T(8,128)(2,1)} %constant.45.clone.backward) | copy-start | bytes 3145732
  51.3 21.9 %copy-start.6 = (f32[1,512,256]{2,1,0:T(8,128)S(1)}, f32[1,512,256]{2,1,0:T(8,128)}, u32[]{:S(2)}) copy-start(f32[1,512,256]{2,1,0:T(8,128)} %kernel.1) | copy-start | bytes 1572868
  51.3 21.9 %all-to-all-start.2 = ((f32[64,8,256]{2,1,0:T(8,128)}), f32[64,8,256]{2,1,0:T(8,128)S(1)}, u32[]{:S(2)}, u32[]{:S(2)}) async-start(f32[64,8,256]{2,1,0:T(8,128)} %shard_map.166), calls=%async_computation.2 | async-start | bytes 1048576 | tf_op jit(solution)/shard_map/all_to_all | solution.py:460
  73.2 25.2 %copy-start.13 = (bf16[128,384]{1,0:T(8,128)(2,1)S(1)}, bf16[128,384]{1,0:T(8,128)(2,1)}, u32[]{:S(2)}) copy-start(bf16[128,384]{1,0:T(8,128)(2,1)} %constant.41.clone.x_table) | copy-start | bytes 294916
  76.0 22.4 %copy-start.9 = (bf16[2,512,512]{2,1,0:T(8,128)(2,1)S(1)}, bf16[2,512,512]{2,1,0:T(8,128)(2,1)}, u32[]{:S(2)}) copy-start(bf16[2,512,512]{2,1,0:T(8,128)(2,1)} %constant.43.clone.y_table) | copy-start | bytes 3145732
  118.1 4.8 %copy-start.1 = (s32[16,512]{1,0:T(8,128)S(1)}, s32[16,512]{1,0:T(8,128)}, u32[]{:S(2)}) copy-start(s32[16,512]{1,0:T(8,128)} %index.1) | copy-start | bytes 98308
  118.1 4.9 %copy-start.2 = (f32[16,512]{1,0:T(8,128)S(1)}, f32[16,512]{1,0:T(8,128)}, u32[]{:S(2)}) copy-start(f32[16,512]{1,0:T(8,128)} %coef.1) | copy-start | bytes 98308
  118.1 15.7 %all-to-all-start.5 = ((f32[64,1,64]{2,1,0:T(1,128)}), f32[64,1,64]{2,1,0:T(1,128)S(1)}, u32[]{:S(2)}, u32[]{:S(2)}) async-start(f32[64,1,64]{2,1,0:T(1,128)} %shard_map.169), calls=%async_computation.5 | async-start | bytes 65536 | tf_op jit(solution)/shard_map/all_to_all | solution.py:460
  123.0 10.8 %copy-start = (s32[1,512,8]{1,2,0:T(8,128)S(1)}, s32[1,512,8]{1,2,0:T(8,128)}, u32[]{:S(2)}) copy-start(s32[1,512,8]{1,2,0:T(8,128)} %param.19) | copy-start | bytes 49156
  123.0 10.8 %copy-start.3 = (f32[1,512,8]{1,2,0:T(8,128)S(1)}, f32[1,512,8]{1,2,0:T(8,128)}, u32[]{:S(2)}) copy-start(f32[1,512,8]{1,2,0:T(8,128)} %param.21) | copy-start | bytes 49156
  123.0 10.8 %copy-start.4 = (s32[1,512]{1,0:T(1,128)S(1)}, s32[1,512]{1,0:T(1,128)}, u32[]{:S(2)}) copy-start(s32[1,512]{1,0:T(1,128)} %counts.1) | copy-start | bytes 6148

commit v7 on v6

--- a/solution.py
+++ b/solution.py
@@ -264,7 +264,7 @@
         out[:, 4 + z, :] = jnp.where(first, im_first, im_cos - re_sin)
 
 
-def spectrum_kernel(factor, kernel, lines, forward, backward, out):
+def spectrum_kernel(factor, kernel, lines, forward, backward, out, scaled):
     size = NY // 2
     green = kernel[0, :size, :].T
     base = factor[4]
@@ -275,12 +275,14 @@
     value = lines[...].reshape(2 * NZ, size)
     sign = jnp.where((iota((2 * NZ, 128), 0) & 4) == 0, 1.0, -1.0)
     wave = table_by_data(forward, value)
-    turned = table_by_data(forward, value[:, :128] * sign)
-    left = jnp.concatenate([own[:, :128]] * 2, axis=0) * wave[:, :128]
-    left = left + jnp.concatenate([mirrored] * 2, axis=0) * turned
-    right = jnp.concatenate([own[:, 128:]] * 2, axis=0) * wave[:, 128:]
-    scaled = jnp.concatenate([left, right], axis=1)
-    out[...] = table_by_data(backward, scaled).reshape(N_SLAB, 8, size)
+    scaled[...] = jnp.concatenate([own] * 2, axis=0) * wave
+
+    @pl.when(factor[2] > 0.0)
+    def _():
+        turned = table_by_data(forward, value[:, :128] * sign)
+        scaled[:, :128] = scaled[:, :128] + jnp.concatenate([mirrored] * 2, axis=0) * turned
+
+    out[...] = table_by_data(backward, scaled[...]).reshape(N_SLAB, 8, size)
 
 
 def gathered(whole, block, slot):
@@ -474,7 +476,8 @@
 
 def run_spectrum(factor, kernel, lines, forward, backward):
     return call(
-        spectrum_kernel, (N_SLAB, 8, 256), [factor, kernel, lines, forward, backward], scalars=1, vmem=24, flops=10**9
+        spectrum_kernel, (N_SLAB, 8, 256), [factor, kernel, lines, forward, backward],
+        [pltpu.VMEM((2 * NZ, NY // 2), F32)], scalars=1, vmem=24, flops=10**9
     )
 
 

time: 136 us -> 135 us (level)
  no operation moved by 1% of the time
where the time goes in v7:
time: 135 us; the launch traced here: 134 us
  waiting for transfers between devices  44.1 us (33%)
  blocking collectives  34.9 us (26%)
  starting transfers between devices  33.4 us (25%)
  Pallas kernels  20.7 us (15%)
    all_to_all x4, waiting for transfers between devices, exchange(): return lax.all_to_all(value, axis, split_axis=0, concat_axis=0, tiled=True)  44.1 us
    all_to_all x2, blocking collectives, exchange(): return lax.all_to_all(value, axis, split_axis=0, concat_axis=0, tiled=True)  34.9 us
    all_to_all x4, starting transfers between devices, exchange(): return lax.all_to_all(value, axis, split_axis=0, concat_axis=0, tiled=True)  33.4 us
    pallas_call x9, Pallas kernels, call(): pl.pallas_call(kernel, out_shape=shape if many else shape[0], in_specs=so...  20.7 us
  transfers between devices with their start and end apart: 4, of which 4 were waited for; matrix products, arithmetic and copies ran while one was open for 0% of the time, Pallas kernels for 0%

profile of v7, /device:TPU:1, one launch (start us, length us, event | category | flops | bytes accessed | tf_op | source)
XLA Modules:
  0.0 134.1 jit_solution(2905572982714959219)
XLA Ops:
  0.0 1.8 %shard_map.163 = f32[64,1,64]{2,1,0:T(1,128)} custom-call(f32[4,128]{1,0:T(4,128)} %bitcast.26, s32[1,512]{1,0:T(1,128)} %counts.1, s32[8,512]{1,0:T(8,128)} %bitcast.23, f32[8,512]{1,0:T(8,128)} %bitcast.30), custom_call_target="tpu_custom_call" | custom-call | flops 10000000 | bytes 53248 | tf_op jit(solution)/shard_map/pallas_call | solution.py:420
  1.8 0.0 copy-start.7
  1.8 0.0 copy-start.8
  1.8 17.1 %all-to-all-start = ((f32[64,1,64]{2,1,0:T(1,128)}), f32[64,1,64]{2,1,0:T(1,128)S(1)}, u32[]{:S(2)}, u32[]{:S(2)}) async-start(f32[64,1,64]{2,1,0:T(1,128)} %shard_map.163), calls=%async_computation | async-start | bytes 65536 | tf_op jit(solution)/shard_map/all_to_all | solution.py:462
  19.0 0.0 copy-start.5
  19.0 0.0 copy-done.7
  19.0 0.0 copy-done.8
  19.0 0.7 copy-done.5
  19.6 0.3 shard_map.164.cells
  19.9 0.0 copy-start.12
  19.9 9.9 %all-to-all-done.arrived = f32[64,1,64]{2,1,0:T(1,128)S(1)} async-done(((f32[64,1,64]{2,1,0:T(1,128)}), f32[64,1,64]{2,1,0:T(1,128)S(1)}, u32[]{:S(2)}, u32[]{:S(2)}) %all-to-all-start) | async-done | bytes 16416 | tf_op jit(solution)/shard_map/all_to_all | solution.py:462
  29.8 0.9 shard_map.165
  30.7 0.0 copy-start.14
  30.7 6.6 %all-to-all-start.1 = ((f32[8,72,128]{2,1,0:T(8,128)}), f32[8,72,128]{2,1,0:T(8,128)S(1)}, u32[]{:S(2)}, u32[]{:S(2)}) async-start(f32[8,72,128]{2,1,0:T(8,128)} %shard_map.165), calls=%async_computation.1 | async-start | bytes 589824 | tf_op jit(solution)/shard_map/all_to_all | solution.py:462
  37.2 0.0 copy-start.15
  37.2 0.1 pad_add_fusion.meta
  37.3 6.7 %all-to-all-done.1.data = f32[8,72,128]{2,1,0:T(8,128)S(1)} async-done(((f32[8,72,128]{2,1,0:T(8,128)}), f32[8,72,128]{2,1,0:T(8,128)S(1)}, u32[]{:S(2)}, u32[]{:S(2)}) %all-to-all-start.1) | async-done | bytes 294944 | tf_op jit(solution)/shard_map/all_to_all | solution.py:462
  44.0 0.0 copy-done.12
  44.0 0.0 copy-done.14
  44.0 0.0 copy-done.15
  44.1 0.0 copy-start.10
  44.1 0.0 copy-start.11
  44.1 7.2 %shard_map.166 = f32[64,8,256]{2,1,0:T(8,128)} custom-call(s32[2]{0:T(128)S(1)} %pad_add_fusion.meta, f32[8,72,128]{2,1,0:T(8,128)S(1)} %all-to-all-done.1.data, f32[2,128]{1,0:T(2,128)S(1)} %copy-done.15, bf16[128,384]{1,0:T(8,128)(2,1)S(1)} %copy-done.14, bf16[2,512,512]{2,1,0:T(8,128)(2,1)S(1)} %copy-done.12), custom_call_target="tpu_custom_call" | custom-call | flops 6000000000 | bytes 1967112 | tf_op jit(solution)/shard_map/pallas_call | solution.py:420
  51.3 0.0 copy-start.6
  51.3 4.8 %all-to-all-start.2 = ((f32[64,8,256]{2,1,0:T(8,128)}), f32[64,8,256]{2,1,0:T(8,128)S(1)}, u32[]{:S(2)}, u32[]{:S(2)}) async-start(f32[64,8,256]{2,1,0:T(8,128)} %shard_map.166), calls=%async_computation.2 | async-start | bytes 1048576 | tf_op jit(solution)/shard_map/all_to_all | solution.py:462
  56.1 0.1 stack.31.factor
  56.1 17.1 %all-to-all-done.2.lines = f32[64,8,256]{2,1,0:T(8,128)S(1)} async-done(((f32[64,8,256]{2,1,0:T(8,128)}), f32[64,8,256]{2,1,0:T(8,128)S(1)}, u32[]{:S(2)}, u32[]{:S(2)}) %all-to-all-start.2) | async-done | bytes 524320 | tf_op jit(solution)/shard_map/all_to_all | solution.py:462
  73.2 0.0 copy-done.10
  73.2 0.0 copy-done.11
  73.2 0.0 copy-done.6
  73.2 0.0 copy-start.13
  73.2 1.8 %shard_map.167 = f32[64,8,256]{2,1,0:T(8,128)S(1)} custom-call(f32[5]{0:T(128)S(1)} %stack.31.factor, f32[1,512,256]{2,1,0:T(8,128)S(1)} %copy-done.6, f32[64,8,256]{2,1,0:T(8,128)S(1)} %all-to-all-done.2.lines, bf16[2,512,512]{2,1,0:T(8,128)(2,1)S(1)} %copy-done.10, bf16[2,512,512]{2,1,0:T(8,128)(2,1)S(1)} %copy-done.11), custom_call_target="tpu_custom_call" | custom-call | flops 1000000000 | bytes 3670036 | tf_op jit(solution)/shard_map/pallas_call | solution.py:420
  75.0 0.0 copy-start.9
  75.0 22.3 %all_to_all.30.arrived = f32[64,8,256]{2,1,0:T(8,128)S(1)} all-to-all(f32[64,8,256]{2,1,0:T(8,128)S(1)} %shard_map.167), channel_id=1, replica_groups=mesh['slab'=64,'patch'=8] {'slab'}, dimensions={0} | all-to-all | bytes 1048576 | tf_op jit(solution)/shard_map/all_to_all | solution.py:462
  97.3 0.0 copy-done.13
  97.3 0.0 copy-done.9
  97.3 6.4 %shard_map.168 = f32[8,32,128]{2,1,0:T(8,128)S(1)} custom-call(s32[2]{0:T(128)S(1)} %pad_add_fusion.meta, f32[64,8,256]{2,1,0:T(8,128)S(1)} %all_to_all.30.arrived, f32[8,72,128]{2,1,0:T(8,128)S(1)} %all-to-all-done.1.data, f32[2,128]{1,0:T(2,128)S(1)} %copy-done.15, bf16[128,384]{1,0:T(8,128)(2,1)S(1)} %copy-done.13, bf16[2,512,512]{2,1,0:T(8,128)(2,1)S(1)} %copy-done.9), custom_call_target="tpu_custom_call" | custom-call | flops 6000000000 | bytes 2098184 | tf_op jit(solution)/shard_map/pallas_call | solution.py:420
  103.7 12.6 %all_to_all.31.parts = f32[8,32,128]{2,1,0:T(8,128)S(1)} all-to-all(f32[8,32,128]{2,1,0:T(8,128)S(1)} %shard_map.168), channel_id=1, replica_groups=mesh['slab'=64,'patch'=8] {'patch'}, dimensions={0} | all-to-all | bytes 262144 | tf_op jit(solution)/shard_map/all_to_all | solution.py:462
  116.4 0.8 shard_map.169
  117.1 0.0 copy-start.1
  117.1 0.0 copy-start.2
  117.1 4.9 %all-to-all-start.5 = ((f32[64,1,64]{2,1,0:T(1,128)}), f32[64,1,64]{2,1,0:T(1,128)S(1)}, u32[]{:S(2)}, u32[]{:S(2)}) async-start(f32[64,1,64]{2,1,0:T(1,128)} %shard_map.169), calls=%async_computation.5 | async-start | bytes 65536 | tf_op jit(solution)/shard_map/all_to_all | solution.py:462
  122.0 0.0 copy-done.1
  122.0 0.0 copy-done.2
  122.0 0.0 copy-start
  122.1 0.0 copy-start.3
  122.1 0.0 copy-start.4
  122.1 0.4 shard_map.170.near
  122.5 10.4 %all-to-all-done.5.arrived = f32[64,1,64]{2,1,0:T(1,128)S(1)} async-done(((f32[64,1,64]{2,1,0:T(1,128)}), f32[64,1,64]{2,1,0:T(1,128)S(1)}, u32[]{:S(2)}, u32[]{:S(2)}) %all-to-all-start.5) | async-done | bytes 16416 | tf_op jit(solution)/shard_map/all_to_all | solution.py:462
  132.8 0.0 copy-done
  132.9 0.0 copy-done.3
  132.9 0.0 copy-done.4
  132.9 1.3 shard_map.171
Async XLA Ops:
  1.8 17.2 %copy-start.7 = (s32[1,512,8]{1,2,0:T(8,128)S(1)}, s32[1,512,8]{1,2,0:T(8,128)}, u32[]{:S(2)}) copy-start(s32[1,512,8]{1,2,0:T(8,128)} %param.22) | copy-start | bytes 49156
  1.8 17.2 %copy-start.8 = (s32[1,512,8]{1,2,0:T(8,128)S(1)}, s32[1,512,8]{1,2,0:T(8,128)}, u32[]{:S(2)}) copy-start(s32[1,512,8]{1,2,0:T(8,128)} %param.23) | copy-start | bytes 49156
  1.8 28.0 %all-to-all-start = ((f32[64,1,64]{2,1,0:T(1,128)}), f32[64,1,64]{2,1,0:T(1,128)S(1)}, u32[]{:S(2)}, u32[]{:S(2)}) async-start(f32[64,1,64]{2,1,0:T(1,128)} %shard_map.163), calls=%async_computation | async-start | bytes 65536 | tf_op jit(solution)/shard_map/all_to_all | solution.py:462
  19.0 0.7 copy-start.5
  19.9 24.1 %copy-start.12 = (bf16[2,512,512]{2,1,0:T(8,128)(2,1)S(1)}, bf16[2,512,512]{2,1,0:T(8,128)(2,1)}, u32[]{:S(2)}) copy-start(bf16[2,512,512]{2,1,0:T(8,128)(2,1)} %constant.42.clone.y_table) | copy-start | bytes 3145732
  30.7 13.4 %copy-start.14 = (bf16[128,384]{1,0:T(8,128)(2,1)S(1)}, bf16[128,384]{1,0:T(8,128)(2,1)}, u32[]{:S(2)}) copy-start(bf16[128,384]{1,0:T(8,128)(2,1)} %constant.40.clone.x_table) | copy-start | bytes 294916
  30.7 13.4 %all-to-all-start.1 = ((f32[8,72,128]{2,1,0:T(8,128)}), f32[8,72,128]{2,1,0:T(8,128)S(1)}, u32[]{:S(2)}, u32[]{:S(2)}) async-start(f32[8,72,128]{2,1,0:T(8,128)} %shard_map.165), calls=%async_computation.1 | async-start | bytes 589824 | tf_op jit(solution)/shard_map/all_to_all | solution.py:462
  37.2 6.8 %copy-start.15 = (f32[2,128]{1,0:T(2,128)S(1)}, f32[2,128]{1,0:T(2,128)}, u32[]{:S(2)}) copy-start(f32[2,128]{1,0:T(2,128)} %constant.39.clone.quarter) | copy-start | bytes 3076
  44.1 29.1 %copy-start.10 = (bf16[2,512,512]{2,1,0:T(8,128)(2,1)S(1)}, bf16[2,512,512]{2,1,0:T(8,128)(2,1)}, u32[]{:S(2)}) copy-start(bf16[2,512,512]{2,1,0:T(8,128)(2,1)} %constant.44.clone.forward) | copy-start | bytes 3145732
  44.1 29.1 %copy-start.11 = (bf16[2,512,512]{2,1,0:T(8,128)(2,1)S(1)}, bf16[2,512,512]{2,1,0:T(8,128)(2,1)}, u32[]{:S(2)}) copy-start(bf16[2,512,512]{2,1,0:T(8,128)(2,1)} %constant.45.clone.backward) | copy-start | bytes 3145732
  51.3 21.9 %copy-start.6 = (f32[1,512,256]{2,1,0:T(8,128)S(1)}, f32[1,512,256]{2,1,0:T(8,128)}, u32[]{:S(2)}) copy-start(f32[1,512,256]{2,1,0:T(8,128)} %kernel.1) | copy-start | bytes 1572868
  51.3 21.9 %all-to-all-start.2 = ((f32[64,8,256]{2,1,0:T(8,128)}), f32[64,8,256]{2,1,0:T(8,128)S(1)}, u32[]{:S(2)}, u32[]{:S(2)}) async-start(f32[64,8,256]{2,1,0:T(8,128)} %shard_map.166), calls=%async_computation.2 | async-start | bytes 1048576 | tf_op jit(solution)/shard_map/all_to_all | solution.py:462
  73.2 24.1 %copy-start.13 = (bf16[128,384]{1,0:T(8,128)(2,1)S(1)}, bf16[128,384]{1,0:T(8,128)(2,1)}, u32[]{:S(2)}) copy-start(bf16[128,384]{1,0:T(8,128)(2,1)} %constant.41.clone.x_table) | copy-start | bytes 294916
  75.0 22.3 %copy-start.9 = (bf16[2,512,512]{2,1,0:T(8,128)(2,1)S(1)}, bf16[2,512,512]{2,1,0:T(8,128)(2,1)}, u32[]{:S(2)}) copy-start(bf16[2,512,512]{2,1,0:T(8,128)(2,1)} %constant.43.clone.y_table) | copy-start | bytes 3145732
  117.1 4.9 %copy-start.1 = (s32[16,512]{1,0:T(8,128)S(1)}, s32[16,512]{1,0:T(8,128)}, u32[]{:S(2)}) copy-start(s32[16,512]{1,0:T(8,128)} %index.1) | copy-start | bytes 98308
  117.1 4.9 %copy-start.2 = (f32[16,512]{1,0:T(8,128)S(1)}, f32[16,512]{1,0:T(8,128)}, u32[]{:S(2)}) copy-start(f32[16,512]{1,0:T(8,128)} %coef.1) | copy-start | bytes 98308
  117.1 15.7 %all-to-all-start.5 = ((f32[64,1,64]{2,1,0:T(1,128)}), f32[64,1,64]{2,1,0:T(1,128)S(1)}, u32[]{:S(2)}, u32[]{:S(2)}) async-start(f32[64,1,64]{2,1,0:T(1,128)} %shard_map.169), calls=%async_computation.5 | async-start | bytes 65536 | tf_op jit(solution)/shard_map/all_to_all | solution.py:462
  122.0 10.8 %copy-start = (s32[1,512,8]{1,2,0:T(8,128)S(1)}, s32[1,512,8]{1,2,0:T(8,128)}, u32[]{:S(2)}) copy-start(s32[1,512,8]{1,2,0:T(8,128)} %param.19) | copy-start | bytes 49156
  122.1 10.8 %copy-start.3 = (f32[1,512,8]{1,2,0:T(8,128)S(1)}, f32[1,512,8]{1,2,0:T(8,128)}, u32[]{:S(2)}) copy-start(f32[1,512,8]{1,2,0:T(8,128)} %param.21) | copy-start | bytes 49156
  122.1 10.8 %copy-start.4 = (s32[1,512]{1,0:T(1,128)S(1)}, s32[1,512]{1,0:T(1,128)}, u32[]{:S(2)}) copy-start(s32[1,512]{1,0:T(1,128)} %counts.1) | copy-start | bytes 6148
